TPU v7x, 512 devices: a whole 4x8x8 slice. The times are simulated.
512 devices in a mesh: src: 32 (over z, x), tgt: 16 (over y, core).
Axes of the slice: x: 4, y: 8, z: 8, core: 2. Of those that a mesh axis runs over, the one named last changes fastest.
Arguments:
- src_emb: float32 [20480, 512], P(('src', 'tgt')), may hold values from -16 to 16
- tgt_emb: float32 [20480, 512], P(('src', 'tgt')), may hold values from -16 to 16
Outputs:
- src_potential: float32 [20480], P(('src', 'tgt'))
- tgt_potential: float32 [20480], P(('src', 'tgt'))
- src_grad: float32 [20480, 512], P(('src', 'tgt'))
- tgt_grad: float32 [20480, 512], P(('src', 'tgt'))
All inputs are finite; a program needn't handle non-finite values.
Results may differ from a plain program's by a relative error of at most 0.0003.
Values sent between devices are 32-bit elements; how exact they have to be, the bound alone decides.
No kernel may reach another device: no remote copies, remote signals or barrier semaphores. Data moves between devices by JAX's collectives and lax.ppermute only.
A program may use at most 64 MiB of HBM per device.

v0:
```python
import math

import jax
import jax.numpy as jnp
from jax import lax
from jax.sharding import PartitionSpec as P

ITERS = 3


entropy_reg = 0.05


def pair_cost(left, right):
    left_sq = jnp.sum(left * left, axis=1)
    right_sq = jnp.sum(right * right, axis=1)
    cross = jnp.dot(
        left, right.T, preferred_element_type=jnp.float32, precision=lax.Precision.HIGHEST
    )
    return (left_sq[:, None] + right_sq[None, :] - 2.0 * cross) / left.shape[1]


def per_device(src_emb, tgt_emb):
    row_count = src_emb.shape[0]
    src_devs = lax.axis_size("src")
    tgt_devs = lax.axis_size("tgt")
    total_src = row_count * src_devs * tgt_devs
    total_tgt = row_count * src_devs * tgt_devs
    src_block = lax.all_gather(src_emb, "tgt", axis=0, tiled=True)
    tgt_block = lax.all_gather(tgt_emb, "src", axis=0, tiled=True)
    cost_tile = pair_cost(src_block, tgt_block)
    tgt_pot = jnp.zeros((tgt_block.shape[0],), jnp.float32)
    src_pot = jnp.zeros((src_block.shape[0],), jnp.float32)
    for iteration in range(ITERS):
        scores = (tgt_pot[None, :] - cost_tile) / entropy_reg
        local_peak = jnp.max(scores, axis=1)
        peak_val = lax.pmax(local_peak, "tgt")
        row_sum = lax.psum(jnp.sum(jnp.exp(scores - peak_val[:, None]), axis=1), "tgt")
        src_pot = -entropy_reg * (peak_val + jnp.log(row_sum) - math.log(total_tgt))
        scores = (src_pot[:, None] - cost_tile) / entropy_reg
        local_peak = jnp.max(scores, axis=0)
        peak_val = lax.pmax(local_peak, "src")
        col_sum = lax.psum(jnp.sum(jnp.exp(scores - peak_val[None, :]), axis=0), "src")
        tgt_pot = -entropy_reg * (peak_val + jnp.log(col_sum) - math.log(total_src))
    weight = jnp.exp((src_pot[:, None] + tgt_pot[None, :] - cost_tile) / entropy_reg)
    row_mass = jnp.sum(weight, axis=1)
    col_mass = jnp.sum(weight, axis=0)
    pushed = jnp.dot(
        weight, tgt_block, preferred_element_type=jnp.float32, precision=lax.Precision.HIGHEST
    )
    src_sum = lax.psum_scatter(
        row_mass[:, None] * src_block - pushed, "tgt", scatter_dimension=0, tiled=True
    )
    pulled = lax.dot_general(
        weight,
        src_block,
        (((0,), (0,)), ((), ())),
        precision=lax.Precision.HIGHEST,
        preferred_element_type=jnp.float32,
    )
    tgt_sum = lax.psum_scatter(
        col_mass[:, None] * tgt_block - pulled, "src", scatter_dimension=0, tiled=True
    )
    src_grad = src_sum / total_tgt
    tgt_grad = tgt_sum / total_src
    src_piece = lax.dynamic_slice_in_dim(src_pot, lax.axis_index("tgt") * row_count, row_count, 0)
    tgt_piece = lax.dynamic_slice_in_dim(tgt_pot, lax.axis_index("src") * row_count, row_count, 0)
    return (src_piece, tgt_piece, src_grad, tgt_grad)


def solution(mesh):
    placed = (P(("src", "tgt"), None), P(("src", "tgt"), None))
    return jax.shard_map(
        per_device,
        mesh=mesh,
        in_specs=placed,
        out_specs=(
            P(("src", "tgt")),
            P(("src", "tgt")),
            P(("src", "tgt"), None),
            P(("src", "tgt"), None),
        ),
        check_vma=False,
    )
```

profile of v0, /device:TPU:56, one launch (start us, length us, event | category | flops | bytes accessed | tf_op | source)
XLA Modules:
  0.0 1034.1 jit_solution(17047557856902924879)
XLA Ops:
  8.7 45.3 %all-gather.3.cloned.1.call-done = f32[640,512]{1,0:T(8,128)} async-done(((f32[40,512]{1,0:T(8,128)}), f32[640,512]{1,0:T(8,128)}) %all-gather.3.cloned.1.call-update) | async-done | bytes 1310736 | tf_op jit(solution)/shard_map/all_gather | solution.py:29
  54.0 1.5 multiply_reduce_fusion.1
  55.5 86.9 %all-gather.5.cloned.1.call-done = f32[1280,512]{1,0:T(8,128)} async-done(((f32[40,512]{1,0:T(8,128)}), f32[1280,512]{1,0:T(8,128)}) %all-gather.5.cloned.1.call-update) | async-done | bytes 2621456 | tf_op jit(solution)/shard_map/all_gather | solution.py:30
  142.4 2.0 multiply_reduce_fusion
  144.4 7.9 fusion.2
  152.3 20.0 %pmax.42 = f32[640]{0:T(1024)S(1)} all-reduce(f32[640]{0:T(1024)S(1)} %get-tuple-element.6), channel_id=1, replica_groups=mesh['src'=32,'tgt'=16] {'tgt'}, use_global_device_ids=true, to_apply=%region_3.0 | all-reduce | flops 640 | bytes 5120 | tf_op jit(solution)/shard_map/pmax | solution.py:37
  173.1 23.6 %psum.42 = f32[640]{0:T(1024)S(1)} all-reduce(f32[640]{0:T(1024)S(1)} %exponential_reduce_fusion.5), channel_id=1, replica_groups=mesh['src'=32,'tgt'=16] {'tgt'}, use_global_device_ids=true, to_apply=%region_5.0 | all-reduce | flops 640 | bytes 5120 | tf_op jit(solution)/shard_map/psum | solution.py:38
  197.1 73.3 %pmax.43 = f32[1280]{0:T(1024)S(1)} all-reduce(f32[1280]{0:T(1024)S(1)} %fusion.3), channel_id=1, replica_groups=mesh['src'=32,'tgt'=16] {'src'}, use_global_device_ids=true, to_apply=%region_7.0 | all-reduce | flops 1280 | bytes 10240 | tf_op jit(solution)/shard_map/pmax | solution.py:42
  271.2 70.7 %psum.43 = f32[1280]{0:T(1024)S(1)} all-reduce(f32[1280]{0:T(1024)S(1)} %exponential_reduce_fusion.4), channel_id=1, replica_groups=mesh['src'=32,'tgt'=16] {'src'}, use_global_device_ids=true, to_apply=%region_9.0 | all-reduce | flops 1280 | bytes 10240 | tf_op jit(solution)/shard_map/psum | solution.py:43
  342.3 23.5 %pmax.44 = f32[640]{0:T(1024)S(1)} all-reduce(f32[640]{0:T(1024)S(1)} %fusion.4), channel_id=1, replica_groups=mesh['src'=32,'tgt'=16] {'tgt'}, use_global_device_ids=true, to_apply=%region_11.0 | all-reduce | flops 640 | bytes 5120 | tf_op jit(solution)/shard_map/pmax | solution.py:37
  366.6 23.6 %psum.44 = f32[640]{0:T(1024)S(1)} all-reduce(f32[640]{0:T(1024)S(1)} %exponential_reduce_fusion.3), channel_id=1, replica_groups=mesh['src'=32,'tgt'=16] {'tgt'}, use_global_device_ids=true, to_apply=%region_13.0 | all-reduce | flops 640 | bytes 5120 | tf_op jit(solution)/shard_map/psum | solution.py:38
  390.5 72.7 %pmax.45 = f32[1280]{0:T(1024)S(1)} all-reduce(f32[1280]{0:T(1024)S(1)} %fusion.5), channel_id=1, replica_groups=mesh['src'=32,'tgt'=16] {'src'}, use_global_device_ids=true, to_apply=%region_15.0 | all-reduce | flops 1280 | bytes 10240 | tf_op jit(solution)/shard_map/pmax | solution.py:42
  463.9 70.9 %psum.45 = f32[1280]{0:T(1024)S(1)} all-reduce(f32[1280]{0:T(1024)S(1)} %exponential_reduce_fusion.2), channel_id=1, replica_groups=mesh['src'=32,'tgt'=16] {'src'}, use_global_device_ids=true, to_apply=%region_17.0 | all-reduce | flops 1280 | bytes 10240 | tf_op jit(solution)/shard_map/psum | solution.py:43
  535.3 23.5 %pmax.46 = f32[640]{0:T(1024)S(1)} all-reduce(f32[640]{0:T(1024)S(1)} %fusion.6), channel_id=1, replica_groups=mesh['src'=32,'tgt'=16] {'tgt'}, use_global_device_ids=true, to_apply=%region_19.0 | all-reduce | flops 640 | bytes 5120 | tf_op jit(solution)/shard_map/pmax | solution.py:37
  559.6 23.6 %psum.46 = f32[640]{0:T(1024)S(1)} all-reduce(f32[640]{0:T(1024)S(1)} %exponential_reduce_fusion.1), channel_id=1, replica_groups=mesh['src'=32,'tgt'=16] {'tgt'}, use_global_device_ids=true, to_apply=%region_21.0 | all-reduce | flops 640 | bytes 5120 | tf_op jit(solution)/shard_map/psum | solution.py:38
  583.6 72.7 %pmax.47 = f32[1280]{0:T(1024)S(1)} all-reduce(f32[1280]{0:T(1024)S(1)} %fusion.7), channel_id=1, replica_groups=mesh['src'=32,'tgt'=16] {'src'}, use_global_device_ids=true, to_apply=%region_23.0 | all-reduce | flops 1280 | bytes 10240 | tf_op jit(solution)/shard_map/pmax | solution.py:42
  656.9 70.7 %psum.47 = f32[1280]{0:T(1024)S(1)} all-reduce(f32[1280]{0:T(1024)S(1)} %exponential_reduce_fusion), channel_id=1, replica_groups=mesh['src'=32,'tgt'=16] {'src'}, use_global_device_ids=true, to_apply=%region_25.0 | all-reduce | flops 1280 | bytes 10240 | tf_op jit(solution)/shard_map/psum | solution.py:43
  727.7 1.0 fusion.8
  729.4 8.2 convolution_subtract_fusion.1
  737.9 14.1 %convolution_subtract_fusion = f32[1280,512]{1,0:T(8,128)} fusion(f32[640,512]{1,0:T(8,128)} %all-gather.3.cloned.1.call-done, f32[1280,512]{1,0:T(8,128)} %all-gather.5.cloned.1.call-done, f32[1280]{0:T(1024)S(1)} %get-tuple-element.4, f32[640,1280]{1,0:T(8,128)S(1)} %get-tuple-element.7, f32[1280]{0:T(1024)S(1)} %add_multiply_fusion, ...), kind=kOutput, calls=%fused_computation.3 | convolution fusion | flops 5036933120 | bytes 9843200 | tf_op jit(solution)/shard_map/dot_general | solution.py:54
  753.2 43.2 %reduce-scatter.3.cloned.1.call-done = f32[40,512]{1,0:T(8,128)} async-done(((f32[640,512]{1,0:T(8,128)}), f32[40,512]{1,0:T(8,128)}) %reduce-scatter.3.cloned.1.call-update) | async-done | bytes 81936 | tf_op jit(solution)/shard_map/reduce_scatter | solution.py:51
  796.3 1.5 broadcast_multiply_fusion.1
  797.9 228.2 %reduce-scatter.5.cloned.1.call-done = f32[40,512]{1,0:T(8,128)} async-done(((f32[1280,512]{1,0:T(8,128)}), f32[40,512]{1,0:T(8,128)}) %reduce-scatter.5.cloned.1.call-update) | async-done | bytes 81936 | tf_op jit(solution)/shard_map/reduce_scatter | solution.py:61
  1026.1 1.5 broadcast_multiply_fusion
  (29 shorter events, 10.2 us)
Async XLA Ops:
  7.2 46.8 %all-gather.3.cloned.1.call-start = ((), (), s32[]{:S(2)}) async-start(), calls=%async_computation.2 | async-start | bytes 1392640 | tf_op jit(solution)/shard_map/all_gather | solution.py:29
  7.9 134.5 %all-gather.5.cloned.1.call-start = ((), (), s32[]{:S(2)}) async-start(), calls=%async_computation.3 | async-start | bytes 2703360 | tf_op jit(solution)/shard_map/all_gather | solution.py:30
  8.6 787.7 %reduce-scatter.3.cloned.1.call-start = ((), (), s32[]{:S(2)}) async-start(), calls=%async_computation.4 | async-start | bytes 1392640 | tf_op jit(solution)/shard_map/reduce_scatter | solution.py:51
  727.7 1.7 copy-start
  737.6 288.4 %reduce-scatter.5.cloned.1.call-start = ((), (), s32[]{:S(2)}) async-start(), calls=%async_computation.5 | async-start | bytes 2703360 | tf_op jit(solution)/shard_map/reduce_scatter | solution.py:61
Sparse Core Ops, SparseCore 0:
  10.1 43.8 all-gather.2
  57.2 85.2 all-gather.4
  737.8 58.5 reduce-scatter.2
  800.6 225.4 reduce-scatter.4
where the time goes:
time: 1040 us; the launch traced here: 1030 us
  blocking collectives  569 us (55%)
  waiting for transfers between devices  405 us (39%)
  matrix products  30.2 us (3%)
  other arithmetic  14.1 us (1%)
  between operations  13.9 us (1%)
    reduce_scatter x1, waiting for transfers between devices, per_device(): lax.psum_scatter(col_mass[:, None] * tgt_block - pulled, 'src', scatter_d...  228 us
    pmax x3, blocking collectives, per_device(): peak_val = lax.pmax(local_peak, 'src')  219 us
    psum x3, blocking collectives, per_device(): lax.psum(jnp.sum(jnp.exp(scores - peak_val[None, :]), axis=0), 'src')  212 us
    all_gather x1, waiting for transfers between devices, per_device(): tgt_block = lax.all_gather(tgt_emb, 'src', axis=0, tiled=True)  86.9 us
    psum x3, blocking collectives, per_device(): lax.psum(jnp.sum(jnp.exp(scores - peak_val[:, None]), axis=1), 'tgt')  70.7 us
    pmax x3, blocking collectives, per_device(): peak_val = lax.pmax(local_peak, 'tgt')  67 us
    all_gather x1, waiting for transfers between devices, per_device(): src_block = lax.all_gather(src_emb, 'tgt', axis=0, tiled=True)  45.3 us
    reduce_scatter x1, waiting for transfers between devices, per_device(): lax.psum_scatter(row_mass[:, None] * src_block - pushed, 'tgt', scatter_d...  43.2 us
  transfers between devices with their start and end apart: 4, of which 4 were waited for; matrix products, arithmetic and copies ran while one was open for 2% of the time, Pallas kernels for 0%

commit v1 on v0

v1 whole, which is shorter than its diff:
```python
import math

import jax
import jax.numpy as jnp
from jax import lax
from jax.experimental import pallas as pl
from jax.experimental.pallas import tpu as pltpu
from jax.sharding import Mesh
from jax.sharding import PartitionSpec as P

ITERS = 3
ENTROPY_REG = 0.05
NZ, NX, NY, NC = 8, 4, 8, 2
LANES = 128

A_OF_X = (0, 0, 1, 1)
B_OF_X = (0, 1, 1, 0)
FLIP_A = [(x, NX - 1 - x) for x in range(NX)]
FLIP_B = [(x, x ^ 1) for x in range(NX)]
SWAP = [(0, 1), (1, 0)]
X_OF_AB = {(A_OF_X[x], B_OF_X[x]): x for x in range(NX)}

ROW_GROUPS = [[X_OF_AB[a, b] * NY + y for a in range(2) for y in range(NY)] for b in range(2)]
COL_GROUPS = [
    [(z * NX + X_OF_AB[a, b]) * NC + c for z in range(NZ) for b in range(2) for c in range(NC)]
    for a in range(2)
]

PAIRS = 4
NEIGHBOUR = [(i, i ^ 1) for i in range(8)]
FIRST = (0, 3)
SECOND = (1, 2)


def ring(step):
    return [(i, (i + step) % 8) for i in range(8)]


def take(buffer, *index):
    start = tuple(index) + (0,) * (buffer.ndim - len(index))
    size = (1,) * len(index) + buffer.shape[len(index):]
    return lax.dynamic_slice(buffer, start, size).reshape(buffer.shape[len(index):])


def gather_ring(shard, axis, at, flip):
    other = lax.ppermute(shard, axis, NEIGHBOUR)
    even = at % 2 == 0
    pair = jnp.concatenate([jnp.where(even, shard, other), jnp.where(even, other, shard)])
    behind = lax.ppermute(pair, axis, ring(2))
    ahead = lax.ppermute(pair, axis, ring(-2))
    across = lax.ppermute(pair, axis, ring(4))
    first = jnp.stack([pair, behind])
    second = jnp.stack([ahead, across])
    return first, lax.ppermute(first, "x", flip), second, lax.ppermute(second, "x", flip)


def tile_kernel(*refs):
    row_refs, col_refs, far_ref = refs[:4], refs[4:8], refs[8]
    src_ref, tgt_ref, cost_ref = refs[9:]
    z, x, y, c = (lax.axis_index(name) for name in ("z", "x", "y", "c"))
    a = x // 2
    b = (x // 2) ^ (x % 2)
    size = row_refs[0].shape[1]
    for half, (mine, other) in enumerate((row_refs[:2], row_refs[2:])):
        for i, step in enumerate((FIRST, SECOND)[half]):
            pair = (y // 2 + step) % PAIRS
            for place, ref in ((a, mine), (1 - a, other)):
                at = pl.multiple_of((place * PAIRS + pair) * size, 8)
                src_ref[pl.ds(at, size), :] = ref[i]
    for half, (mine, other) in enumerate((col_refs[:2], col_refs[2:])):
        for i, step in enumerate((FIRST, SECOND)[half]):
            pair = (z // 2 + step) % PAIRS
            for k, (place, ref) in enumerate(((b, mine), (1 - b, other))):
                at = pl.multiple_of(((c * 2 + place) * PAIRS + pair) * size, 8)
                tgt_ref[pl.ds(at, size), :] = ref[i]
                at = pl.multiple_of((((1 - c) * 2 + place) * PAIRS + pair) * size, 8)
                tgt_ref[pl.ds(at, size), :] = far_ref[half * 4 + k * 2 + i]
    rows, width = src_ref.shape
    cols = tgt_ref.shape[0]
    step = 256
    left = src_ref[...]
    left_sq = jnp.sum(left * left, axis=1, keepdims=True)
    ones = jnp.ones((8, width), jnp.float32)

    @pl.loop(0, cols // step)
    def _(j):
        at = pl.multiple_of(j * step, step)
        right = tgt_ref[pl.ds(at, step), :]
        dims = (((1,), (1,)), ((), ()))
        cross = lax.dot_general(
            src_ref[...],
            right,
            dims,
            precision=lax.Precision.HIGHEST,
            preferred_element_type=jnp.float32,
        )
        right_sq = lax.dot_general(
            ones,
            right * right,
            dims,
            precision=lax.Precision.HIGHEST,
            preferred_element_type=jnp.float32,
        )[:1]
        cost_ref[:, pl.ds(at, step)] = (left_sq + right_sq - 2.0 * cross) / width


def tile(row_pieces, col_pieces, far_piece):
    size, width = row_pieces[0].shape[1:]
    rows, cols = 2 * PAIRS * size, 4 * PAIRS * size
    whole = pl.BlockSpec(memory_space=pltpu.VMEM)
    return pl.pallas_call(
        tile_kernel,
        out_shape=(
            jax.ShapeDtypeStruct((rows, width), jnp.float32),
            jax.ShapeDtypeStruct((cols, width), jnp.float32),
            jax.ShapeDtypeStruct((rows, cols), jnp.float32),
        ),
        in_specs=[whole] * 9,
        out_specs=(whole,) * 3,
        compiler_params=pltpu.CompilerParams(vmem_limit_bytes=48 * 1024 * 1024),
    )(*row_pieces, *col_pieces, far_piece)


def scatter_ring(partial, axis, at, flip, own):
    moves = {2: ring(4), 1: ring(2), 3: ring(-2)}
    here = at // 2
    total = None
    for group in ((2, 1), (3, 0)):
        sent = jnp.stack([take(partial, 1 - own, (here + k) % PAIRS) for k in group])
        got = lax.ppermute(sent, "x", flip)
        for i, k in enumerate(group):
            part = take(partial, own, (here + k) % PAIRS) + got[i]
            if k:
                part = lax.ppermute(part, axis, moves[k])
            total = part if total is None else total + part
    total = total.reshape(2, -1, total.shape[-1])
    return take(total, at % 2) + lax.ppermute(take(total, 1 - at % 2), axis, NEIGHBOUR)


def exchange(local, axes, groups, count):
    size = local.shape[0]
    flat = local.reshape(1, size // LANES, LANES)
    sent = jnp.broadcast_to(flat, (count, size // LANES, LANES))
    got = lax.all_to_all(
        sent, axes, split_axis=0, concat_axis=0, axis_index_groups=groups, tiled=True
    )
    peak = jnp.max(got, axis=0)
    total = jnp.sum(jnp.exp(got - peak[None]), axis=0)
    return (peak + jnp.log(total)).reshape(size)


def local_lse(scores, axis):
    peak = jnp.max(scores, axis=axis, keepdims=True)
    total = jnp.sum(jnp.exp(scores - peak), axis=axis)
    return jnp.squeeze(peak, axis) + jnp.log(total)


def per_device(src_emb, tgt_emb):
    rows, width = src_emb.shape
    z, x, y, c = (lax.axis_index(name) for name in ("z", "x", "y", "c"))
    a = x // 2
    b = (x // 2) ^ (x % 2)
    total_points = rows * NZ * NX * NY * NC
    near, near_flip, rest, rest_flip = gather_ring(tgt_emb, "z", z, FLIP_B)
    col_pieces = (near, near_flip, rest, rest_flip)
    far_piece = lax.ppermute(
        jnp.concatenate([near, near_flip, rest, rest_flip]), "c", SWAP
    )
    near, near_flip, rest, rest_flip = gather_ring(src_emb, "y", y, FLIP_A)
    row_pieces = (near, near_flip, rest, rest_flip)
    src_block, tgt_block, cost = tile(row_pieces, col_pieces, far_piece)
    tgt_pot = jnp.zeros((tgt_block.shape[0],), jnp.float32)
    log_total = math.log(total_points)
    for _ in range(ITERS):
        lse = local_lse((tgt_pot[None, :] - cost) / ENTROPY_REG, 1)
        lse = exchange(lse, ("x", "y"), ROW_GROUPS, 2 * NY)
        src_pot = -ENTROPY_REG * (lse - log_total)
        lse = local_lse((src_pot[:, None] - cost) / ENTROPY_REG, 0)
        lse = exchange(lse, ("z", "x", "c"), COL_GROUPS, 2 * NZ * NC)
        tgt_pot = -ENTROPY_REG * (lse - log_total)
    weight = jnp.exp((src_pot[:, None] + tgt_pot[None, :] - cost) / ENTROPY_REG)
    row_mass = jnp.sum(weight, axis=1)
    col_mass = jnp.sum(weight, axis=0)
    pulled = lax.dot_general(
        weight,
        src_block,
        (((0,), (0,)), ((), ())),
        precision=lax.Precision.HIGH,
        preferred_element_type=jnp.float32,
    )
    tgt_part = (col_mass[:, None] * tgt_block - pulled).reshape(NC, -1, width)
    across = lax.ppermute(take(tgt_part, 1 - c), "c", SWAP)
    tgt_half = (take(tgt_part, c) + across).reshape(2, PAIRS, 2 * rows, width)
    tgt_sum = scatter_ring(tgt_half, "z", z, FLIP_B, b)
    pushed = jnp.dot(
        weight, tgt_block, preferred_element_type=jnp.float32, precision=lax.Precision.HIGH
    )
    src_part = (row_mass[:, None] * src_block - pushed).reshape(2, PAIRS, 2 * rows, width)
    src_sum = scatter_ring(src_part, "y", y, FLIP_A, a)
    src_piece = take(src_pot.reshape(2, NY, rows), a, y)
    tgt_piece = take(tgt_pot.reshape(NC, 2, NZ, rows), c, b, z)
    return src_piece, tgt_piece, src_sum / total_points, tgt_sum / total_points


def solution(mesh):
    grid = Mesh(mesh.devices.reshape(NZ, NX, NY, NC), ("z", "x", "y", "c"))
    split = ("z", "x", "y", "c")
    return jax.shard_map(
        per_device,
        mesh=grid,
        in_specs=(P(split, None), P(split, None)),
        out_specs=(P(split), P(split), P(split, None), P(split, None)),
        check_vma=False,
    )
```

time: 1040 us -> 308 us (0.30)
  blocking collectives: 569 us -> 77.6 us
  waiting for transfers between devices: 405 us -> 58.5 us
  starting transfers between devices: 0.38 us -> 106 us
  matrix products: 30.2 us -> 10.9 us
  other arithmetic: 14.1 us -> 26.7 us
  between operations: 13.9 us -> 1.63 us
  Pallas kernels: 0 us -> 11 us
  local copies, waits for them, and re-layouts: 1.86 us -> 12.7 us
    pmax x6 -> x0, blocking collectives: 286 us -> none  [the longest x3 219 us: per_device(): peak_val = lax.pmax(local_peak, 'src')]
    psum x6 -> x0, blocking collectives: 283 us -> none  [the longest x3 212 us: per_device(): lax.psum(jnp.sum(jnp.exp(scores - peak_val[None, :]), axis=0), 'src')]
    reduce_scatter x2 -> x0, waiting for transfers between devices: 271 us -> none  [the longest x1 228 us: per_device(): lax.psum_scatter(col_mass[:, None] * tgt_block - pulled, 'src', scatter_d...]
    all_gather x2 -> x0, waiting for transfers between devices: 132 us -> none  [the longest x1 86.9 us: per_device(): tgt_block = lax.all_gather(tgt_emb, 'src', axis=0, tiled=True)]
    ppermute x0 -> x26, starting transfers between devices: none -> 102 us  [the longest x6 22.9 us: scatter_ring(): part = lax.ppermute(part, axis, moves[k])]
    all_to_all x0 -> x5, blocking collectives: none -> 77.6 us  [exchange(): lax.all_to_all(sent, axes, split_axis=0, concat_axis=0, axis_index_groups...]
    ppermute x0 -> x26, waiting for transfers between devices: none -> 46.2 us  [the longest x2 13.1 us: gather_ring(): lax.ppermute(second, 'x', flip)]
    reduce_max x5 -> x12, other arithmetic: 1.99 us -> 15 us  [the longest x6 14.8 us: local_lse(): peak = jnp.max(scores, axis=axis, keepdims=True)]
  transfers between devices with their start and end apart: 4 -> 27, of which waited for: 4 -> 15; matrix products, arithmetic and copies ran while one was open for 2% -> 4% of each run, Pallas kernels for 0% -> 0%
where the time goes in v1:
time: 308 us; the launch traced here: 305 us
  starting transfers between devices  106 us (34%)
  blocking collectives  77.6 us (25%)
  waiting for transfers between devices  58.5 us (19%)
  other arithmetic  26.7 us (9%)
  local copies, waits for them, and re-layouts  12.7 us (4%)
  Pallas kernels  11 us (4%)
  matrix products  10.9 us (4%)
    all_to_all x5, blocking collectives, exchange(): lax.all_to_all(sent, axes, split_axis=0, concat_axis=0, axis_index_groups...  77.6 us
    ppermute x6, starting transfers between devices, scatter_ring(): part = lax.ppermute(part, axis, moves[k])  22.9 us
    ppermute x2, starting transfers between devices, gather_ring(): across = lax.ppermute(pair, axis, ring(4))  15.6 us
    reduce_max x6, other arithmetic, local_lse(): peak = jnp.max(scores, axis=axis, keepdims=True)  14.8 us
    ppermute x2, waiting for transfers between devices, gather_ring(): lax.ppermute(second, 'x', flip)  13.1 us
    ppermute x4, starting transfers between devices, scatter_ring(): got = lax.ppermute(sent, 'x', flip)  13 us
    all_to_all x1, waiting for transfers between devices, exchange(): lax.all_to_all(sent, axes, split_axis=0, concat_axis=0, axis_index_groups...  12.4 us
    pallas_call x1, Pallas kernels, tile(): pl.pallas_call(tile_kernel, out_shape=(jax.ShapeDtypeStruct((rows, width)...  11 us
  transfers between devices with their start and end apart: 27, of which 15 were waited for; matrix products, arithmetic and copies ran while one was open for 4% of the time, Pallas kernels for 0%

profile of v1, /device:TPU:56, one launch (start us, length us, event | category | flops | bytes accessed | tf_op | source)
XLA Modules:
  0.0 305.4 jit_solution(3836458420399334832)
XLA Ops:
  0.6 4.4 %collective-permute-start.6 = (f32[40,512]{1,0:T(8,128)}, f32[40,512]{1,0:T(8,128)S(1)}, u32[]{:S(2)}, u32[]{:S(2)}) collective-permute-start(f32[40,512]{1,0:T(8,128)} %param.3), channel_id=1, source_target_pairs={{0,64},{64,0},{128,192},{192,128},{256,320},{320,256},{384,448},{4... | collective-permute-start | bytes 245768 | tf_op jit(solution)/shard_map/ppermute | solution.py:46
  8.6 6.1 %collective-permute-start.7 = (f32[80,512]{1,0:T(8,128)S(1)}, f32[80,512]{1,0:T(8,128)S(1)}, u32[]{:S(2)}, u32[]{:S(2)}) collective-permute-start(f32[80,512]{1,0:T(8,128)S(1)} %get-tuple-element.27), channel_id=1, source_target_pairs={{0,128},{64,192},{128,256},{192,320},{256,384},{320,448},{384,0},{... | collective-permute-start | bytes 491528 | tf_op jit(solution)/shard_map/ppermute | solution.py:49
  14.7 8.7 %collective-permute-start.10 = (f32[80,512]{1,0:T(8,128)S(1)}, f32[80,512]{1,0:T(8,128)S(1)}, u32[]{:S(2)}, u32[]{:S(2)}) collective-permute-start(f32[80,512]{1,0:T(8,128)S(1)} %get-tuple-element.27), channel_id=1, source_target_pairs={{0,256},{64,320},{128,384},{192,448},{256,0},{320,64},{384,128},{4... | collective-permute-start | bytes 491528 | tf_op jit(solution)/shard_map/ppermute | solution.py:51
  44.0 5.3 %collective-permute-done.11.refs_7_ = f32[2,80,512]{2,1,0:T(8,128)S(1)} collective-permute-done((f32[2,80,512]{2,1,0:T(8,128)S(1)}, f32[2,80,512]{2,1,0:T(8,128)S(1)}, u32[]{:S(2)}, u32[]{:S(2)}) %collective-permute-start.11) | collective-permute-done | bytes 327712 | tf_op jit(solution)/shard_map/ppermute | solution.py:54
  61.5 6.8 %collective-permute-start.4 = (f32[80,512]{1,0:T(8,128)S(1)}, f32[80,512]{1,0:T(8,128)S(1)}, u32[]{:S(2)}, u32[]{:S(2)}) collective-permute-start(f32[80,512]{1,0:T(8,128)S(1)} %get-tuple-element.31), channel_id=1, source_target_pairs={{0,8},{2,10},{4,12},{6,14},{8,0},{10,2},{12,4},{14,6},{1,9},{3,11}... | collective-permute-start | bytes 491528 | tf_op jit(solution)/shard_map/ppermute | solution.py:51
  71.8 4.7 %collective-permute-start.2 = (f32[2,80,512]{2,1,0:T(8,128)S(1)}, f32[2,80,512]{2,1,0:T(8,128)S(1)}, u32[]{:S(2)}, u32[]{:S(2)}) collective-permute-start(f32[2,80,512]{2,1,0:T(8,128)S(1)} %pad_maximum_fusion.refs_0_), channel_id=1, source_target_pairs={{0,48},{16,32},{32,16},{48,0},{1,49},{17,33},{33,17},{49,1},{2,50}... | collective-permute-start | bytes 983048 | tf_op jit(solution)/shard_map/ppermute | solution.py:54
  79.9 4.7 %collective-permute-start.5 = (f32[2,80,512]{2,1,0:T(8,128)S(1)}, f32[2,80,512]{2,1,0:T(8,128)S(1)}, u32[]{:S(2)}, u32[]{:S(2)}) collective-permute-start(f32[2,80,512]{2,1,0:T(8,128)S(1)} %pad_maximum_fusion.1.refs_2_), channel_id=1, source_target_pairs={{0,48},{16,32},{32,16},{48,0},{1,49},{17,33},{33,17},{49,1},{2,50}... | collective-permute-start | bytes 983048 | tf_op jit(solution)/shard_map/ppermute | solution.py:54
  84.6 7.8 %collective-permute-done.5.refs_3_ = f32[2,80,512]{2,1,0:T(8,128)S(1)} collective-permute-done((f32[2,80,512]{2,1,0:T(8,128)S(1)}, f32[2,80,512]{2,1,0:T(8,128)S(1)}, u32[]{:S(2)}, u32[]{:S(2)}) %collective-permute-start.5) | collective-permute-done | bytes 327712 | tf_op jit(solution)/shard_map/ppermute | solution.py:54
  94.3 11.0 %shard_map.57 = (f32[640,512]{1,0:T(8,128)S(1)}, f32[1280,512]{1,0:T(8,128)}, f32[640,1280]{1,0:T(8,128)}) custom-call(f32[2,80,512]{2,1,0:T(8,128)S(1)} %pad_maximum_fusion.refs_0_, f32[2,80,512]{2,1,0:T(8,128)S(1)} %collective-permute-done.2.refs_1_, f32[2,80,512]{2,1,0:T(8,128)S(1)} %pad_maximum_fusion.1.refs_2_, ...), custom_call_target="tpu_custom_call" | custom-call | tf_op jit(solution)/shard_map/pallas_call | solution.py:111
  109.0 20.3 %all_to_all.30 = f32[16,5,128]{2,1,0:T(8,128)S(1)} all-to-all(f32[16,5,128]{2,1,0:T(8,128)S(1)} %broadcast_in_dim.12), channel_id=1, replica_groups={{0,2,4,6,8,10,12,14,48,50,52,54,56,58,60,62},{16,18,20,22,24,26,28,30,3..., dimensions={0} | all-to-all | bytes 81920 | tf_op jit(solution)/shard_map/all_to_all | solution.py:144
  133.0 17.5 %all_to_all.31 = f32[32,10,128]{2,1,0:T(8,128)S(1)} all-to-all(f32[32,10,128]{2,1,0:T(8,128)S(1)} %broadcast_in_dim.13), channel_id=1, replica_groups={{0,1,16,17,64,65,80,81,128,129,144,145,192,193,208,209,256,257,272,273,..., dimensions={0} | all-to-all | bytes 327680 | tf_op jit(solution)/shard_map/all_to_all | solution.py:144
  154.3 12.4 %all_to_all.32 = f32[16,5,128]{2,1,0:T(8,128)S(1)} all-to-all(f32[16,5,128]{2,1,0:T(8,128)S(1)} %broadcast_in_dim.14), channel_id=1, replica_groups={{0,2,4,6,8,10,12,14,48,50,52,54,56,58,60,62},{16,18,20,22,24,26,28,30,3..., dimensions={0} | all-to-all | bytes 81920 | tf_op jit(solution)/shard_map/all_to_all | solution.py:144
  170.4 15.2 %all_to_all.33 = f32[32,10,128]{2,1,0:T(8,128)S(1)} all-to-all(f32[32,10,128]{2,1,0:T(8,128)S(1)} %broadcast_in_dim.15), channel_id=1, replica_groups={{0,1,16,17,64,65,80,81,128,129,144,145,192,193,208,209,256,257,272,273,..., dimensions={0} | all-to-all | bytes 327680 | tf_op jit(solution)/shard_map/all_to_all | solution.py:144
  189.4 12.2 %all_to_all.34 = f32[16,5,128]{2,1,0:T(8,128)S(1)} all-to-all(f32[16,5,128]{2,1,0:T(8,128)S(1)} %broadcast_in_dim.16), channel_id=1, replica_groups={{0,2,4,6,8,10,12,14,48,50,52,54,56,58,60,62},{16,18,20,22,24,26,28,30,3..., dimensions={0} | all-to-all | bytes 81920 | tf_op jit(solution)/shard_map/all_to_all | solution.py:144
  206.0 3.9 %all-to-all-start.5 = ((f32[32,10,128]{2,1,0:T(8,128)}), f32[32,10,128]{2,1,0:T(8,128)S(1)}, u32[]{:S(2)}, u32[]{:S(2)}) async-start(f32[32,10,128]{2,1,0:T(8,128)} %broadcast_in_dim.17), calls=%async_computation.5 | async-start | bytes 524288 | tf_op jit(solution)/shard_map/all_to_all | solution.py:144
  209.9 12.4 %all-to-all-done.5 = f32[32,10,128]{2,1,0:T(8,128)S(1)} async-done(((f32[32,10,128]{2,1,0:T(8,128)}), f32[32,10,128]{2,1,0:T(8,128)S(1)}, u32[]{:S(2)}, u32[]{:S(2)}) %all-to-all-start.5) | async-done | bytes 163872 | tf_op jit(solution)/shard_map/all_to_all | solution.py:144
  225.5 5.4 %multiply_subtract_fusion = f32[1280,512]{1,0:T(8,128)S(1)} fusion(f32[1280,512]{1,0:T(8,128)} %get-tuple-element.9, f32[1280]{0:T(1024)S(1)} %get-tuple-element.10, f32[640,512]{1,0:T(8,128)S(1)} %get-tuple-element.8, f32[640,1280]{1,0:T(8,128)S(1)} %copy-done.10, f32[1280]{0:T(1024)S(1)} %bitcast.155, f32[640]{0:T(1024)S(1)} %bitcast.152), kind=kOutput, calls=%fused_computation.19 | convolution fusion | flops 2520350720 | bytes 9843200 | tf_op jit(solution)/shard_map/dot_general | solution.py:184
  236.5 5.6 %multiply_subtract_fusion.1 = f32[640,512]{1,0:T(8,128)S(1)} fusion(f32[640,512]{1,0:T(8,128)S(1)} %get-tuple-element.8, f32[640]{0:T(1024)S(1)} %get-tuple-element.11, f32[1280,512]{1,0:T(8,128)} %get-tuple-element.9, f32[640,1280]{1,0:T(8,128)} %get-tuple-element.7, f32[1280]{0:T(1024)S(1)} %bitcast.156, f32[640]{0:T(1024)S(1)} %bitcast.153), kind=kOutput, calls=%fused_computation.22 | convolution fusion | flops 2519695360 | bytes 8529920 | tf_op jit(solution)/shard_map/dot_general | solution.py:195
  244.8 4.6 %collective-permute-start.13 = (f32[2,80,512]{2,1,0:T(8,128)S(1)}, f32[2,80,512]{2,1,0:T(8,128)S(1)}, u32[]{:S(2)}, u32[]{:S(2)}) collective-permute-start(f32[2,80,512]{2,1,0:T(8,128)S(1)} %pad_maximum_fusion.4), channel_id=1, source_target_pairs={{0,48},{16,32},{32,16},{48,0},{1,49},{17,33},{33,17},{49,1},{2,50}... | collective-permute-start | bytes 983048 | tf_op jit(solution)/shard_map/ppermute | solution.py:130
  256.2 6.3 %collective-permute-done.13 = f32[2,80,512]{2,1,0:T(8,128)S(1)} collective-permute-done((f32[2,80,512]{2,1,0:T(8,128)S(1)}, f32[2,80,512]{2,1,0:T(8,128)S(1)}, u32[]{:S(2)}, u32[]{:S(2)}) %collective-permute-start.13) | collective-permute-done | bytes 327712 | tf_op jit(solution)/shard_map/ppermute | solution.py:130
  265.1 6.2 %collective-permute-start.14 = (f32[80,512]{1,0:T(8,128)S(1)}, f32[80,512]{1,0:T(8,128)S(1)}, u32[]{:S(2)}, u32[]{:S(2)}) collective-permute-start(f32[80,512]{1,0:T(8,128)S(1)} %get-tuple-element.15), channel_id=1, source_target_pairs={{0,8},{2,10},{4,12},{6,14},{8,0},{10,2},{12,4},{14,6},{1,9},{3,11}... | collective-permute-start | bytes 491528 | tf_op jit(solution)/shard_map/ppermute | solution.py:134
  271.3 3.7 %collective-permute-start.15 = (f32[80,512]{1,0:T(8,128)S(1)}, f32[80,512]{1,0:T(8,128)S(1)}, u32[]{:S(2)}, u32[]{:S(2)}) collective-permute-start(f32[80,512]{1,0:T(8,128)S(1)} %get-tuple-element.14), channel_id=1, source_target_pairs={{0,4},{2,6},{4,8},{6,10},{8,12},{10,14},{12,0},{14,2},{1,5},{3,7},... | collective-permute-start | bytes 491528 | tf_op jit(solution)/shard_map/ppermute | solution.py:134
  277.8 5.9 %collective-permute-start.21 = (f32[80,512]{1,0:T(8,128)S(1)}, f32[80,512]{1,0:T(8,128)S(1)}, u32[]{:S(2)}, u32[]{:S(2)}) collective-permute-start(f32[80,512]{1,0:T(8,128)S(1)} %get-tuple-element.13), channel_id=1, source_target_pairs={{0,256},{64,320},{128,384},{192,448},{256,0},{320,64},{384,128},{4... | collective-permute-start | bytes 491528 | tf_op jit(solution)/shard_map/ppermute | solution.py:134
  295.4 6.8 %collective-permute-start.25 = (f32[40,512]{1,0:T(8,128)S(1)}, f32[40,512]{1,0:T(8,128)S(1)}, u32[]{:S(2)}, u32[]{:S(2)}) collective-permute-start(f32[40,512]{1,0:T(8,128)S(1)} %dynamic-slice_bitcast_fusion.9), channel_id=1, source_target_pairs={{0,64},{64,0},{128,192},{192,128},{256,320},{320,256},{384,448},{4... | collective-permute-start | bytes 245768 | tf_op jit(solution)/shard_map/ppermute | solution.py:137
  (143 shorter events, 106.1 us)
Async XLA Ops:
  8.6 19.2 %collective-permute-start.7 = (f32[80,512]{1,0:T(8,128)S(1)}, f32[80,512]{1,0:T(8,128)S(1)}, u32[]{:S(2)}, u32[]{:S(2)}) collective-permute-start(f32[80,512]{1,0:T(8,128)S(1)} %get-tuple-element.27), channel_id=1, source_target_pairs={{0,128},{64,192},{128,256},{192,320},{256,384},{320,448},{384,0},{... | collective-permute-start | bytes 491528 | tf_op jit(solution)/shard_map/ppermute | solution.py:49
  14.7 20.2 %collective-permute-start.10 = (f32[80,512]{1,0:T(8,128)S(1)}, f32[80,512]{1,0:T(8,128)S(1)}, u32[]{:S(2)}, u32[]{:S(2)}) collective-permute-start(f32[80,512]{1,0:T(8,128)S(1)} %get-tuple-element.27), channel_id=1, source_target_pairs={{0,256},{64,320},{128,384},{192,448},{256,0},{320,64},{384,128},{4... | collective-permute-start | bytes 491528 | tf_op jit(solution)/shard_map/ppermute | solution.py:51
  23.5 14.3 %collective-permute-start.9 = (f32[80,512]{1,0:T(8,128)S(1)}, f32[80,512]{1,0:T(8,128)S(1)}, u32[]{:S(2)}, u32[]{:S(2)}) collective-permute-start(f32[80,512]{1,0:T(8,128)S(1)} %get-tuple-element.27), channel_id=1, source_target_pairs={{0,384},{64,448},{128,0},{192,64},{256,128},{320,192},{384,256},{4... | collective-permute-start | bytes 491528 | tf_op jit(solution)/shard_map/ppermute | solution.py:50
  27.8 14.0 %collective-permute-start.8 = (f32[2,80,512]{2,1,0:T(8,128)S(1)}, f32[2,80,512]{2,1,0:T(8,128)S(1)}, u32[]{:S(2)}, u32[]{:S(2)}) collective-permute-start(f32[2,80,512]{2,1,0:T(8,128)S(1)} %pad_maximum_fusion.2.refs_4_), channel_id=1, source_target_pairs={{0,16},{16,0},{32,48},{48,32},{1,17},{17,1},{33,49},{49,33},{2,18}... | collective-permute-start | bytes 983048 | tf_op jit(solution)/shard_map/ppermute | solution.py:54
  37.8 11.5 %collective-permute-start.11 = (f32[2,80,512]{2,1,0:T(8,128)S(1)}, f32[2,80,512]{2,1,0:T(8,128)S(1)}, u32[]{:S(2)}, u32[]{:S(2)}) collective-permute-start(f32[2,80,512]{2,1,0:T(8,128)S(1)} %pad_maximum_fusion.3.refs_6_), channel_id=1, source_target_pairs={{0,16},{16,0},{32,48},{48,32},{1,17},{17,1},{33,49},{49,33},{2,18}... | collective-permute-start | bytes 983048 | tf_op jit(solution)/shard_map/ppermute | solution.py:54
  50.1 42.3 %collective-permute-start.12 = (f32[8,80,512]{2,1,0:T(8,128)}, f32[8,80,512]{2,1,0:T(8,128)S(1)}, u32[]{:S(2)}, u32[]{:S(2)}) collective-permute-start(f32[8,80,512]{2,1,0:T(8,128)} %constant_dynamic-update-slice_fusion), channel_id=1, source_target_pairs={{0,1},{1,0},{2,3},{3,2},{4,5},{5,4},{6,7},{7,6},{8,9},{9,8},{10,11... | collective-permute-start | bytes 3932168 | tf_op jit(solution)/shard_map/ppermute | solution.py:166
  58.8 12.9 %collective-permute-start.1 = (f32[80,512]{1,0:T(8,128)S(1)}, f32[80,512]{1,0:T(8,128)S(1)}, u32[]{:S(2)}, u32[]{:S(2)}) collective-permute-start(f32[80,512]{1,0:T(8,128)S(1)} %get-tuple-element.31), channel_id=1, source_target_pairs={{0,4},{2,6},{4,8},{6,10},{8,12},{10,14},{12,0},{14,2},{1,5},{3,7},... | collective-permute-start | bytes 491528 | tf_op jit(solution)/shard_map/ppermute | solution.py:49
  61.5 16.0 %collective-permute-start.4 = (f32[80,512]{1,0:T(8,128)S(1)}, f32[80,512]{1,0:T(8,128)S(1)}, u32[]{:S(2)}, u32[]{:S(2)}) collective-permute-start(f32[80,512]{1,0:T(8,128)S(1)} %get-tuple-element.31), channel_id=1, source_target_pairs={{0,8},{2,10},{4,12},{6,14},{8,0},{10,2},{12,4},{14,6},{1,9},{3,11}... | collective-permute-start | bytes 491528 | tf_op jit(solution)/shard_map/ppermute | solution.py:51
  68.4 11.5 %collective-permute-start.3 = (f32[80,512]{1,0:T(8,128)S(1)}, f32[80,512]{1,0:T(8,128)S(1)}, u32[]{:S(2)}, u32[]{:S(2)}) collective-permute-start(f32[80,512]{1,0:T(8,128)S(1)} %get-tuple-element.31), channel_id=1, source_target_pairs={{0,12},{2,14},{4,0},{6,2},{8,4},{10,6},{12,8},{14,10},{1,13},{3,15... | collective-permute-start | bytes 491528 | tf_op jit(solution)/shard_map/ppermute | solution.py:50
  71.8 12.8 %collective-permute-start.2 = (f32[2,80,512]{2,1,0:T(8,128)S(1)}, f32[2,80,512]{2,1,0:T(8,128)S(1)}, u32[]{:S(2)}, u32[]{:S(2)}) collective-permute-start(f32[2,80,512]{2,1,0:T(8,128)S(1)} %pad_maximum_fusion.refs_0_), channel_id=1, source_target_pairs={{0,48},{16,32},{32,16},{48,0},{1,49},{17,33},{33,17},{49,1},{2,50}... | collective-permute-start | bytes 983048 | tf_op jit(solution)/shard_map/ppermute | solution.py:54
  79.9 12.5 %collective-permute-start.5 = (f32[2,80,512]{2,1,0:T(8,128)S(1)}, f32[2,80,512]{2,1,0:T(8,128)S(1)}, u32[]{:S(2)}, u32[]{:S(2)}) collective-permute-start(f32[2,80,512]{2,1,0:T(8,128)S(1)} %pad_maximum_fusion.1.refs_2_), channel_id=1, source_target_pairs={{0,48},{16,32},{32,16},{48,0},{1,49},{17,33},{33,17},{49,1},{2,50}... | collective-permute-start | bytes 983048 | tf_op jit(solution)/shard_map/ppermute | solution.py:54
  206.0 16.2 %all-to-all-start.5 = ((f32[32,10,128]{2,1,0:T(8,128)}), f32[32,10,128]{2,1,0:T(8,128)S(1)}, u32[]{:S(2)}, u32[]{:S(2)}) async-start(f32[32,10,128]{2,1,0:T(8,128)} %broadcast_in_dim.17), calls=%async_computation.5 | async-start | bytes 524288 | tf_op jit(solution)/shard_map/all_to_all | solution.py:144
  233.6 15.8 %collective-permute-start.19 = (f32[640,512]{1,0:T(8,128)}, f32[640,512]{1,0:T(8,128)S(1)}, u32[]{:S(2)}, u32[]{:S(2)}) collective-permute-start(f32[640,512]{1,0:T(8,128)} %dynamic-slice_bitcast_fusion), channel_id=1, source_target_pairs={{0,1},{1,0},{2,3},{3,2},{4,5},{5,4},{6,7},{7,6},{8,9},{9,8},{10,11... | collective-permute-start | bytes 3932168 | tf_op jit(solution)/shard_map/ppermute | solution.py:192
  242.2 14.1 %collective-permute-start.16 = (f32[2,80,512]{2,1,0:T(8,128)S(1)}, f32[2,80,512]{2,1,0:T(8,128)S(1)}, u32[]{:S(2)}, u32[]{:S(2)}) collective-permute-start(f32[2,80,512]{2,1,0:T(8,128)S(1)} %pad_maximum_fusion.5), channel_id=1, source_target_pairs={{0,48},{16,32},{32,16},{48,0},{1,49},{17,33},{33,17},{49,1},{2,50}... | collective-permute-start | bytes 983048 | tf_op jit(solution)/shard_map/ppermute | solution.py:130
  244.8 17.8 %collective-permute-start.13 = (f32[2,80,512]{2,1,0:T(8,128)S(1)}, f32[2,80,512]{2,1,0:T(8,128)S(1)}, u32[]{:S(2)}, u32[]{:S(2)}) collective-permute-start(f32[2,80,512]{2,1,0:T(8,128)S(1)} %pad_maximum_fusion.4), channel_id=1, source_target_pairs={{0,48},{16,32},{32,16},{48,0},{1,49},{17,33},{33,17},{49,1},{2,50}... | collective-permute-start | bytes 983048 | tf_op jit(solution)/shard_map/ppermute | solution.py:130
  249.8 25.2 %collective-permute-start.23 = (f32[2,80,512]{2,1,0:T(8,128)S(1)}, f32[2,80,512]{2,1,0:T(8,128)S(1)}, u32[]{:S(2)}, u32[]{:S(2)}) collective-permute-start(f32[2,80,512]{2,1,0:T(8,128)S(1)} %pad_maximum_fusion.7), channel_id=1, source_target_pairs={{0,16},{16,0},{32,48},{48,32},{1,17},{17,1},{33,49},{49,33},{2,18}... | collective-permute-start | bytes 983048 | tf_op jit(solution)/shard_map/ppermute | solution.py:130
  252.0 23.0 %collective-permute-start.20 = (f32[2,80,512]{2,1,0:T(8,128)S(1)}, f32[2,80,512]{2,1,0:T(8,128)S(1)}, u32[]{:S(2)}, u32[]{:S(2)}) collective-permute-start(f32[2,80,512]{2,1,0:T(8,128)S(1)} %pad_maximum_fusion.6), channel_id=1, source_target_pairs={{0,16},{16,0},{32,48},{48,32},{1,17},{17,1},{33,49},{49,33},{2,18}... | collective-permute-start | bytes 983048 | tf_op jit(solution)/shard_map/ppermute | solution.py:130
  262.6 21.1 %collective-permute-start.17 = (f32[80,512]{1,0:T(8,128)S(1)}, f32[80,512]{1,0:T(8,128)S(1)}, u32[]{:S(2)}, u32[]{:S(2)}) collective-permute-start(f32[80,512]{1,0:T(8,128)S(1)} %get-tuple-element.21), channel_id=1, source_target_pairs={{0,12},{2,14},{4,0},{6,2},{8,4},{10,6},{12,8},{14,10},{1,13},{3,15... | collective-permute-start | bytes 491528 | tf_op jit(solution)/shard_map/ppermute | solution.py:134
  265.1 20.6 %collective-permute-start.14 = (f32[80,512]{1,0:T(8,128)S(1)}, f32[80,512]{1,0:T(8,128)S(1)}, u32[]{:S(2)}, u32[]{:S(2)}) collective-permute-start(f32[80,512]{1,0:T(8,128)S(1)} %get-tuple-element.15), channel_id=1, source_target_pairs={{0,8},{2,10},{4,12},{6,14},{8,0},{10,2},{12,4},{14,6},{1,9},{3,11}... | collective-permute-start | bytes 491528 | tf_op jit(solution)/shard_map/ppermute | solution.py:134
  271.3 15.5 %collective-permute-start.15 = (f32[80,512]{1,0:T(8,128)S(1)}, f32[80,512]{1,0:T(8,128)S(1)}, u32[]{:S(2)}, u32[]{:S(2)}) collective-permute-start(f32[80,512]{1,0:T(8,128)S(1)} %get-tuple-element.14), channel_id=1, source_target_pairs={{0,4},{2,6},{4,8},{6,10},{8,12},{10,14},{12,0},{14,2},{1,5},{3,7},... | collective-permute-start | bytes 491528 | tf_op jit(solution)/shard_map/ppermute | solution.py:134
  275.1 14.0 %collective-permute-start.24 = (f32[80,512]{1,0:T(8,128)S(1)}, f32[80,512]{1,0:T(8,128)S(1)}, u32[]{:S(2)}, u32[]{:S(2)}) collective-permute-start(f32[80,512]{1,0:T(8,128)S(1)} %get-tuple-element.16), channel_id=1, source_target_pairs={{0,384},{64,448},{128,0},{192,64},{256,128},{320,192},{384,256},{4... | collective-permute-start | bytes 491528 | tf_op jit(solution)/shard_map/ppermute | solution.py:134
  277.8 14.8 %collective-permute-start.21 = (f32[80,512]{1,0:T(8,128)S(1)}, f32[80,512]{1,0:T(8,128)S(1)}, u32[]{:S(2)}, u32[]{:S(2)}) collective-permute-start(f32[80,512]{1,0:T(8,128)S(1)} %get-tuple-element.13), channel_id=1, source_target_pairs={{0,256},{64,320},{128,384},{192,448},{256,0},{320,64},{384,128},{4... | collective-permute-start | bytes 491528 | tf_op jit(solution)/shard_map/ppermute | solution.py:134
  283.7 11.6 %collective-permute-start.22 = (f32[80,512]{1,0:T(8,128)S(1)}, f32[80,512]{1,0:T(8,128)S(1)}, u32[]{:S(2)}, u32[]{:S(2)}) collective-permute-start(f32[80,512]{1,0:T(8,128)S(1)} %get-tuple-element.12), channel_id=1, source_target_pairs={{0,128},{64,192},{128,256},{192,320},{256,384},{320,448},{384,0},{... | collective-permute-start | bytes 491528 | tf_op jit(solution)/shard_map/ppermute | solution.py:134
  286.9 15.3 %collective-permute-start.18 = (f32[40,512]{1,0:T(8,128)S(1)}, f32[40,512]{1,0:T(8,128)S(1)}, u32[]{:S(2)}, u32[]{:S(2)}) collective-permute-start(f32[40,512]{1,0:T(8,128)S(1)} %dynamic-slice_bitcast_fusion.10), channel_id=1, source_target_pairs={{0,2},{2,0},{4,6},{6,4},{8,10},{10,8},{12,14},{14,12},{1,3},{3,1},... | collective-permute-start | bytes 245768 | tf_op jit(solution)/shard_map/ppermute | solution.py:137
  (17 other events, 118.4 us)

commit v2 on v0

v2 whole, which is shorter than its diff:
```python
import math

import jax
import jax.numpy as jnp
from jax import lax
from jax.sharding import Mesh
from jax.sharding import PartitionSpec as P

ITERS = 3
ENTROPY_REG = 0.05
NZ, NX, NY, NC = 8, 4, 8, 2
LANES = 128

A_OF_X = (0, 0, 1, 1)
B_OF_X = (0, 1, 1, 0)
FLIP_A = [(x, NX - 1 - x) for x in range(NX)]
FLIP_B = [(x, x ^ 1) for x in range(NX)]
SWAP = [(0, 1), (1, 0)]
X_OF_AB = {(A_OF_X[x], B_OF_X[x]): x for x in range(NX)}

ROW_GROUPS = [[X_OF_AB[a, b] * NY + y for a in range(2) for y in range(NY)] for b in range(2)]
COL_GROUPS = [
    [(z * NX + X_OF_AB[a, b]) * NC + c for z in range(NZ) for b in range(2) for c in range(NC)]
    for a in range(2)
]

SIDE_GROUPS = [
    [z * NX + X_OF_AB[a, b] for z in range(NZ) for b in range(2)] for a in range(2)
]


def take(buffer, index):
    return lax.dynamic_index_in_dim(buffer, index, 0, keepdims=False)


def all_to_all(blocks, axes, groups):
    return lax.all_to_all(
        blocks, axes, split_axis=0, concat_axis=0, axis_index_groups=groups, tiled=True
    )


def gather(shard, axes, groups):
    blocks = jnp.broadcast_to(shard[None], (len(groups[0]),) + shard.shape)
    return all_to_all(blocks, axes, groups).reshape(-1, shard.shape[1])


def scatter(partial, axes, groups):
    count = len(groups[0])
    blocks = partial.reshape(count, partial.shape[0] // count, partial.shape[1])
    return jnp.sum(all_to_all(blocks, axes, groups), axis=0)


def exchange(local, axes, groups, count):
    size = local.shape[0]
    flat = local.reshape(1, size // LANES, LANES)
    sent = jnp.broadcast_to(flat, (count, size // LANES, LANES))
    got = all_to_all(sent, axes, groups)
    peak = jnp.max(got, axis=0)
    total = jnp.sum(jnp.exp(got - peak[None]), axis=0)
    return (peak + jnp.log(total)).reshape(size)


def local_lse(scores, axis):
    peak = jnp.max(scores, axis=axis, keepdims=True)
    total = jnp.sum(jnp.exp(scores - peak), axis=axis)
    return jnp.squeeze(peak, axis) + jnp.log(total)


def per_device(src_emb, tgt_emb):
    rows, width = src_emb.shape
    z, x, y, c = (lax.axis_index(name) for name in ("z", "x", "y", "c"))
    a = x // 2
    b = (x // 2) ^ (x % 2)
    total_points = rows * NZ * NX * NY * NC
    mine = gather(tgt_emb, ("z", "x"), SIDE_GROUPS)
    src_block = gather(src_emb, ("x", "y"), ROW_GROUPS)
    other = lax.ppermute(mine, "c", SWAP)
    tgt_block = jnp.where(
        c == 0, jnp.concatenate([mine, other]), jnp.concatenate([other, mine])
    )
    left_sq = jnp.sum(src_block * src_block, axis=1)
    right_sq = jnp.sum(tgt_block * tgt_block, axis=1)
    cross = jnp.dot(
        src_block,
        tgt_block.T,
        preferred_element_type=jnp.float32,
        precision=lax.Precision.HIGHEST,
    )
    cost = (left_sq[:, None] + right_sq[None, :] - 2.0 * cross) / width
    tgt_pot = jnp.zeros((tgt_block.shape[0],), jnp.float32)
    log_total = math.log(total_points)
    for _ in range(ITERS):
        lse = local_lse((tgt_pot[None, :] - cost) / ENTROPY_REG, 1)
        lse = exchange(lse, ("x", "y"), ROW_GROUPS, 2 * NY)
        src_pot = -ENTROPY_REG * (lse - log_total)
        lse = local_lse((src_pot[:, None] - cost) / ENTROPY_REG, 0)
        lse = exchange(lse, ("z", "x", "c"), COL_GROUPS, 2 * NZ * NC)
        tgt_pot = -ENTROPY_REG * (lse - log_total)
    weight = jnp.exp((src_pot[:, None] + tgt_pot[None, :] - cost) / ENTROPY_REG)
    row_mass = jnp.sum(weight, axis=1)
    col_mass = jnp.sum(weight, axis=0)
    pulled = lax.dot_general(
        weight,
        src_block,
        (((0,), (0,)), ((), ())),
        precision=lax.Precision.HIGH,
        preferred_element_type=jnp.float32,
    )
    tgt_part = (col_mass[:, None] * tgt_block - pulled).reshape(NC, -1, width)
    across = lax.ppermute(take(tgt_part, 1 - c), "c", SWAP)
    tgt_sum = scatter(take(tgt_part, c) + across, ("z", "x"), SIDE_GROUPS)
    pushed = jnp.dot(
        weight, tgt_block, preferred_element_type=jnp.float32, precision=lax.Precision.HIGH
    )
    src_sum = scatter(row_mass[:, None] * src_block - pushed, ("x", "y"), ROW_GROUPS)
    src_piece = take(src_pot.reshape(-1, rows), a * NY + y)
    tgt_piece = take(tgt_pot.reshape(-1, rows), (c * NZ + z) * 2 + b)
    return src_piece, tgt_piece, src_sum / total_points, tgt_sum / total_points


def solution(mesh):
    grid = Mesh(mesh.devices.reshape(NZ, NX, NY, NC), ("z", "x", "y", "c"))
    split = ("z", "x", "y", "c")
    return jax.shard_map(
        per_device,
        mesh=grid,
        in_specs=(P(split, None), P(split, None)),
        out_specs=(P(split), P(split), P(split, None), P(split, None)),
        check_vma=False,
    )
```

time: 1040 us -> 279 us (0.27)
  blocking collectives: 569 us -> 131 us
  waiting for transfers between devices: 405 us -> 77 us
  starting transfers between devices: 0.38 us -> 22.4 us
  between operations: 13.9 us -> 0.99 us
    pmax x6 -> x0, blocking collectives: 286 us -> none  [the longest x3 219 us: per_device(): peak_val = lax.pmax(local_peak, 'src')]
    psum x6 -> x0, blocking collectives: 283 us -> none  [the longest x3 212 us: per_device(): lax.psum(jnp.sum(jnp.exp(scores - peak_val[None, :]), axis=0), 'src')]
    reduce_scatter x2 -> x0, waiting for transfers between devices: 271 us -> none  [the longest x1 228 us: per_device(): lax.psum_scatter(col_mass[:, None] * tgt_block - pulled, 'src', scatter_d...]
    all_gather x2 -> x0, waiting for transfers between devices: 132 us -> none  [the longest x1 86.9 us: per_device(): tgt_block = lax.all_gather(tgt_emb, 'src', axis=0, tiled=True)]
    all_to_all x0 -> x7, blocking collectives: none -> 131 us  [all_to_all(): lax.all_to_all(blocks, axes, split_axis=0, concat_axis=0, axis_index_grou...]
    all_to_all x0 -> x3, waiting for transfers between devices: none -> 74 us  [all_to_all(): lax.all_to_all(blocks, axes, split_axis=0, concat_axis=0, axis_index_grou...]
    all_to_all x0 -> x3, starting transfers between devices: none -> 18.5 us  [all_to_all(): lax.all_to_all(blocks, axes, split_axis=0, concat_axis=0, axis_index_grou...]
  transfers between devices with their start and end apart: 4 -> 5, of which waited for: 4 -> 4; matrix products, arithmetic and copies ran while one was open for 2% -> 4% of each run, Pallas kernels for 0% -> 0%
where the time goes in v2:
time: 279 us; the launch traced here: 276 us
  blocking collectives  131 us (47%)
  waiting for transfers between devices  77 us (28%)
  matrix products  22.6 us (8%)
  starting transfers between devices  22.4 us (8%)
  other arithmetic  16 us (6%)
  local copies, waits for them, and re-layouts  5.54 us (2%)
    all_to_all x7, blocking collectives, all_to_all(): lax.all_to_all(blocks, axes, split_axis=0, concat_axis=0, axis_index_grou...  131 us
    all_to_all x3, waiting for transfers between devices, all_to_all(): lax.all_to_all(blocks, axes, split_axis=0, concat_axis=0, axis_index_grou...  74 us
    all_to_all x3, starting transfers between devices, all_to_all(): lax.all_to_all(blocks, axes, split_axis=0, concat_axis=0, axis_index_grou...  18.5 us
    dot_general x1, matrix products, per_device(): jnp.dot(src_block, tgt_block.T, preferred_element_type=jnp.float32, preci...  9.75 us
    dot_general x1, matrix products, per_device(): lax.dot_general(weight, src_block, (((0,), (0,)), ((), ())), precision=la...  6.62 us
    dot_general x1, matrix products, per_device(): jnp.dot(weight, tgt_block, preferred_element_type=jnp.float32, precision=...  6.22 us
  transfers between devices with their start and end apart: 5, of which 4 were waited for; matrix products, arithmetic and copies ran while one was open for 4% of the time, Pallas kernels for 0%

profile of v2, /device:TPU:56, one launch (start us, length us, event | category | flops | bytes accessed | tf_op | source)
XLA Modules:
  0.0 275.9 jit_solution(16293428604825650066)
XLA Ops:
  1.7 45.7 %all_to_all.50 = f32[16,40,512]{2,1,0:T(8,128)S(1)} all-to-all(f32[16,40,512]{2,1,0:T(8,128)S(1)} %broadcast_in_dim.17), channel_id=1, replica_groups={{0,16,64,80,128,144,192,208,256,272,320,336,384,400,448,464},{48,32,112..., dimensions={0} | all-to-all | bytes 2621440 | tf_op jit(solution)/shard_map/all_to_all | solution.py:37
  47.5 1.4 broadcast_in_dim.16
  48.8 8.4 %all-to-all-start = ((f32[16,40,512]{2,1,0:T(8,128)}), f32[16,40,512]{2,1,0:T(8,128)S(1)}, u32[]{:S(2)}, u32[]{:S(2)}) async-start(f32[16,40,512]{2,1,0:T(8,128)} %broadcast_in_dim.16), calls=%async_computation | async-start | bytes 2621440 | tf_op jit(solution)/shard_map/all_to_all | solution.py:37
  57.3 1.9 collective-permute-start
  59.2 28.2 %all-to-all-done = f32[16,40,512]{2,1,0:T(8,128)S(1)} async-done(((f32[16,40,512]{2,1,0:T(8,128)}), f32[16,40,512]{2,1,0:T(8,128)S(1)}, u32[]{:S(2)}, u32[]{:S(2)}) %all-to-all-start) | async-done | bytes 1310752 | tf_op jit(solution)/shard_map/all_to_all | solution.py:37
  87.7 2.2 multiply_reduce_fusion
  90.0 9.8 %fusion.3 = (f32[640]{0:T(1024)S(1)}, f32[640,1280]{0,1:T(8,128)S(1)}) fusion(f32[640,512]{1,0:T(8,128)} %bitcast.48, f32[640,512]{1,0:T(8,128)} %collective-permute-done, f32[640,512]{1,0:T(8,128)} %bitcast.45, pred[]{:T(512)S(6)} %eq.5, f32[1280]{0:T(1024)S(1)} %multiply_reduce_fusion, f32[640]{0:T(1024)S(1)} %add.217), kind=kOutput, calls=%fused_computation.17 | convolution fusion | flops 5040864768 | bytes 7219201 | tf_op jit(solution)/shard_map/dot_general | solution.py:83
  100.4 14.0 %all_to_all.51 = f32[16,5,128]{2,1,0:T(8,128)S(1)} all-to-all(f32[16,5,128]{2,1,0:T(8,128)S(1)} %broadcast_in_dim.18), channel_id=1, replica_groups={{0,2,4,6,8,10,12,14,48,50,52,54,56,58,60,62},{16,18,20,22,24,26,28,30,3..., dimensions={0} | all-to-all | bytes 81920 | tf_op jit(solution)/shard_map/all_to_all | solution.py:37
  115.7 16.5 %all_to_all.52 = f32[32,10,128]{2,1,0:T(8,128)S(1)} all-to-all(f32[32,10,128]{2,1,0:T(8,128)S(1)} %broadcast_in_dim.19), channel_id=1, replica_groups={{0,1,16,17,64,65,80,81,128,129,144,145,192,193,208,209,256,257,272,273,..., dimensions={0} | all-to-all | bytes 327680 | tf_op jit(solution)/shard_map/all_to_all | solution.py:37
  133.5 12.5 %all_to_all.53 = f32[16,5,128]{2,1,0:T(8,128)S(1)} all-to-all(f32[16,5,128]{2,1,0:T(8,128)S(1)} %broadcast_in_dim.20), channel_id=1, replica_groups={{0,2,4,6,8,10,12,14,48,50,52,54,56,58,60,62},{16,18,20,22,24,26,28,30,3..., dimensions={0} | all-to-all | bytes 81920 | tf_op jit(solution)/shard_map/all_to_all | solution.py:37
  147.4 15.1 %all_to_all.54 = f32[32,10,128]{2,1,0:T(8,128)S(1)} all-to-all(f32[32,10,128]{2,1,0:T(8,128)S(1)} %broadcast_in_dim.21), channel_id=1, replica_groups={{0,1,16,17,64,65,80,81,128,129,144,145,192,193,208,209,256,257,272,273,..., dimensions={0} | all-to-all | bytes 327680 | tf_op jit(solution)/shard_map/all_to_all | solution.py:37
  163.7 12.4 %all_to_all.55 = f32[16,5,128]{2,1,0:T(8,128)S(1)} all-to-all(f32[16,5,128]{2,1,0:T(8,128)S(1)} %broadcast_in_dim.22), channel_id=1, replica_groups={{0,2,4,6,8,10,12,14,48,50,52,54,56,58,60,62},{16,18,20,22,24,26,28,30,3..., dimensions={0} | all-to-all | bytes 81920 | tf_op jit(solution)/shard_map/all_to_all | solution.py:37
  177.4 15.2 %all_to_all.56 = f32[32,10,128]{2,1,0:T(8,128)S(1)} all-to-all(f32[32,10,128]{2,1,0:T(8,128)S(1)} %broadcast_in_dim.23), channel_id=1, replica_groups={{0,1,16,17,64,65,80,81,128,129,144,145,192,193,208,209,256,257,272,273,..., dimensions={0} | all-to-all | bytes 327680 | tf_op jit(solution)/shard_map/all_to_all | solution.py:37
  194.4 6.2 %convolution_subtract_fusion = f32[640,512]{1,0:T(8,128)} fusion(f32[640,512]{1,0:T(8,128)S(1)} %bitcast.50, f32[640]{0:T(1024)S(1)} %get-tuple-element.5, f32[640,512]{1,0:T(8,128)} %collective-permute-done, f32[640,512]{1,0:T(8,128)S(1)} %bitcast.47, pred[]{:T(512)S(6)} %eq.5, f32[640,1280]{0,1:T(8,128)S(1)} %get-tuple-element.7, f32[1280]{0:T(1024)S(1)} %bitcast.60, ...), kind=kOutput, calls=%fused_computation.26 | convolution fusion | flops 2521661440 | bytes 8529921 | tf_op jit(solution)/shard_map/dot_general | solution.py:112
  200.6 6.3 %all-to-all-start.8 = ((f32[16,40,512]{2,1,0:T(8,128)}), f32[16,40,512]{2,1,0:T(8,128)}, u32[]{:S(2)}, u32[]{:S(2)}) async-start(f32[16,40,512]{2,1,0:T(8,128)} %bitcast.53), calls=%async_computation.8 | async-start | bytes 2621440 | tf_op jit(solution)/shard_map/all_to_all | solution.py:37
  206.9 6.6 %multiply_subtract_fusion = f32[1280,512]{1,0:T(8,128)S(1)} fusion(f32[1280]{0:T(1024)S(1)} %get-tuple-element.4, f32[640,512]{1,0:T(8,128)} %bitcast.46, f32[640,512]{1,0:T(8,128)} %collective-permute-done, pred[]{:T(512)S(6)} %eq.5, f32[640,512]{1,0:T(8,128)} %bitcast.49, f32[640,1280]{0,1:T(8,128)S(1)} %get-tuple-element.7, f32[1280]{0:T(1024)S(1)} %bitcast.61, ...), kind=kOutput, calls=%fused_computation.24 | convolution fusion | flops 2522316800 | bytes 9843201 | tf_op jit(solution)/shard_map/dot_general | solution.py:102
  213.5 1.5 copy-done.4
  215.1 1.9 collective-permute-start.1
  217.1 3.0 %collective-permute-done.1 = f32[640,512]{1,0:T(8,128)S(1)} collective-permute-done((f32[640,512]{1,0:T(8,128)S(1)}, f32[640,512]{1,0:T(8,128)S(1)}, u32[]{:S(2)}, u32[]{:S(2)}) %collective-permute-start.1) | collective-permute-done | bytes 1310752 | tf_op jit(solution)/shard_map/ppermute | solution.py:110
  220.1 2.7 bitcast_add_fusion
  222.8 15.7 %all-to-all-done.8 = f32[16,40,512]{2,1,0:T(8,128)} async-done(((f32[16,40,512]{2,1,0:T(8,128)}), f32[16,40,512]{2,1,0:T(8,128)}, u32[]{:S(2)}, u32[]{:S(2)}) %all-to-all-start.8) | async-done | bytes 1310752 | tf_op jit(solution)/shard_map/all_to_all | solution.py:37
  238.4 3.8 %all-to-all-start.9 = ((f32[16,40,512]{2,1,0:T(8,128)}), f32[16,40,512]{2,1,0:T(8,128)S(1)}, u32[]{:S(2)}, u32[]{:S(2)}) async-start(f32[16,40,512]{2,1,0:T(8,128)} %bitcast.21), calls=%async_computation.9 | async-start | bytes 2621440 | tf_op jit(solution)/shard_map/all_to_all | solution.py:37
  243.0 1.4 reduce_sum.177
  245.1 30.1 %all-to-all-done.9 = f32[16,40,512]{2,1,0:T(8,128)S(1)} async-done(((f32[16,40,512]{2,1,0:T(8,128)}), f32[16,40,512]{2,1,0:T(8,128)S(1)}, u32[]{:S(2)}, u32[]{:S(2)}) %all-to-all-start.9) | async-done | bytes 1310752 | tf_op jit(solution)/shard_map/all_to_all | solution.py:37
  (64 shorter events, 12.3 us)
Async XLA Ops:
  0.6 46.8 %copy-start.5 = (f32[40,512]{1,0:T(8,128)S(1)}, f32[40,512]{1,0:T(8,128)}, u32[]{:S(2)}) copy-start(f32[40,512]{1,0:T(8,128)} %param.2) | copy-start | bytes 245764
  47.5 42.5 %copy-start = (f32[16,40,512]{2,1,0:T(8,128)}, f32[16,40,512]{2,1,0:T(8,128)S(1)}, u32[]{:S(2)}) copy-start(f32[16,40,512]{2,1,0:T(8,128)S(1)} %all_to_all.50) | copy-start | bytes 3932164
  48.8 38.6 %all-to-all-start = ((f32[16,40,512]{2,1,0:T(8,128)}), f32[16,40,512]{2,1,0:T(8,128)S(1)}, u32[]{:S(2)}, u32[]{:S(2)}) async-start(f32[16,40,512]{2,1,0:T(8,128)} %broadcast_in_dim.16), calls=%async_computation | async-start | bytes 2621440 | tf_op jit(solution)/shard_map/all_to_all | solution.py:37
  57.3 30.4 %collective-permute-start = (f32[640,512]{1,0:T(8,128)S(1)}, f32[640,512]{1,0:T(8,128)}, u32[]{:S(2)}, u32[]{:S(2)}) collective-permute-start(f32[640,512]{1,0:T(8,128)S(1)} %bitcast.43), channel_id=1, source_target_pairs={{0,1},{1,0},{2,3},{3,2},{4,5},{5,4},{6,7},{7,6},{8,9},{9,8},{10,11... | collective-permute-start | bytes 3932168 | tf_op jit(solution)/shard_map/ppermute | solution.py:77
  87.4 2.5 copy-start.2
  192.7 1.3 copy-start.1
  192.7 1.7 copy-start.3
  200.6 37.8 %all-to-all-start.8 = ((f32[16,40,512]{2,1,0:T(8,128)}), f32[16,40,512]{2,1,0:T(8,128)}, u32[]{:S(2)}, u32[]{:S(2)}) async-start(f32[16,40,512]{2,1,0:T(8,128)} %bitcast.53), calls=%async_computation.8 | async-start | bytes 2621440 | tf_op jit(solution)/shard_map/all_to_all | solution.py:37
  213.5 1.5 copy-start.4
  215.1 4.9 %collective-permute-start.1 = (f32[640,512]{1,0:T(8,128)S(1)}, f32[640,512]{1,0:T(8,128)S(1)}, u32[]{:S(2)}, u32[]{:S(2)}) collective-permute-start(f32[640,512]{1,0:T(8,128)S(1)} %dynamic-slice_bitcast_fusion), channel_id=1, source_target_pairs={{0,1},{1,0},{2,3},{3,2},{4,5},{5,4},{6,7},{7,6},{8,9},{9,8},{10,11... | collective-permute-start | bytes 3932168 | tf_op jit(solution)/shard_map/ppermute | solution.py:110
  238.4 36.7 %all-to-all-start.9 = ((f32[16,40,512]{2,1,0:T(8,128)}), f32[16,40,512]{2,1,0:T(8,128)S(1)}, u32[]{:S(2)}, u32[]{:S(2)}) async-start(f32[16,40,512]{2,1,0:T(8,128)} %bitcast.21), calls=%async_computation.9 | async-start | bytes 2621440 | tf_op jit(solution)/shard_map/all_to_all | solution.py:37

commit v3 on v2

--- a/solution.py
+++ b/solution.py
@@ -3,6 +3,8 @@
 import jax
 import jax.numpy as jnp
 from jax import lax
+from jax.experimental import pallas as pl
+from jax.experimental.pallas import tpu as pltpu
 from jax.sharding import Mesh
 from jax.sharding import PartitionSpec as P
 
@@ -39,15 +41,123 @@
     )
 
 
-def gather(shard, axes, groups):
+PAIRS = 4
+NEIGHBOUR = [(i, i ^ 1) for i in range(8)]
+FIRST = (0, 3)
+SECOND = (1, 2)
+PASSES = ((0, 0), (0, 1), (1, 0), (1, 1), (0, 2), (2, 0))
+WHOLE = pl.BlockSpec(memory_space=pltpu.VMEM)
+VMEM_LIMIT = 16 * 1024 * 1024
+
+
+def ring(step):
+    return [(i, (i + step) % 8) for i in range(8)]
+
+
+def gather_blocks(shard, axes, groups):
     blocks = jnp.broadcast_to(shard[None], (len(groups[0]),) + shard.shape)
     return all_to_all(blocks, axes, groups).reshape(-1, shard.shape[1])
 
 
-def scatter(partial, axes, groups):
+def scatter_blocks(partial, axes, groups):
     count = len(groups[0])
     blocks = partial.reshape(count, partial.shape[0] // count, partial.shape[1])
     return jnp.sum(all_to_all(blocks, axes, groups), axis=0)
+
+
+def gather_ring(shard, axis, at, flip):
+    other = lax.ppermute(shard, axis, NEIGHBOUR)
+    even = at % 2 == 0
+    pair = jnp.concatenate([jnp.where(even, shard, other), jnp.where(even, other, shard)])
+    behind = lax.ppermute(pair, axis, ring(2))
+    ahead = lax.ppermute(pair, axis, ring(-2))
+    across = lax.ppermute(pair, axis, ring(4))
+    first = jnp.stack([pair, behind])
+    second = jnp.stack([ahead, across])
+    return first, lax.ppermute(first, "x", flip), second, lax.ppermute(second, "x", flip)
+
+
+def scatter_ring(partial, axis, at, flip, own):
+    moves = {2: ring(4), 1: ring(2), 3: ring(-2)}
+    here = at // 2
+
+    def piece(side, k):
+        return take(take(partial, side), (here + k) % PAIRS)
+
+    total = None
+    for group in ((2, 1), (3, 0)):
+        sent = jnp.stack([piece(1 - own, k) for k in group])
+        got = lax.ppermute(sent, "x", flip)
+        for i, k in enumerate(group):
+            part = piece(own, k) + got[i]
+            if k:
+                part = lax.ppermute(part, axis, moves[k])
+            total = part if total is None else total + part
+    total = total.reshape(2, -1, total.shape[-1])
+    return take(total, at % 2) + lax.ppermute(take(total, 1 - at % 2), axis, NEIGHBOUR)
+
+
+def parts_of(values):
+    high = values.astype(jnp.bfloat16)
+    rest = values - high.astype(jnp.float32)
+    mid = rest.astype(jnp.bfloat16)
+    low = (rest - mid.astype(jnp.float32)).astype(jnp.bfloat16)
+    return high, mid, low
+
+
+def tile_kernel(*refs):
+    row_refs, mine_ref, other_ref = refs[:4], refs[4], refs[5]
+    src_ref, tgt_ref, cost_ref, high_ref, mid_ref, low_ref = refs[6:]
+    x, y, c = (lax.axis_index(name) for name in ("x", "y", "c"))
+    a = x // 2
+    size = row_refs[0].shape[1]
+    for half, (mine, other) in enumerate((row_refs[:2], row_refs[2:])):
+        for i, step in enumerate((FIRST, SECOND)[half]):
+            pair = (y // 2 + step) % PAIRS
+            for place, ref in ((a, mine), (1 - a, other)):
+                at = pl.multiple_of((place * PAIRS + pair) * size, 8)
+                src_ref[pl.ds(at, size), :] = ref[i]
+    half = mine_ref.shape[0]
+    tgt_ref[pl.ds(pl.multiple_of(c * half, 8), half), :] = mine_ref[...]
+    tgt_ref[pl.ds(pl.multiple_of((1 - c) * half, 8), half), :] = other_ref[...]
+    cols, width = tgt_ref.shape
+    step = 256
+    left = src_ref[...]
+    left_sq = jnp.sum(left * left, axis=1, keepdims=True)
+    high_ref[...], mid_ref[...], low_ref[...] = parts_of(left)
+    left_parts = (high_ref, mid_ref, low_ref)
+    ones = jnp.ones((8, width), jnp.bfloat16)
+    dims = (((1,), (1,)), ((), ()))
+
+    def product(p, q):
+        return lax.dot_general(p, q, dims, preferred_element_type=jnp.float32)
+
+    @pl.loop(0, cols // step)
+    def _(j):
+        at = pl.multiple_of(j * step, step)
+        right = tgt_ref[pl.ds(at, step), :]
+        right_parts = parts_of(right)
+        cross = sum(product(left_parts[p][...], right_parts[q]) for p, q in PASSES)
+        right_sq = sum(product(ones, part) for part in parts_of(right * right))[:1]
+        cost_ref[:, pl.ds(at, step)] = (left_sq + right_sq - 2.0 * cross) / width
+
+
+def tile(row_pieces, mine, other):
+    size, width = row_pieces[0].shape[1:]
+    rows, cols = 2 * PAIRS * size, 2 * mine.shape[0]
+    part = pltpu.VMEM((rows, width), jnp.bfloat16)
+    return pl.pallas_call(
+        tile_kernel,
+        out_shape=(
+            jax.ShapeDtypeStruct((rows, width), jnp.float32),
+            jax.ShapeDtypeStruct((cols, width), jnp.float32),
+            jax.ShapeDtypeStruct((rows, cols), jnp.float32),
+        ),
+        in_specs=[WHOLE] * 6,
+        out_specs=(WHOLE,) * 3,
+        scratch_shapes=[part] * 3,
+        compiler_params=pltpu.CompilerParams(vmem_limit_bytes=VMEM_LIMIT),
+    )(*row_pieces, mine, other)
 
 
 def exchange(local, axes, groups, count):
@@ -72,21 +182,11 @@
     a = x // 2
     b = (x // 2) ^ (x % 2)
     total_points = rows * NZ * NX * NY * NC
-    mine = gather(tgt_emb, ("z", "x"), SIDE_GROUPS)
-    src_block = gather(src_emb, ("x", "y"), ROW_GROUPS)
+    mine = gather_blocks(tgt_emb, ("z", "x"), SIDE_GROUPS)
+    row_pieces = gather_ring(src_emb, "y", y, FLIP_A)
+    mine, row_pieces = lax.optimization_barrier((mine, row_pieces))
     other = lax.ppermute(mine, "c", SWAP)
-    tgt_block = jnp.where(
-        c == 0, jnp.concatenate([mine, other]), jnp.concatenate([other, mine])
-    )
-    left_sq = jnp.sum(src_block * src_block, axis=1)
-    right_sq = jnp.sum(tgt_block * tgt_block, axis=1)
-    cross = jnp.dot(
-        src_block,
-        tgt_block.T,
-        preferred_element_type=jnp.float32,
-        precision=lax.Precision.HIGHEST,
-    )
-    cost = (left_sq[:, None] + right_sq[None, :] - 2.0 * cross) / width
+    src_block, tgt_block, cost = tile(row_pieces, mine, other)
     tgt_pot = jnp.zeros((tgt_block.shape[0],), jnp.float32)
     log_total = math.log(total_points)
     for _ in range(ITERS):
@@ -108,11 +208,12 @@
     )
     tgt_part = (col_mass[:, None] * tgt_block - pulled).reshape(NC, -1, width)
     across = lax.ppermute(take(tgt_part, 1 - c), "c", SWAP)
-    tgt_sum = scatter(take(tgt_part, c) + across, ("z", "x"), SIDE_GROUPS)
+    tgt_sum = scatter_blocks(take(tgt_part, c) + across, ("z", "x"), SIDE_GROUPS)
     pushed = jnp.dot(
         weight, tgt_block, preferred_element_type=jnp.float32, precision=lax.Precision.HIGH
     )
-    src_sum = scatter(row_mass[:, None] * src_block - pushed, ("x", "y"), ROW_GROUPS)
+    src_part = (row_mass[:, None] * src_block - pushed).reshape(2, PAIRS, 2 * rows, width)
+    src_sum = scatter_ring(src_part, "y", y, FLIP_A, a)
     src_piece = take(src_pot.reshape(-1, rows), a * NY + y)
     tgt_piece = take(tgt_pot.reshape(-1, rows), (c * NZ + z) * 2 + b)
     return src_piece, tgt_piece, src_sum / total_points, tgt_sum / total_points

time: 279 us -> 264 us (0.946)
  blocking collectives: 131 us -> 79.7 us
  starting transfers between devices: 22.4 us -> 67.5 us
  waiting for transfers between devices: 77 us -> 59.2 us
  matrix products: 22.6 us -> 9.75 us
  local copies, waits for them, and re-layouts: 5.54 us -> 18 us
  Pallas kernels: 0 us -> 8.36 us
    all_to_all x3, waiting for transfers between devices: 74 us -> 12.4 us  [all_to_all(): lax.all_to_all(blocks, axes, split_axis=0, concat_axis=0, axis_index_grou...]
    all_to_all x7 -> x5, blocking collectives: 131 us -> 79.7 us  [all_to_all(): lax.all_to_all(blocks, axes, split_axis=0, concat_axis=0, axis_index_grou...]
    ppermute x0 -> x12, starting transfers between devices: none -> 44.1 us  [the longest x3 12.4 us: scatter_ring(): part = lax.ppermute(part, axis, moves[k])]
    ppermute x0 -> x12, waiting for transfers between devices: none -> 41.5 us  [the longest x2 12.8 us: scatter_ring(): got = lax.ppermute(sent, 'x', flip)]
    unnamed x12 -> x32, local copies, waits for them, and re-layouts: 2.16 us -> 13.1 us
    dot_general x1 -> x0, matrix products: 9.75 us -> none  [per_device(): jnp.dot(src_block, tgt_block.T, preferred_element_type=jnp.float32, preci...]
    pallas_call x0 -> x1, Pallas kernels: none -> 8.36 us  [tile(): pl.pallas_call(tile_kernel, out_shape=(jax.ShapeDtypeStruct((rows, width)...]
  transfers between devices with their start and end apart: 5 -> 17, of which waited for: 4 -> 12; matrix products, arithmetic and copies ran while one was open for 4% -> 3% of each run, Pallas kernels for 0% -> 0%
where the time goes in v3:
time: 264 us; the launch traced here: 260 us
  blocking collectives  79.7 us (30%)
  starting transfers between devices  67.5 us (26%)
  waiting for transfers between devices  59.2 us (22%)
  local copies, waits for them, and re-layouts  18 us (7%)
  other arithmetic  16.5 us (6%)
  matrix products  9.75 us (4%)
  Pallas kernels  8.36 us (3%)
    all_to_all x5, blocking collectives, all_to_all(): lax.all_to_all(blocks, axes, split_axis=0, concat_axis=0, axis_index_grou...  79.7 us
    all_to_all x3, starting transfers between devices, all_to_all(): lax.all_to_all(blocks, axes, split_axis=0, concat_axis=0, axis_index_grou...  19.6 us
    unnamed x32, local copies, waits for them, and re-layouts  13.1 us
    ppermute x2, waiting for transfers between devices, scatter_ring(): got = lax.ppermute(sent, 'x', flip)  12.8 us
    ppermute x3, starting transfers between devices, scatter_ring(): part = lax.ppermute(part, axis, moves[k])  12.4 us
    all_to_all x3, waiting for transfers between devices, all_to_all(): lax.all_to_all(blocks, axes, split_axis=0, concat_axis=0, axis_index_grou...  12.4 us
    ppermute x3, waiting for transfers between devices, scatter_ring(): part = lax.ppermute(part, axis, moves[k])  11.3 us
    pallas_call x1, Pallas kernels, tile(): pl.pallas_call(tile_kernel, out_shape=(jax.ShapeDtypeStruct((rows, width)...  8.36 us
  transfers between devices with their start and end apart: 17, of which 12 were waited for; matrix products, arithmetic and copies ran while one was open for 3% of the time, Pallas kernels for 0%

profile of v3, /device:TPU:56, one launch (start us, length us, event | category | flops | bytes accessed | tf_op | source)
XLA Modules:
  0.0 260.3 jit_solution(7907734831579534469)
XLA Ops:
  2.8 11.3 %all-to-all-start = ((f32[16,40,512]{2,1,0:T(8,128)}), f32[16,40,512]{2,1,0:T(8,128)S(1)}, u32[]{:S(2)}, u32[]{:S(2)}) async-start(f32[16,40,512]{2,1,0:T(8,128)} %broadcast_in_dim.14), calls=%async_computation | async-start | bytes 2621440 | tf_op jit(solution)/shard_map/all_to_all | solution.py:39
  23.2 6.8 %collective-permute-start.4 = (f32[80,512]{1,0:T(8,128)S(1)}, f32[80,512]{1,0:T(8,128)S(1)}, u32[]{:S(2)}, u32[]{:S(2)}) collective-permute-start(f32[80,512]{1,0:T(8,128)S(1)} %get-tuple-element.30), channel_id=1, source_target_pairs={{0,8},{2,10},{4,12},{6,14},{8,0},{10,2},{12,4},{14,6},{1,9},{3,11}... | collective-permute-start | bytes 491528 | tf_op jit(solution)/shard_map/ppermute | solution.py:74
  32.1 4.0 %collective-permute-start.2 = (f32[2,80,512]{2,1,0:T(8,128)S(1)}, f32[2,80,512]{2,1,0:T(8,128)S(1)}, u32[]{:S(2)}, u32[]{:S(2)}) collective-permute-start(f32[2,80,512]{2,1,0:T(8,128)S(1)} %pad_maximum_fusion.refs_0_), channel_id=1, source_target_pairs={{0,48},{16,32},{32,16},{48,0},{1,49},{17,33},{33,17},{49,1},{2,50}... | collective-permute-start | bytes 983048 | tf_op jit(solution)/shard_map/ppermute | solution.py:77
  40.4 4.0 %collective-permute-start.5 = (f32[2,80,512]{2,1,0:T(8,128)S(1)}, f32[2,80,512]{2,1,0:T(8,128)S(1)}, u32[]{:S(2)}, u32[]{:S(2)}) collective-permute-start(f32[2,80,512]{2,1,0:T(8,128)S(1)} %pad_maximum_fusion.1.refs_2_), channel_id=1, source_target_pairs={{0,48},{16,32},{32,16},{48,0},{1,49},{17,33},{33,17},{49,1},{2,50}... | collective-permute-start | bytes 983048 | tf_op jit(solution)/shard_map/ppermute | solution.py:77
  45.9 6.2 %collective-permute-done.5.refs_3_ = f32[2,80,512]{2,1,0:T(8,128)S(1)} collective-permute-done((f32[2,80,512]{2,1,0:T(8,128)S(1)}, f32[2,80,512]{2,1,0:T(8,128)S(1)}, u32[]{:S(2)}, u32[]{:S(2)}) %collective-permute-start.5) | collective-permute-done | bytes 327712 | tf_op jit(solution)/shard_map/ppermute | solution.py:77
  62.9 8.4 %shard_map.57 = (f32[640,512]{1,0:T(8,128)S(1)}, f32[1280,512]{1,0:T(8,128)S(1)}, f32[640,1280]{1,0:T(8,128)S(1)}) custom-call(f32[2,80,512]{2,1,0:T(8,128)S(1)} %copy-done.6, f32[2,80,512]{2,1,0:T(8,128)S(1)} %copy-done.10, f32[2,80,512]{2,1,0:T(8,128)S(1)} %copy-done.8, f32[2,80,512]{2,1,0:T(8,128)S(1)} %copy-done.12, f32[640,512]{1,0:T(8,128)S(1)} %bitcast.83, ...), custom_call_target="tpu_custom_call" | custom-call | tf_op jit(solution)/shard_map/pallas_call | solution.py:149
  74.0 20.2 %all_to_all.40 = f32[16,5,128]{2,1,0:T(8,128)S(1)} all-to-all(f32[16,5,128]{2,1,0:T(8,128)S(1)} %broadcast_in_dim.15), channel_id=1, replica_groups={{0,2,4,6,8,10,12,14,48,50,52,54,56,58,60,62},{16,18,20,22,24,26,28,30,3..., dimensions={0} | all-to-all | bytes 81920 | tf_op jit(solution)/shard_map/all_to_all | solution.py:39
  95.5 19.5 %all_to_all.41 = f32[32,10,128]{2,1,0:T(8,128)S(1)} all-to-all(f32[32,10,128]{2,1,0:T(8,128)S(1)} %broadcast_in_dim.16), channel_id=1, replica_groups={{0,1,16,17,64,65,80,81,128,129,144,145,192,193,208,209,256,257,272,273,..., dimensions={0} | all-to-all | bytes 327680 | tf_op jit(solution)/shard_map/all_to_all | solution.py:39
  116.3 12.5 %all_to_all.42 = f32[16,5,128]{2,1,0:T(8,128)S(1)} all-to-all(f32[16,5,128]{2,1,0:T(8,128)S(1)} %broadcast_in_dim.17), channel_id=1, replica_groups={{0,2,4,6,8,10,12,14,48,50,52,54,56,58,60,62},{16,18,20,22,24,26,28,30,3..., dimensions={0} | all-to-all | bytes 81920 | tf_op jit(solution)/shard_map/all_to_all | solution.py:39
  130.1 15.2 %all_to_all.43 = f32[32,10,128]{2,1,0:T(8,128)S(1)} all-to-all(f32[32,10,128]{2,1,0:T(8,128)S(1)} %broadcast_in_dim.18), channel_id=1, replica_groups={{0,1,16,17,64,65,80,81,128,129,144,145,192,193,208,209,256,257,272,273,..., dimensions={0} | all-to-all | bytes 327680 | tf_op jit(solution)/shard_map/all_to_all | solution.py:39
  146.6 12.2 %all_to_all.44 = f32[16,5,128]{2,1,0:T(8,128)S(1)} all-to-all(f32[16,5,128]{2,1,0:T(8,128)S(1)} %broadcast_in_dim.19), channel_id=1, replica_groups={{0,2,4,6,8,10,12,14,48,50,52,54,56,58,60,62},{16,18,20,22,24,26,28,30,3..., dimensions={0} | all-to-all | bytes 81920 | tf_op jit(solution)/shard_map/all_to_all | solution.py:39
  160.8 3.9 %all-to-all-start.6 = ((f32[32,10,128]{2,1,0:T(8,128)}), f32[32,10,128]{2,1,0:T(8,128)S(1)}, u32[]{:S(2)}, u32[]{:S(2)}) async-start(f32[32,10,128]{2,1,0:T(8,128)} %broadcast_in_dim.20), calls=%async_computation.6 | async-start | bytes 524288 | tf_op jit(solution)/shard_map/all_to_all | solution.py:39
  164.7 12.4 %all-to-all-done.6 = f32[32,10,128]{2,1,0:T(8,128)S(1)} async-done(((f32[32,10,128]{2,1,0:T(8,128)}), f32[32,10,128]{2,1,0:T(8,128)S(1)}, u32[]{:S(2)}, u32[]{:S(2)}) %all-to-all-start.6) | async-done | bytes 163872 | tf_op jit(solution)/shard_map/all_to_all | solution.py:39
  178.8 4.8 %multiply_subtract_fusion = f32[1280,512]{1,0:T(8,128)S(1)} fusion(f32[1280,512]{1,0:T(8,128)S(1)} %copy-done.3, f32[1280]{0:T(1024)S(1)} %get-tuple-element.20, f32[640,512]{1,0:T(8,128)} %copy-done.4, f32[640,1280]{1,0:T(8,128)S(1)} %get-tuple-element.17, f32[1280]{0:T(1024)S(1)} %bitcast.101, f32[640]{0:T(1024)S(1)} %bitcast.98), kind=kOutput, calls=%fused_computation.19 | convolution fusion | flops 2520350720 | bytes 9843200 | tf_op jit(solution)/shard_map/dot_general | solution.py:202
  194.6 4.4 %all-to-all-start.7 = ((f32[16,40,512]{2,1,0:T(8,128)}), f32[16,40,512]{2,1,0:T(8,128)}, u32[]{:S(2)}, u32[]{:S(2)}) async-start(f32[16,40,512]{2,1,0:T(8,128)} %bitcast.86), calls=%async_computation.7 | async-start | bytes 2621440 | tf_op jit(solution)/shard_map/all_to_all | solution.py:39
  199.2 4.9 %multiply_subtract_fusion.1 = f32[640,512]{1,0:T(8,128)S(1)} fusion(f32[640,512]{1,0:T(8,128)} %copy-done.4, f32[640]{0:T(1024)S(1)} %get-tuple-element.21, f32[1280,512]{1,0:T(8,128)} %copy-done.2, f32[640,1280]{1,0:T(8,128)S(1)} %get-tuple-element.17, f32[1280]{0:T(1024)S(1)} %bitcast.102, f32[640]{0:T(1024)S(1)} %bitcast.99), kind=kOutput, calls=%fused_computation.22 | convolution fusion | flops 2519695360 | bytes 8529920 | tf_op jit(solution)/shard_map/dot_general | solution.py:212
  207.7 4.6 %collective-permute-start.7 = (f32[2,80,512]{2,1,0:T(8,128)S(1)}, f32[2,80,512]{2,1,0:T(8,128)S(1)}, u32[]{:S(2)}, u32[]{:S(2)}) collective-permute-start(f32[2,80,512]{2,1,0:T(8,128)S(1)} %pad_maximum_fusion.2), channel_id=1, source_target_pairs={{0,48},{16,32},{32,16},{48,0},{1,49},{17,33},{33,17},{49,1},{2,50}... | collective-permute-start | bytes 983048 | tf_op jit(solution)/shard_map/ppermute | solution.py:90
  212.4 6.5 %collective-permute-done.10 = f32[2,80,512]{2,1,0:T(8,128)S(1)} collective-permute-done((f32[2,80,512]{2,1,0:T(8,128)S(1)}, f32[2,80,512]{2,1,0:T(8,128)S(1)}, u32[]{:S(2)}, u32[]{:S(2)}) %collective-permute-start.10) | collective-permute-done | bytes 327712 | tf_op jit(solution)/shard_map/ppermute | solution.py:90
  218.9 6.2 %collective-permute-done.7 = f32[2,80,512]{2,1,0:T(8,128)S(1)} collective-permute-done((f32[2,80,512]{2,1,0:T(8,128)S(1)}, f32[2,80,512]{2,1,0:T(8,128)S(1)}, u32[]{:S(2)}, u32[]{:S(2)}) %collective-permute-start.7) | collective-permute-done | bytes 327712 | tf_op jit(solution)/shard_map/ppermute | solution.py:90
  228.7 6.2 %collective-permute-start.8 = (f32[80,512]{1,0:T(8,128)S(1)}, f32[80,512]{1,0:T(8,128)S(1)}, u32[]{:S(2)}, u32[]{:S(2)}) collective-permute-start(f32[80,512]{1,0:T(8,128)S(1)} %get-tuple-element.23), channel_id=1, source_target_pairs={{0,8},{2,10},{4,12},{6,14},{8,0},{10,2},{12,4},{14,6},{1,9},{3,11}... | collective-permute-start | bytes 491528 | tf_op jit(solution)/shard_map/ppermute | solution.py:94
  235.0 3.7 %collective-permute-start.9 = (f32[80,512]{1,0:T(8,128)S(1)}, f32[80,512]{1,0:T(8,128)S(1)}, u32[]{:S(2)}, u32[]{:S(2)}) collective-permute-start(f32[80,512]{1,0:T(8,128)S(1)} %get-tuple-element.22), channel_id=1, source_target_pairs={{0,4},{2,6},{4,8},{6,10},{8,12},{10,14},{12,0},{14,2},{1,5},{3,7},... | collective-permute-start | bytes 491528 | tf_op jit(solution)/shard_map/ppermute | solution.py:94
  238.9 5.4 %collective-permute-done.8 = f32[80,512]{1,0:T(8,128)S(1)} collective-permute-done((f32[80,512]{1,0:T(8,128)S(1)}, f32[80,512]{1,0:T(8,128)S(1)}, u32[]{:S(2)}, u32[]{:S(2)}) %collective-permute-start.8) | collective-permute-done | bytes 163872 | tf_op jit(solution)/shard_map/ppermute | solution.py:94
  244.3 5.9 %collective-permute-done.9 = f32[80,512]{1,0:T(8,128)S(1)} collective-permute-done((f32[80,512]{1,0:T(8,128)S(1)}, f32[80,512]{1,0:T(8,128)S(1)}, u32[]{:S(2)}, u32[]{:S(2)}) %collective-permute-start.9) | collective-permute-done | bytes 163872 | tf_op jit(solution)/shard_map/ppermute | solution.py:94
  253.7 3.9 %collective-permute-done.12 = f32[40,512]{1,0:T(8,128)S(1)} collective-permute-done((f32[40,512]{1,0:T(8,128)S(1)}, f32[40,512]{1,0:T(8,128)S(1)}, u32[]{:S(2)}, u32[]{:S(2)}) %collective-permute-start.12) | collective-permute-done | bytes 81952 | tf_op jit(solution)/shard_map/ppermute | solution.py:97
  (112 shorter events, 65.6 us)
Async XLA Ops:
  0.6 13.5 %copy-start.15 = (f32[40,512]{1,0:T(8,128)S(1)}, f32[40,512]{1,0:T(8,128)}, u32[]{:S(2)}) copy-start(f32[40,512]{1,0:T(8,128)} %param.2) | copy-start | bytes 245764
  2.8 50.0 %all-to-all-start = ((f32[16,40,512]{2,1,0:T(8,128)}), f32[16,40,512]{2,1,0:T(8,128)S(1)}, u32[]{:S(2)}, u32[]{:S(2)}) async-start(f32[16,40,512]{2,1,0:T(8,128)} %broadcast_in_dim.14), calls=%async_computation | async-start | bytes 2621440 | tf_op jit(solution)/shard_map/all_to_all | solution.py:39
  14.1 6.3 %collective-permute-start = (f32[40,512]{1,0:T(8,128)S(1)}, f32[40,512]{1,0:T(8,128)S(1)}, u32[]{:S(2)}, u32[]{:S(2)}) collective-permute-start(f32[40,512]{1,0:T(8,128)S(1)} %copy-done.15), channel_id=1, source_target_pairs={{0,2},{2,0},{4,6},{6,4},{8,10},{10,8},{12,14},{14,12},{1,3},{3,1},... | collective-permute-start | bytes 245768 | tf_op jit(solution)/shard_map/ppermute | solution.py:69
  20.5 11.5 %collective-permute-start.1 = (f32[80,512]{1,0:T(8,128)S(1)}, f32[80,512]{1,0:T(8,128)S(1)}, u32[]{:S(2)}, u32[]{:S(2)}) collective-permute-start(f32[80,512]{1,0:T(8,128)S(1)} %get-tuple-element.30), channel_id=1, source_target_pairs={{0,4},{2,6},{4,8},{6,10},{8,12},{10,14},{12,0},{14,2},{1,5},{3,7},... | collective-permute-start | bytes 491528 | tf_op jit(solution)/shard_map/ppermute | solution.py:72
  23.2 15.3 %collective-permute-start.4 = (f32[80,512]{1,0:T(8,128)S(1)}, f32[80,512]{1,0:T(8,128)S(1)}, u32[]{:S(2)}, u32[]{:S(2)}) collective-permute-start(f32[80,512]{1,0:T(8,128)S(1)} %get-tuple-element.30), channel_id=1, source_target_pairs={{0,8},{2,10},{4,12},{6,14},{8,0},{10,2},{12,4},{14,6},{1,9},{3,11}... | collective-permute-start | bytes 491528 | tf_op jit(solution)/shard_map/ppermute | solution.py:74
  30.1 10.3 %collective-permute-start.3 = (f32[80,512]{1,0:T(8,128)S(1)}, f32[80,512]{1,0:T(8,128)S(1)}, u32[]{:S(2)}, u32[]{:S(2)}) collective-permute-start(f32[80,512]{1,0:T(8,128)S(1)} %get-tuple-element.30), channel_id=1, source_target_pairs={{0,12},{2,14},{4,0},{6,2},{8,4},{10,6},{12,8},{14,10},{1,13},{3,15... | collective-permute-start | bytes 491528 | tf_op jit(solution)/shard_map/ppermute | solution.py:73
  32.1 22.7 %copy-start.5 = (f32[2,80,512]{2,1,0:T(8,128)}, f32[2,80,512]{2,1,0:T(8,128)S(1)}, u32[]{:S(2)}) copy-start(f32[2,80,512]{2,1,0:T(8,128)S(1)} %pad_maximum_fusion.refs_0_) | copy-start | bytes 983044
  32.1 13.1 %collective-permute-start.2 = (f32[2,80,512]{2,1,0:T(8,128)S(1)}, f32[2,80,512]{2,1,0:T(8,128)S(1)}, u32[]{:S(2)}, u32[]{:S(2)}) collective-permute-start(f32[2,80,512]{2,1,0:T(8,128)S(1)} %pad_maximum_fusion.refs_0_), channel_id=1, source_target_pairs={{0,48},{16,32},{32,16},{48,0},{1,49},{17,33},{33,17},{49,1},{2,50}... | collective-permute-start | bytes 983048 | tf_op jit(solution)/shard_map/ppermute | solution.py:77
  40.4 11.7 %collective-permute-start.5 = (f32[2,80,512]{2,1,0:T(8,128)S(1)}, f32[2,80,512]{2,1,0:T(8,128)S(1)}, u32[]{:S(2)}, u32[]{:S(2)}) collective-permute-start(f32[2,80,512]{2,1,0:T(8,128)S(1)} %pad_maximum_fusion.1.refs_2_), channel_id=1, source_target_pairs={{0,48},{16,32},{32,16},{48,0},{1,49},{17,33},{33,17},{49,1},{2,50}... | collective-permute-start | bytes 983048 | tf_op jit(solution)/shard_map/ppermute | solution.py:77
  52.8 4.9 %collective-permute-start.6 = (f32[640,512]{1,0:T(8,128)S(1)}, f32[640,512]{1,0:T(8,128)S(1)}, u32[]{:S(2)}, u32[]{:S(2)}) collective-permute-start(f32[640,512]{1,0:T(8,128)S(1)} %bitcast.82), channel_id=1, source_target_pairs={{0,1},{1,0},{2,3},{3,2},{4,5},{5,4},{6,7},{7,6},{8,9},{9,8},{10,11... | collective-permute-start | bytes 3932168 | tf_op jit(solution)/shard_map/ppermute | solution.py:188
  57.7 1.3 copy-start.1
  71.3 1.5 copy-start.2
  72.8 1.2 copy-start.4
  160.8 16.2 %all-to-all-start.6 = ((f32[32,10,128]{2,1,0:T(8,128)}), f32[32,10,128]{2,1,0:T(8,128)S(1)}, u32[]{:S(2)}, u32[]{:S(2)}) async-start(f32[32,10,128]{2,1,0:T(8,128)} %broadcast_in_dim.20), calls=%async_computation.6 | async-start | bytes 524288 | tf_op jit(solution)/shard_map/all_to_all | solution.py:39
  177.1 1.7 copy-start.3
  183.7 1.5 copy-start.13
  186.3 5.3 %collective-permute-start.13 = (f32[640,512]{1,0:T(8,128)}, f32[640,512]{1,0:T(8,128)}, u32[]{:S(2)}, u32[]{:S(2)}) collective-permute-start(f32[640,512]{1,0:T(8,128)} %dynamic-slice_bitcast_fusion), channel_id=1, source_target_pairs={{0,1},{1,0},{2,3},{3,2},{4,5},{5,4},{6,7},{7,6},{8,9},{9,8},{10,11... | collective-permute-start | bytes 3932168 | tf_op jit(solution)/shard_map/ppermute | solution.py:210
  194.6 63.6 %all-to-all-start.7 = ((f32[16,40,512]{2,1,0:T(8,128)}), f32[16,40,512]{2,1,0:T(8,128)}, u32[]{:S(2)}, u32[]{:S(2)}) async-start(f32[16,40,512]{2,1,0:T(8,128)} %bitcast.86), calls=%async_computation.7 | async-start | bytes 2621440 | tf_op jit(solution)/shard_map/all_to_all | solution.py:39
  205.2 13.7 %collective-permute-start.10 = (f32[2,80,512]{2,1,0:T(8,128)S(1)}, f32[2,80,512]{2,1,0:T(8,128)S(1)}, u32[]{:S(2)}, u32[]{:S(2)}) collective-permute-start(f32[2,80,512]{2,1,0:T(8,128)S(1)} %pad_maximum_fusion.3), channel_id=1, source_target_pairs={{0,48},{16,32},{32,16},{48,0},{1,49},{17,33},{33,17},{49,1},{2,50}... | collective-permute-start | bytes 983048 | tf_op jit(solution)/shard_map/ppermute | solution.py:90
  207.7 17.4 %collective-permute-start.7 = (f32[2,80,512]{2,1,0:T(8,128)S(1)}, f32[2,80,512]{2,1,0:T(8,128)S(1)}, u32[]{:S(2)}, u32[]{:S(2)}) collective-permute-start(f32[2,80,512]{2,1,0:T(8,128)S(1)} %pad_maximum_fusion.2), channel_id=1, source_target_pairs={{0,48},{16,32},{32,16},{48,0},{1,49},{17,33},{33,17},{49,1},{2,50}... | collective-permute-start | bytes 983048 | tf_op jit(solution)/shard_map/ppermute | solution.py:90
  226.3 12.6 %collective-permute-start.11 = (f32[80,512]{1,0:T(8,128)S(1)}, f32[80,512]{1,0:T(8,128)S(1)}, u32[]{:S(2)}, u32[]{:S(2)}) collective-permute-start(f32[80,512]{1,0:T(8,128)S(1)} %get-tuple-element.24), channel_id=1, source_target_pairs={{0,12},{2,14},{4,0},{6,2},{8,4},{10,6},{12,8},{14,10},{1,13},{3,15... | collective-permute-start | bytes 491528 | tf_op jit(solution)/shard_map/ppermute | solution.py:94
  228.7 15.6 %collective-permute-start.8 = (f32[80,512]{1,0:T(8,128)S(1)}, f32[80,512]{1,0:T(8,128)S(1)}, u32[]{:S(2)}, u32[]{:S(2)}) collective-permute-start(f32[80,512]{1,0:T(8,128)S(1)} %get-tuple-element.23), channel_id=1, source_target_pairs={{0,8},{2,10},{4,12},{6,14},{8,0},{10,2},{12,4},{14,6},{1,9},{3,11}... | collective-permute-start | bytes 491528 | tf_op jit(solution)/shard_map/ppermute | solution.py:94
  235.0 15.3 %collective-permute-start.9 = (f32[80,512]{1,0:T(8,128)S(1)}, f32[80,512]{1,0:T(8,128)S(1)}, u32[]{:S(2)}, u32[]{:S(2)}) collective-permute-start(f32[80,512]{1,0:T(8,128)S(1)} %get-tuple-element.22), channel_id=1, source_target_pairs={{0,4},{2,6},{4,8},{6,10},{8,12},{10,14},{12,0},{14,2},{1,5},{3,7},... | collective-permute-start | bytes 491528 | tf_op jit(solution)/shard_map/ppermute | solution.py:94
  251.2 6.3 %collective-permute-start.12 = (f32[40,512]{1,0:T(8,128)S(1)}, f32[40,512]{1,0:T(8,128)S(1)}, u32[]{:S(2)}, u32[]{:S(2)}) collective-permute-start(f32[40,512]{1,0:T(8,128)S(1)} %dynamic-slice_bitcast_fusion.5), channel_id=1, source_target_pairs={{0,2},{2,0},{4,6},{6,4},{8,10},{10,8},{12,14},{14,12},{1,3},{3,1},... | collective-permute-start | bytes 245768 | tf_op jit(solution)/shard_map/ppermute | solution.py:97
  (9 other events, 8.2 us)

commit v4 on v3

v4 whole, which is shorter than its diff:
```python
import math

import jax
import jax.numpy as jnp
from jax import lax
from jax.experimental import pallas as pl
from jax.experimental.pallas import tpu as pltpu
from jax.sharding import Mesh
from jax.sharding import PartitionSpec as P

ITERS = 3
ENTROPY_REG = 0.05
NZ, NX, NY, NC = 8, 4, 8, 2
LANES = 128

A_OF_X = (0, 0, 1, 1)
B_OF_X = (0, 1, 1, 0)
FLIP_A = [(x, NX - 1 - x) for x in range(NX)]
FLIP_B = [(x, x ^ 1) for x in range(NX)]
SWAP = [(0, 1), (1, 0)]
X_OF_AB = {(A_OF_X[x], B_OF_X[x]): x for x in range(NX)}

ROW_GROUPS = [[X_OF_AB[a, b] * NY + y for a in range(2) for y in range(NY)] for b in range(2)]
COL_GROUPS = [
    [(z * NX + X_OF_AB[a, b]) * NC + c for z in range(NZ) for b in range(2) for c in range(NC)]
    for a in range(2)
]

SIDE_GROUPS = [
    [z * NX + X_OF_AB[a, b] for z in range(NZ) for b in range(2)] for a in range(2)
]


def take(buffer, index):
    return lax.dynamic_index_in_dim(buffer, index, 0, keepdims=False)


def all_to_all(blocks, axes, groups):
    return lax.all_to_all(
        blocks, axes, split_axis=0, concat_axis=0, axis_index_groups=groups, tiled=True
    )


STEPS = (4, 3, 5, 2, 6, 1, 7)
PASSES = ((0, 0), (0, 1), (1, 0), (1, 1), (0, 2), (2, 0))
IN_HBM = pl.BlockSpec(memory_space=pltpu.HBM)
WHOLE = pl.BlockSpec(memory_space=pltpu.VMEM)
VMEM_LIMIT = 24 * 1024 * 1024


def ring(step):
    return [(i, (i + step) % 8) for i in range(8)]


def gather_blocks(shard, axes, groups):
    blocks = jnp.broadcast_to(shard[None], (len(groups[0]),) + shard.shape)
    return all_to_all(blocks, axes, groups).reshape(-1, shard.shape[1])


def scatter_blocks(partial, axes, groups):
    count = len(groups[0])
    blocks = partial.reshape(count, partial.shape[0] // count, partial.shape[1])
    return jnp.sum(all_to_all(blocks, axes, groups), axis=0)


def gather_ring(shard, a):
    other = lax.ppermute(shard, "x", FLIP_A)
    pair = jnp.stack([jnp.where(a == 0, shard, other), jnp.where(a == 0, other, shard)])
    return (pair,) + tuple(lax.ppermute(pair, "y", ring(k)) for k in STEPS)


def scatter_ring(partial, y, a):
    total = take(partial, y)
    for k in STEPS:
        total = total + lax.ppermute(take(partial, (y + k) % NY), "y", ring(k))
    return take(total, a) + lax.ppermute(take(total, 1 - a), "x", FLIP_A)


def parts_of(values):
    high = values.astype(jnp.bfloat16)
    rest = values - high.astype(jnp.float32)
    mid = rest.astype(jnp.bfloat16)
    low = (rest - mid.astype(jnp.float32)).astype(jnp.bfloat16)
    return high, mid, low


def product(p, q, contract):
    return lax.dot_general(
        p, q, ((contract[:1], contract[1:]), ((), ())), preferred_element_type=jnp.float32
    )


def three_products(p, q, contract):
    return (
        product(p[0], q[0], contract)
        + product(p[0], q[1], contract)
        + product(p[1], q[0], contract)
    )


def tile_kernel(*refs):
    row_refs, mine_ref, other_ref = refs[:8], refs[8], refs[9]
    src_out, tgt_out, cost_ref, src_ref, tgt_ref = refs[10:15]
    high_ref, mid_ref, low_ref, row_sem, col_sem, out_sem = refs[15:]
    y, c = lax.axis_index("y"), lax.axis_index("c")
    size = row_refs[0].shape[0]
    row_copies = []
    for i, step in enumerate((0,) + STEPS):
        at = pl.multiple_of((y + NY - step) % NY * size, 8)
        row_copies.append(
            pltpu.make_async_copy(row_refs[i], src_ref.at[pl.ds(at, size)], row_sem.at[i])
        )
    half = mine_ref.shape[0]
    col_copies = []
    for i, (place, ref) in enumerate(((c, mine_ref), (1 - c, other_ref))):
        at = pl.multiple_of(place * half, 8)
        col_copies.append(
            pltpu.make_async_copy(ref, tgt_ref.at[pl.ds(at, half)], col_sem.at[i])
        )
    for copy in row_copies + col_copies:
        copy.start()
    for copy in row_copies:
        copy.wait()
    cols, width = tgt_ref.shape
    step = 256
    left = src_ref[...]
    left_sq = jnp.sum(left * left, axis=1, keepdims=True)
    high_ref[...], mid_ref[...], low_ref[...] = parts_of(left)
    left_parts = (high_ref, mid_ref, low_ref)
    ones = jnp.ones((8, width), jnp.bfloat16)
    for copy in col_copies:
        copy.wait()
    out_copies = (
        pltpu.make_async_copy(src_ref, src_out, out_sem.at[0]),
        pltpu.make_async_copy(tgt_ref, tgt_out, out_sem.at[1]),
    )
    for copy in out_copies:
        copy.start()

    @pl.loop(0, cols // step)
    def _(j):
        at = pl.multiple_of(j * step, step)
        right = tgt_ref[pl.ds(at, step), :]
        right_parts = parts_of(right)
        cross = sum(product(left_parts[p][...], right_parts[q], (1, 1)) for p, q in PASSES)
        right_sq = sum(product(ones, part, (1, 1)) for part in parts_of(right * right))[:1]
        cost_ref[:, pl.ds(at, step)] = (left_sq + right_sq - 2.0 * cross) / width

    for copy in out_copies:
        copy.wait()


def tile(row_pieces, mine, other):
    size, width = row_pieces[0].shape
    rows, cols = NY * size, 2 * mine.shape[0]
    part = pltpu.VMEM((rows, width), jnp.bfloat16)
    return pl.pallas_call(
        tile_kernel,
        out_shape=(
            jax.ShapeDtypeStruct((rows, width), jnp.float32),
            jax.ShapeDtypeStruct((cols, width), jnp.float32),
            jax.ShapeDtypeStruct((rows, cols), jnp.float32),
        ),
        in_specs=[IN_HBM] * 10,
        out_specs=(IN_HBM, IN_HBM, WHOLE),
        scratch_shapes=[
            pltpu.VMEM((rows, width), jnp.float32),
            pltpu.VMEM((cols, width), jnp.float32),
            part,
            part,
            part,
            pltpu.SemaphoreType.DMA((NY,)),
            pltpu.SemaphoreType.DMA((2,)),
            pltpu.SemaphoreType.DMA((2,)),
        ],
        compiler_params=pltpu.CompilerParams(vmem_limit_bytes=VMEM_LIMIT),
    )(*row_pieces, mine, other)


def half_of(high_ref, mid_ref, place):
    size = high_ref.shape[1] // 2
    at = pl.ds(pl.multiple_of(place * size, LANES), size)
    return high_ref[:, at], mid_ref[:, at]


def pull(weight_parts, src_ref, tgt):
    src_parts = parts_of(src_ref[...])
    pulled = three_products(weight_parts, src_parts, (0, 0))
    ones = jnp.ones((src_ref.shape[0], LANES), jnp.bfloat16)
    mass = sum(product(part, ones, (0, 0)) for part in weight_parts)[:, :1]
    return mass * tgt - pulled


def send_kernel(
    src_pot_ref, tgt_pot_ref, cost_ref, src_hbm, tgt_hbm, sent_ref, high_ref, mid_ref,
    src_ref, tgt_ref, sem,
):
    rows, cols = cost_ref.shape
    half = cols // 2
    place = 1 - lax.axis_index("c")
    there = tgt_hbm.at[pl.ds(pl.multiple_of(place * half, 8), half)]
    copies = (
        pltpu.make_async_copy(src_hbm, src_ref, sem.at[0]),
        pltpu.make_async_copy(there, tgt_ref, sem.at[1]),
    )
    for copy in copies:
        copy.start()
    lane = lax.broadcasted_iota(jnp.int32, (LANES, LANES), 1)
    sub = lax.broadcasted_iota(jnp.int32, (LANES, LANES), 0)
    for i in range(rows // LANES):
        row = jnp.broadcast_to(src_pot_ref[i : i + 1, :], (LANES, LANES))
        column = jnp.sum(jnp.where(lane == sub, row, 0.0), axis=1, keepdims=True)
        at = slice(i * LANES, (i + 1) * LANES)
        for j in range(cols // LANES):
            to = slice(j * LANES, (j + 1) * LANES)
            total = column + tgt_pot_ref[j : j + 1, :] - cost_ref[at, to]
            weight = jnp.exp(total / ENTROPY_REG)
            high = weight.astype(jnp.bfloat16)
            high_ref[at, to] = high
            mid_ref[at, to] = (weight - high.astype(jnp.float32)).astype(jnp.bfloat16)
    for copy in copies:
        copy.wait()
    sent_ref[...] = pull(half_of(high_ref, mid_ref, place), src_ref, tgt_ref[...])


def push_kernel(high_ref, mid_ref, src_ref, tgt_ref, out_ref):
    weight_parts = high_ref[...], mid_ref[...]
    pushed = three_products(weight_parts, parts_of(tgt_ref[...]), (1, 0))
    ones = jnp.ones((tgt_ref.shape[0], LANES), jnp.bfloat16)
    mass = sum(product(part, ones, (1, 0)) for part in weight_parts)[:, :1]
    out_ref[...] = mass * src_ref[...] - pushed


def keep_kernel(high_ref, mid_ref, src_ref, tgt_ref, came_ref, out_ref):
    place = lax.axis_index("c")
    half = came_ref.shape[0]
    tgt = tgt_ref[pl.ds(pl.multiple_of(place * half, 8), half), :]
    out_ref[...] = pull(half_of(high_ref, mid_ref, place), src_ref, tgt) + came_ref[...]


def on_tile(kernel, out_shape, *args):
    return pl.pallas_call(
        kernel,
        out_shape=out_shape,
        in_specs=[WHOLE] * len(args),
        out_specs=jax.tree.map(lambda _: WHOLE, out_shape),
        compiler_params=pltpu.CompilerParams(vmem_limit_bytes=VMEM_LIMIT),
    )(*args)


def exchange(local, axes, groups, count):
    size = local.shape[0]
    flat = local.reshape(1, size // LANES, LANES)
    sent = jnp.broadcast_to(flat, (count, size // LANES, LANES))
    got = all_to_all(sent, axes, groups)
    peak = jnp.max(got, axis=0)
    total = jnp.sum(jnp.exp(got - peak[None]), axis=0)
    return peak + jnp.log(total)


def local_lse(scores, axis):
    peak = jnp.max(scores, axis=axis, keepdims=True)
    total = jnp.sum(jnp.exp(scores - peak), axis=axis)
    return jnp.squeeze(peak, axis) + jnp.log(total)


def per_device(src_emb, tgt_emb):
    rows, width = src_emb.shape
    z, x, y, c = (lax.axis_index(name) for name in ("z", "x", "y", "c"))
    a = x // 2
    b = (x // 2) ^ (x % 2)
    total_points = rows * NZ * NX * NY * NC
    mine = gather_blocks(tgt_emb, ("z", "x"), SIDE_GROUPS)
    row_pieces = tuple(piece.reshape(-1, width) for piece in gather_ring(src_emb, a))
    mine, row_pieces = lax.optimization_barrier((mine, row_pieces))
    other = lax.ppermute(mine, "c", SWAP)
    src_block, tgt_block, cost = tile(row_pieces, mine, other)
    tile_rows, tile_cols = cost.shape
    tgt_pot = jnp.zeros((tile_cols,), jnp.float32)
    log_total = math.log(total_points)
    for _ in range(ITERS):
        lse = local_lse((tgt_pot.reshape(1, tile_cols) - cost) / ENTROPY_REG, 1)
        lse = exchange(lse, ("x", "y"), ROW_GROUPS, 2 * NY)
        src_pot = -ENTROPY_REG * (lse - log_total)
        lse = local_lse((src_pot.reshape(tile_rows, 1) - cost) / ENTROPY_REG, 0)
        lse = exchange(lse, ("z", "x", "c"), COL_GROUPS, 2 * NZ * NC)
        tgt_pot = -ENTROPY_REG * (lse - log_total)
    part = jax.ShapeDtypeStruct(cost.shape, jnp.bfloat16)
    block = jax.ShapeDtypeStruct(src_block.shape, jnp.float32)
    half = jax.ShapeDtypeStruct(mine.shape, jnp.float32)
    sent, high, mid = pl.pallas_call(
        send_kernel,
        out_shape=(half, part, part),
        in_specs=[WHOLE] * 3 + [IN_HBM] * 2,
        out_specs=(WHOLE,) * 3,
        scratch_shapes=[
            pltpu.VMEM(src_block.shape, jnp.float32),
            pltpu.VMEM(mine.shape, jnp.float32),
            pltpu.SemaphoreType.DMA((2,)),
        ],
        compiler_params=pltpu.CompilerParams(vmem_limit_bytes=VMEM_LIMIT),
    )(src_pot, tgt_pot, cost, src_block, tgt_block)
    came = lax.ppermute(sent, "c", SWAP)
    src_part = on_tile(push_kernel, block, high, mid, src_block, tgt_block)
    came, src_part = lax.optimization_barrier((came, src_part))
    tgt_half = on_tile(keep_kernel, half, high, mid, src_block, tgt_block, came)
    tgt_sum = scatter_blocks(tgt_half, ("z", "x"), SIDE_GROUPS)
    src_sum = scatter_ring(src_part.reshape(NY, 2, rows, width), y, a)
    src_piece = take(src_pot.reshape(-1, rows), y * 2 + a)
    tgt_piece = take(tgt_pot.reshape(-1, rows), (c * NZ + z) * 2 + b)
    return src_piece, tgt_piece, src_sum / total_points, tgt_sum / total_points


def solution(mesh):
    grid = Mesh(mesh.devices.reshape(NZ, NX, NY, NC), ("z", "x", "y", "c"))
    split = ("z", "x", "y", "c")
    return jax.shard_map(
        per_device,
        mesh=grid,
        in_specs=(P(split, None), P(split, None)),
        out_specs=(P(split), P(split), P(split, None), P(split, None)),
        check_vma=False,
    )
```

time: 264 us -> 252 us (0.955)
  waiting for transfers between devices: 59.2 us -> 21.8 us
  starting transfers between devices: 67.5 us -> 80.4 us
  Pallas kernels: 8.36 us -> 21 us
  blocking collectives: 79.7 us -> 91.4 us
  matrix products: 9.75 us -> 0 us
  other arithmetic: 16.5 us -> 10.2 us
  local copies, waits for them, and re-layouts: 18 us -> 21 us
    ppermute x13 -> x17, waiting for transfers between devices: 44.9 us -> 19.9 us  [the longest x7 9.12 us: scatter_ring(): total = total + lax.ppermute(take(partial, (y + k) % NY), 'y', ring(k))]
    ppermute x13 -> x17, starting transfers between devices: 46 us -> 63.5 us  [the longest x7 28.5 us: gather_ring(): return (pair,) + tuple((lax.ppermute(pair, 'y', ring(k)) for k in STEPS))]
    all_to_all x3 -> x2, waiting for transfers between devices: 12.4 us -> 0.01 us  [all_to_all(): lax.all_to_all(blocks, axes, split_axis=0, concat_axis=0, axis_index_grou...]
    all_to_all x5 -> x6, blocking collectives: 79.7 us -> 91.4 us  [all_to_all(): lax.all_to_all(blocks, axes, split_axis=0, concat_axis=0, axis_index_grou...]
    pallas_call x0 -> x3, Pallas kernels: none -> 10.7 us  [the longest x2 7.06 us: on_tile(): pl.pallas_call(kernel, out_shape=out_shape, in_specs=[WHOLE] * len(args),...]
    dot_general x2 -> x0, matrix products: 9.75 us -> none  [the longest x1 4.93 us: per_device(): jnp.dot(weight, tgt_block, preferred_element_type=jnp.float32, precision=...]
    all_to_all x3 -> x2, starting transfers between devices: 19.6 us -> 15 us  [all_to_all(): lax.all_to_all(blocks, axes, split_axis=0, concat_axis=0, axis_index_grou...]
    unnamed x32 -> x42, local copies, waits for them, and re-layouts: 13.1 us -> 17.1 us
  transfers between devices with their start and end apart: 17 -> 20, of which waited for: 12 -> 9; matrix products, arithmetic and copies ran while one was open for 3% -> 1% of each run, Pallas kernels for 0% -> 1%
where the time goes in v4:
time: 252 us; the launch traced here: 247 us
  blocking collectives  91.4 us (36%)
  starting transfers between devices  80.4 us (32%)
  waiting for transfers between devices  21.8 us (9%)
  local copies, waits for them, and re-layouts  21 us (8%)
  Pallas kernels  21 us (8%)
  other arithmetic  10.2 us (4%)
    all_to_all x6, blocking collectives, all_to_all(): lax.all_to_all(blocks, axes, split_axis=0, concat_axis=0, axis_index_grou...  91.4 us
    ppermute x7, starting transfers between devices, gather_ring(): return (pair,) + tuple((lax.ppermute(pair, 'y', ring(k)) for k in STEPS))  28.5 us
    ppermute x7, starting transfers between devices, scatter_ring(): total = total + lax.ppermute(take(partial, (y + k) % NY), 'y', ring(k))  26.4 us
    unnamed x42, local copies, waits for them, and re-layouts  17.1 us
    all_to_all x2, starting transfers between devices, all_to_all(): lax.all_to_all(blocks, axes, split_axis=0, concat_axis=0, axis_index_grou...  15 us
    pallas_call x1, Pallas kernels, tile(): pl.pallas_call(tile_kernel, out_shape=(jax.ShapeDtypeStruct((rows, width)...  10.3 us
    ppermute x7, waiting for transfers between devices, scatter_ring(): total = total + lax.ppermute(take(partial, (y + k) % NY), 'y', ring(k))  9.12 us
    pallas_call x2, Pallas kernels, on_tile(): pl.pallas_call(kernel, out_shape=out_shape, in_specs=[WHOLE] * len(args),...  7.06 us
  transfers between devices with their start and end apart: 20, of which 9 were waited for; matrix products, arithmetic and copies ran while one was open for 1% of the time, Pallas kernels for 1%

profile of v4, /device:TPU:56, one launch (start us, length us, event | category | flops | bytes accessed | tf_op | source)
XLA Modules:
  0.0 247.1 jit_solution(681870495008436795)
XLA Ops:
  2.8 11.3 %all-to-all-start = ((f32[16,40,512]{2,1,0:T(8,128)}), f32[16,40,512]{2,1,0:T(8,128)S(1)}, u32[]{:S(2)}, u32[]{:S(2)}) async-start(f32[16,40,512]{2,1,0:T(8,128)} %broadcast_in_dim.14), calls=%async_computation | async-start | bytes 2621440 | tf_op jit(solution)/shard_map/all_to_all | solution.py:39
  14.1 4.0 %collective-permute-start = (f32[40,512]{1,0:T(8,128)S(1)}, f32[40,512]{1,0:T(8,128)S(1)}, u32[]{:S(2)}, u32[]{:S(2)}) collective-permute-start(f32[40,512]{1,0:T(8,128)S(1)} %copy-done.20), channel_id=1, source_target_pairs={{0,48},{16,32},{32,16},{48,0},{1,49},{17,33},{33,17},{49,1},{2,50}... | collective-permute-start | bytes 245768 | tf_op jit(solution)/shard_map/ppermute | solution.py:67
  18.2 3.5 %collective-permute-done = f32[40,512]{1,0:T(8,128)S(1)} collective-permute-done((f32[40,512]{1,0:T(8,128)S(1)}, f32[40,512]{1,0:T(8,128)S(1)}, u32[]{:S(2)}, u32[]{:S(2)}) %collective-permute-start) | collective-permute-done | bytes 81952 | tf_op jit(solution)/shard_map/ppermute | solution.py:67
  25.0 3.8 %collective-permute-start.1 = (f32[2,40,512]{2,1,0:T(8,128)S(1)}, f32[2,40,512]{2,1,0:T(8,128)S(1)}, u32[]{:S(2)}, u32[]{:S(2)}) collective-permute-start(f32[2,40,512]{2,1,0:T(8,128)S(1)} %pad_maximum_fusion), channel_id=1, source_target_pairs={{0,8},{2,10},{4,12},{6,14},{8,0},{10,2},{12,4},{14,6},{1,9},{3,11}... | collective-permute-start | bytes 491528 | tf_op jit(solution)/shard_map/ppermute | solution.py:69
  28.8 5.8 %collective-permute-start.2 = (f32[2,40,512]{2,1,0:T(8,128)S(1)}, f32[2,40,512]{2,1,0:T(8,128)S(1)}, u32[]{:S(2)}, u32[]{:S(2)}) collective-permute-start(f32[2,40,512]{2,1,0:T(8,128)S(1)} %pad_maximum_fusion), channel_id=1, source_target_pairs={{0,6},{2,8},{4,10},{6,12},{8,14},{10,0},{12,2},{14,4},{1,7},{3,9},... | collective-permute-start | bytes 491528 | tf_op jit(solution)/shard_map/ppermute | solution.py:69
  36.6 6.8 %collective-permute-start.4 = (f32[2,40,512]{2,1,0:T(8,128)S(1)}, f32[2,40,512]{2,1,0:T(8,128)S(1)}, u32[]{:S(2)}, u32[]{:S(2)}) collective-permute-start(f32[2,40,512]{2,1,0:T(8,128)S(1)} %pad_maximum_fusion), channel_id=1, source_target_pairs={{0,4},{2,6},{4,8},{6,10},{8,12},{10,14},{12,0},{14,2},{1,5},{3,7},... | collective-permute-start | bytes 491528 | tf_op jit(solution)/shard_map/ppermute | solution.py:69
  46.7 5.0 %collective-permute-start.6 = (f32[2,40,512]{2,1,0:T(8,128)S(1)}, f32[2,40,512]{2,1,0:T(8,128)S(1)}, u32[]{:S(2)}, u32[]{:S(2)}) collective-permute-start(f32[2,40,512]{2,1,0:T(8,128)S(1)} %pad_maximum_fusion), channel_id=1, source_target_pairs={{0,2},{2,4},{4,6},{6,8},{8,10},{10,12},{12,14},{14,0},{1,3},{3,5},... | collective-permute-start | bytes 491528 | tf_op jit(solution)/shard_map/ppermute | solution.py:69
  70.5 10.3 %shard_map.57 = (f32[640,512]{1,0:T(8,128)S(1)}, f32[1280,512]{1,0:T(8,128)S(1)}, f32[640,1280]{1,0:T(8,128)S(1)}) custom-call(f32[80,512]{1,0:T(8,128)S(1)} %bitcast.78, f32[80,512]{1,0:T(8,128)S(1)} %bitcast.80, f32[80,512]{1,0:T(8,128)S(1)} %bitcast.81, f32[80,512]{1,0:T(8,128)S(1)} %bitcast.82, f32[80,512]{1,0:T(8,128)S(1)} %bitcast.83, ...), custom_call_target="tpu_custom_call" | custom-call | tf_op jit(solution)/shard_map/pallas_call | solution.py:157
  82.7 16.6 %all_to_all.40 = f32[16,5,128]{2,1,0:T(8,128)S(1)} all-to-all(f32[16,5,128]{2,1,0:T(8,128)S(1)} %broadcast_in_dim.15), channel_id=1, replica_groups={{0,2,4,6,8,10,12,14,48,50,52,54,56,58,60,62},{16,18,20,22,24,26,28,30,3..., dimensions={0} | all-to-all | bytes 81920 | tf_op jit(solution)/shard_map/all_to_all | solution.py:39
  100.6 19.5 %all_to_all.41 = f32[32,10,128]{2,1,0:T(8,128)S(1)} all-to-all(f32[32,10,128]{2,1,0:T(8,128)S(1)} %broadcast_in_dim.16), channel_id=1, replica_groups={{0,1,16,17,64,65,80,81,128,129,144,145,192,193,208,209,256,257,272,273,..., dimensions={0} | all-to-all | bytes 327680 | tf_op jit(solution)/shard_map/all_to_all | solution.py:39
  121.5 12.5 %all_to_all.42 = f32[16,5,128]{2,1,0:T(8,128)S(1)} all-to-all(f32[16,5,128]{2,1,0:T(8,128)S(1)} %broadcast_in_dim.17), channel_id=1, replica_groups={{0,2,4,6,8,10,12,14,48,50,52,54,56,58,60,62},{16,18,20,22,24,26,28,30,3..., dimensions={0} | all-to-all | bytes 81920 | tf_op jit(solution)/shard_map/all_to_all | solution.py:39
  135.2 15.2 %all_to_all.43 = f32[32,10,128]{2,1,0:T(8,128)S(1)} all-to-all(f32[32,10,128]{2,1,0:T(8,128)S(1)} %broadcast_in_dim.18), channel_id=1, replica_groups={{0,1,16,17,64,65,80,81,128,129,144,145,192,193,208,209,256,257,272,273,..., dimensions={0} | all-to-all | bytes 327680 | tf_op jit(solution)/shard_map/all_to_all | solution.py:39
  151.8 12.2 %all_to_all.44 = f32[16,5,128]{2,1,0:T(8,128)S(1)} all-to-all(f32[16,5,128]{2,1,0:T(8,128)S(1)} %broadcast_in_dim.19), channel_id=1, replica_groups={{0,2,4,6,8,10,12,14,48,50,52,54,56,58,60,62},{16,18,20,22,24,26,28,30,3..., dimensions={0} | all-to-all | bytes 81920 | tf_op jit(solution)/shard_map/all_to_all | solution.py:39
  165.3 15.2 %all_to_all.45 = f32[32,10,128]{2,1,0:T(8,128)S(1)} all-to-all(f32[32,10,128]{2,1,0:T(8,128)S(1)} %broadcast_in_dim.20), channel_id=1, replica_groups={{0,1,16,17,64,65,80,81,128,129,144,145,192,193,208,209,256,257,272,273,..., dimensions={0} | all-to-all | bytes 327680 | tf_op jit(solution)/shard_map/all_to_all | solution.py:39
  183.7 3.6 %shard_map.58 = (f32[640,512]{1,0:T(8,128)S(1)}, bf16[640,1280]{1,0:T(8,128)(2,1)S(1)}, bf16[640,1280]{1,0:T(8,128)(2,1)S(1)}) custom-call(f32[5,128]{1,0:T(8,128)S(1)} %add_multiply_fusion.1.src_pot_ref, f32[10,128]{1,0:T(8,128)S(1)} %add_multiply_fusion.tgt_pot_ref, f32[640,1280]{1,0:T(8,128)S(1)} %get-tuple-element.30.cost_ref, f32[640,512]{1,0:T(8,128)S(1)} %copy-done.3, ...), custom_call_target="tpu_custom_call" | custom-call | tf_op jit(solution)/shard_map/pallas_call | solution.py:291
  189.2 3.7 %shard_map.59 = f32[640,512]{1,0:T(8,128)S(1)} custom-call(bf16[640,1280]{1,0:T(8,128)(2,1)S(1)} %get-tuple-element.34.high_ref, bf16[640,1280]{1,0:T(8,128)(2,1)S(1)} %get-tuple-element.35.mid_ref, f32[640,512]{1,0:T(8,128)S(1)} %copy-done.3, f32[1280,512]{1,0:T(8,128)S(1)} %copy-done.1), custom_call_target="tpu_custom_call" | custom-call | tf_op jit(solution)/shard_map/pallas_call | solution.py:242
  192.9 3.4 %shard_map.60 = f32[640,512]{1,0:T(8,128)} custom-call(bf16[640,1280]{1,0:T(8,128)(2,1)S(1)} %get-tuple-element.34.high_ref, bf16[640,1280]{1,0:T(8,128)(2,1)S(1)} %get-tuple-element.35.mid_ref, f32[640,512]{1,0:T(8,128)S(1)} %copy-done.3, f32[1280,512]{1,0:T(8,128)S(1)} %copy-done.1, f32[640,512]{1,0:T(8,128)S(1)} %collective-permute-done.9.came_ref), custom_call_target="tpu_custom_call" | custom-call | tf_op jit(solution)/shard_map/pallas_call | solution.py:242
  196.3 3.7 %all-to-all-start.7 = ((f32[16,40,512]{2,1,0:T(8,128)}), f32[16,40,512]{2,1,0:T(8,128)S(1)}, u32[]{:S(2)}, u32[]{:S(2)}) async-start(f32[16,40,512]{2,1,0:T(8,128)} %bitcast.35), calls=%async_computation.7 | async-start | bytes 2621440 | tf_op jit(solution)/shard_map/all_to_all | solution.py:39
  201.0 4.5 %collective-permute-start.10 = (f32[2,40,512]{2,1,0:T(8,128)S(1)}, f32[2,40,512]{2,1,0:T(8,128)S(1)}, u32[]{:S(2)}, u32[]{:S(2)}) collective-permute-start(f32[2,40,512]{2,1,0:T(8,128)S(1)} %get-tuple-element.38), channel_id=1, source_target_pairs={{0,8},{2,10},{4,12},{6,14},{8,0},{10,2},{12,4},{14,6},{1,9},{3,11}... | collective-permute-start | bytes 491528 | tf_op jit(solution)/shard_map/ppermute | solution.py:75
  205.5 4.2 %collective-permute-start.11 = (f32[2,40,512]{2,1,0:T(8,128)S(1)}, f32[2,40,512]{2,1,0:T(8,128)S(1)}, u32[]{:S(2)}, u32[]{:S(2)}) collective-permute-start(f32[2,40,512]{2,1,0:T(8,128)S(1)} %get-tuple-element.44), channel_id=1, source_target_pairs={{0,6},{2,8},{4,10},{6,12},{8,14},{10,0},{12,2},{14,4},{1,7},{3,9},... | collective-permute-start | bytes 491528 | tf_op jit(solution)/shard_map/ppermute | solution.py:75
  209.7 3.4 %collective-permute-start.12 = (f32[2,40,512]{2,1,0:T(8,128)}, f32[2,40,512]{2,1,0:T(8,128)}, u32[]{:S(2)}, u32[]{:S(2)}) collective-permute-start(f32[2,40,512]{2,1,0:T(8,128)} %get-tuple-element.43), channel_id=1, source_target_pairs={{0,10},{2,12},{4,14},{6,0},{8,2},{10,4},{12,6},{14,8},{1,11},{3,13... | collective-permute-start | bytes 491528 | tf_op jit(solution)/shard_map/ppermute | solution.py:75
  213.1 4.7 %collective-permute-start.13 = (f32[2,40,512]{2,1,0:T(8,128)}, f32[2,40,512]{2,1,0:T(8,128)}, u32[]{:S(2)}, u32[]{:S(2)}) collective-permute-start(f32[2,40,512]{2,1,0:T(8,128)} %get-tuple-element.42), channel_id=1, source_target_pairs={{0,4},{2,6},{4,8},{6,10},{8,12},{10,14},{12,0},{14,2},{1,5},{3,7},... | collective-permute-start | bytes 491528 | tf_op jit(solution)/shard_map/ppermute | solution.py:75
  220.5 4.3 %collective-permute-start.15 = (f32[2,40,512]{2,1,0:T(8,128)S(1)}, f32[2,40,512]{2,1,0:T(8,128)}, u32[]{:S(2)}, u32[]{:S(2)}) collective-permute-start(f32[2,40,512]{2,1,0:T(8,128)S(1)} %get-tuple-element.40), channel_id=1, source_target_pairs={{0,2},{2,4},{4,6},{6,8},{8,10},{10,12},{12,14},{14,0},{1,3},{3,5},... | collective-permute-start | bytes 491528 | tf_op jit(solution)/shard_map/ppermute | solution.py:75
  241.3 4.4 %collective-permute-done.17 = f32[40,512]{1,0:T(8,128)S(1)} collective-permute-done((f32[40,512]{1,0:T(8,128)S(1)}, f32[40,512]{1,0:T(8,128)S(1)}, u32[]{:S(2)}, u32[]{:S(2)}) %collective-permute-start.17) | collective-permute-done | bytes 81952 | tf_op jit(solution)/shard_map/ppermute | solution.py:76
  (122 shorter events, 64.0 us)
Async XLA Ops:
  0.6 13.5 %copy-start.20 = (f32[40,512]{1,0:T(8,128)S(1)}, f32[40,512]{1,0:T(8,128)}, u32[]{:S(2)}) copy-start(f32[40,512]{1,0:T(8,128)} %param.2) | copy-start | bytes 245764
  2.8 55.1 %all-to-all-start = ((f32[16,40,512]{2,1,0:T(8,128)}), f32[16,40,512]{2,1,0:T(8,128)S(1)}, u32[]{:S(2)}, u32[]{:S(2)}) async-start(f32[16,40,512]{2,1,0:T(8,128)} %broadcast_in_dim.14), calls=%async_computation | async-start | bytes 2621440 | tf_op jit(solution)/shard_map/all_to_all | solution.py:39
  14.1 7.5 %collective-permute-start = (f32[40,512]{1,0:T(8,128)S(1)}, f32[40,512]{1,0:T(8,128)S(1)}, u32[]{:S(2)}, u32[]{:S(2)}) collective-permute-start(f32[40,512]{1,0:T(8,128)S(1)} %copy-done.20), channel_id=1, source_target_pairs={{0,48},{16,32},{32,16},{48,0},{1,49},{17,33},{33,17},{49,1},{2,50}... | collective-permute-start | bytes 245768 | tf_op jit(solution)/shard_map/ppermute | solution.py:67
  21.7 21.7 %collective-permute-start.7 = (f32[2,40,512]{2,1,0:T(8,128)S(1)}, f32[2,40,512]{2,1,0:T(8,128)S(1)}, u32[]{:S(2)}, u32[]{:S(2)}) collective-permute-start(f32[2,40,512]{2,1,0:T(8,128)S(1)} %pad_maximum_fusion), channel_id=1, source_target_pairs={{0,14},{2,0},{4,2},{6,4},{8,6},{10,8},{12,10},{14,12},{1,15},{3,1}... | collective-permute-start | bytes 491528 | tf_op jit(solution)/shard_map/ppermute | solution.py:69
  25.0 21.0 %collective-permute-start.1 = (f32[2,40,512]{2,1,0:T(8,128)S(1)}, f32[2,40,512]{2,1,0:T(8,128)S(1)}, u32[]{:S(2)}, u32[]{:S(2)}) collective-permute-start(f32[2,40,512]{2,1,0:T(8,128)S(1)} %pad_maximum_fusion), channel_id=1, source_target_pairs={{0,8},{2,10},{4,12},{6,14},{8,0},{10,2},{12,4},{14,6},{1,9},{3,11}... | collective-permute-start | bytes 491528 | tf_op jit(solution)/shard_map/ppermute | solution.py:69
  28.8 22.9 %collective-permute-start.2 = (f32[2,40,512]{2,1,0:T(8,128)S(1)}, f32[2,40,512]{2,1,0:T(8,128)S(1)}, u32[]{:S(2)}, u32[]{:S(2)}) collective-permute-start(f32[2,40,512]{2,1,0:T(8,128)S(1)} %pad_maximum_fusion), channel_id=1, source_target_pairs={{0,6},{2,8},{4,10},{6,12},{8,14},{10,0},{12,2},{14,4},{1,7},{3,9},... | collective-permute-start | bytes 491528 | tf_op jit(solution)/shard_map/ppermute | solution.py:69
  34.6 18.2 %collective-permute-start.3 = (f32[2,40,512]{2,1,0:T(8,128)S(1)}, f32[2,40,512]{2,1,0:T(8,128)S(1)}, u32[]{:S(2)}, u32[]{:S(2)}) collective-permute-start(f32[2,40,512]{2,1,0:T(8,128)S(1)} %pad_maximum_fusion), channel_id=1, source_target_pairs={{0,10},{2,12},{4,14},{6,0},{8,2},{10,4},{12,6},{14,8},{1,11},{3,13... | collective-permute-start | bytes 491528 | tf_op jit(solution)/shard_map/ppermute | solution.py:69
  36.6 19.3 %collective-permute-start.4 = (f32[2,40,512]{2,1,0:T(8,128)S(1)}, f32[2,40,512]{2,1,0:T(8,128)S(1)}, u32[]{:S(2)}, u32[]{:S(2)}) collective-permute-start(f32[2,40,512]{2,1,0:T(8,128)S(1)} %pad_maximum_fusion), channel_id=1, source_target_pairs={{0,4},{2,6},{4,8},{6,10},{8,12},{10,14},{12,0},{14,2},{1,5},{3,7},... | collective-permute-start | bytes 491528 | tf_op jit(solution)/shard_map/ppermute | solution.py:69
  44.1 12.5 %collective-permute-start.5 = (f32[2,40,512]{2,1,0:T(8,128)S(1)}, f32[2,40,512]{2,1,0:T(8,128)S(1)}, u32[]{:S(2)}, u32[]{:S(2)}) collective-permute-start(f32[2,40,512]{2,1,0:T(8,128)S(1)} %pad_maximum_fusion), channel_id=1, source_target_pairs={{0,12},{2,14},{4,0},{6,2},{8,4},{10,6},{12,8},{14,10},{1,13},{3,15... | collective-permute-start | bytes 491528 | tf_op jit(solution)/shard_map/ppermute | solution.py:69
  46.7 10.5 %collective-permute-start.6 = (f32[2,40,512]{2,1,0:T(8,128)S(1)}, f32[2,40,512]{2,1,0:T(8,128)S(1)}, u32[]{:S(2)}, u32[]{:S(2)}) collective-permute-start(f32[2,40,512]{2,1,0:T(8,128)S(1)} %pad_maximum_fusion), channel_id=1, source_target_pairs={{0,2},{2,4},{4,6},{6,8},{8,10},{10,12},{12,14},{14,0},{1,3},{3,5},... | collective-permute-start | bytes 491528 | tf_op jit(solution)/shard_map/ppermute | solution.py:69
  57.9 4.9 %collective-permute-start.8 = (f32[640,512]{1,0:T(8,128)S(1)}, f32[640,512]{1,0:T(8,128)S(1)}, u32[]{:S(2)}, u32[]{:S(2)}) collective-permute-start(f32[640,512]{1,0:T(8,128)S(1)} %bitcast.74), channel_id=1, source_target_pairs={{0,1},{1,0},{2,3},{3,2},{4,5},{5,4},{6,7},{7,6},{8,9},{9,8},{10,11... | collective-permute-start | bytes 3932168 | tf_op jit(solution)/shard_map/ppermute | solution.py:276
  80.8 1.5 copy-start
  80.8 1.9 copy-start.2
  180.6 1.7 copy-start.1
  187.3 5.6 %collective-permute-start.9 = (f32[640,512]{1,0:T(8,128)S(1)}, f32[640,512]{1,0:T(8,128)S(1)}, u32[]{:S(2)}, u32[]{:S(2)}) collective-permute-start(f32[640,512]{1,0:T(8,128)S(1)} %get-tuple-element.33), channel_id=1, source_target_pairs={{0,1},{1,0},{2,3},{3,2},{4,5},{5,4},{6,7},{7,6},{8,9},{9,8},{10,11... | collective-permute-start | bytes 3932168 | tf_op jit(solution)/shard_map/ppermute | solution.py:303
  196.3 50.0 %all-to-all-start.7 = ((f32[16,40,512]{2,1,0:T(8,128)}), f32[16,40,512]{2,1,0:T(8,128)S(1)}, u32[]{:S(2)}, u32[]{:S(2)}) async-start(f32[16,40,512]{2,1,0:T(8,128)} %bitcast.35), calls=%async_computation.7 | async-start | bytes 2621440 | tf_op jit(solution)/shard_map/all_to_all | solution.py:39
  201.0 19.5 %collective-permute-start.10 = (f32[2,40,512]{2,1,0:T(8,128)S(1)}, f32[2,40,512]{2,1,0:T(8,128)S(1)}, u32[]{:S(2)}, u32[]{:S(2)}) collective-permute-start(f32[2,40,512]{2,1,0:T(8,128)S(1)} %get-tuple-element.38), channel_id=1, source_target_pairs={{0,8},{2,10},{4,12},{6,14},{8,0},{10,2},{12,4},{14,6},{1,9},{3,11}... | collective-permute-start | bytes 491528 | tf_op jit(solution)/shard_map/ppermute | solution.py:75
  205.5 19.3 %collective-permute-start.11 = (f32[2,40,512]{2,1,0:T(8,128)S(1)}, f32[2,40,512]{2,1,0:T(8,128)S(1)}, u32[]{:S(2)}, u32[]{:S(2)}) collective-permute-start(f32[2,40,512]{2,1,0:T(8,128)S(1)} %get-tuple-element.44), channel_id=1, source_target_pairs={{0,6},{2,8},{4,10},{6,12},{8,14},{10,0},{12,2},{14,4},{1,7},{3,9},... | collective-permute-start | bytes 491528 | tf_op jit(solution)/shard_map/ppermute | solution.py:75
  209.7 21.0 %collective-permute-start.12 = (f32[2,40,512]{2,1,0:T(8,128)}, f32[2,40,512]{2,1,0:T(8,128)}, u32[]{:S(2)}, u32[]{:S(2)}) collective-permute-start(f32[2,40,512]{2,1,0:T(8,128)} %get-tuple-element.43), channel_id=1, source_target_pairs={{0,10},{2,12},{4,14},{6,0},{8,2},{10,4},{12,6},{14,8},{1,11},{3,13... | collective-permute-start | bytes 491528 | tf_op jit(solution)/shard_map/ppermute | solution.py:75
  213.1 20.9 %collective-permute-start.13 = (f32[2,40,512]{2,1,0:T(8,128)}, f32[2,40,512]{2,1,0:T(8,128)}, u32[]{:S(2)}, u32[]{:S(2)}) collective-permute-start(f32[2,40,512]{2,1,0:T(8,128)} %get-tuple-element.42), channel_id=1, source_target_pairs={{0,4},{2,6},{4,8},{6,10},{8,12},{10,14},{12,0},{14,2},{1,5},{3,7},... | collective-permute-start | bytes 491528 | tf_op jit(solution)/shard_map/ppermute | solution.py:75
  217.8 16.3 %collective-permute-start.14 = (f32[2,40,512]{2,1,0:T(8,128)S(1)}, f32[2,40,512]{2,1,0:T(8,128)}, u32[]{:S(2)}, u32[]{:S(2)}) collective-permute-start(f32[2,40,512]{2,1,0:T(8,128)S(1)} %get-tuple-element.41), channel_id=1, source_target_pairs={{0,12},{2,14},{4,0},{6,2},{8,4},{10,6},{12,8},{14,10},{1,13},{3,15... | collective-permute-start | bytes 491528 | tf_op jit(solution)/shard_map/ppermute | solution.py:75
  220.5 15.6 %collective-permute-start.15 = (f32[2,40,512]{2,1,0:T(8,128)S(1)}, f32[2,40,512]{2,1,0:T(8,128)}, u32[]{:S(2)}, u32[]{:S(2)}) collective-permute-start(f32[2,40,512]{2,1,0:T(8,128)S(1)} %get-tuple-element.40), channel_id=1, source_target_pairs={{0,2},{2,4},{4,6},{6,8},{8,10},{10,12},{12,14},{14,0},{1,3},{3,5},... | collective-permute-start | bytes 491528 | tf_op jit(solution)/shard_map/ppermute | solution.py:75
  224.8 12.0 %collective-permute-start.16 = (f32[2,40,512]{2,1,0:T(8,128)S(1)}, f32[2,40,512]{2,1,0:T(8,128)}, u32[]{:S(2)}, u32[]{:S(2)}) collective-permute-start(f32[2,40,512]{2,1,0:T(8,128)S(1)} %get-tuple-element.39), channel_id=1, source_target_pairs={{0,14},{2,0},{4,2},{6,4},{8,6},{10,8},{12,10},{14,12},{1,15},{3,1}... | collective-permute-start | bytes 491528 | tf_op jit(solution)/shard_map/ppermute | solution.py:75
  238.2 7.5 %collective-permute-start.17 = (f32[40,512]{1,0:T(8,128)S(1)}, f32[40,512]{1,0:T(8,128)S(1)}, u32[]{:S(2)}, u32[]{:S(2)}) collective-permute-start(f32[40,512]{1,0:T(8,128)S(1)} %dynamic-slice_bitcast_fusion.7), channel_id=1, source_target_pairs={{0,48},{16,32},{32,16},{48,0},{1,49},{17,33},{33,17},{49,1},{2,50}... | collective-permute-start | bytes 245768 | tf_op jit(solution)/shard_map/ppermute | solution.py:76
  (17 other events, 14.7 us)

commit v5 on v4

v5 whole, which is shorter than its diff:
```python
import math

import jax
import jax.numpy as jnp
from jax import lax
from jax.experimental import pallas as pl
from jax.experimental.pallas import tpu as pltpu
from jax.sharding import Mesh
from jax.sharding import PartitionSpec as P

ITERS = 3
ENTROPY_REG = 0.05
NZ, NX, NY, NC = 8, 4, 8, 2
LANES = 128

A_OF_X = (0, 0, 1, 1)
B_OF_X = (0, 1, 1, 0)
FLIP_A = [(x, NX - 1 - x) for x in range(NX)]
FLIP_B = [(x, x ^ 1) for x in range(NX)]
SWAP = [(0, 1), (1, 0)]
X_OF_AB = {(A_OF_X[x], B_OF_X[x]): x for x in range(NX)}

ROW_GROUPS = [[X_OF_AB[a, b] * NY + y for a in range(2) for y in range(NY)] for b in range(2)]
COL_GROUPS = [
    [(z * NX + X_OF_AB[a, b]) * NC + c for z in range(NZ) for b in range(2) for c in range(NC)]
    for a in range(2)
]

SIDE_GROUPS = [
    [z * NX + X_OF_AB[a, b] for z in range(NZ) for b in range(2)] for a in range(2)
]


def take(buffer, index):
    return lax.dynamic_index_in_dim(buffer, index, 0, keepdims=False)


def all_to_all(blocks, axes, groups):
    return lax.all_to_all(
        blocks, axes, split_axis=0, concat_axis=0, axis_index_groups=groups, tiled=True
    )


NEAR = (0, 1, 7, 2)
FAR = (6, 3, 5, 4)
SEND_FIRST = (4, 3, 5, 2)
SEND_LAST = (6, 1, 7, 0)
PASSES = ((0, 0), (0, 1), (1, 0), (1, 1), (0, 2), (2, 0))
IN_HBM = pl.BlockSpec(memory_space=pltpu.HBM)
WHOLE = pl.BlockSpec(memory_space=pltpu.VMEM)
VMEM_LIMIT = 24 * 1024 * 1024


def ring(step):
    return [(i, (i + step) % 8) for i in range(8)]


def gather_blocks(shard, axes, groups):
    blocks = jnp.broadcast_to(shard[None], (len(groups[0]),) + shard.shape)
    return all_to_all(blocks, axes, groups).reshape(-1, shard.shape[1])


def scatter_blocks(partial, axes, groups):
    count = len(groups[0])
    blocks = partial.reshape(count, partial.shape[0] // count, partial.shape[1])
    return jnp.sum(all_to_all(blocks, axes, groups), axis=0)


def gather_ring(shard):
    behind = {k: lax.ppermute(shard, "y", ring(k)) if k else shard for k in NEAR + FAR}
    pieces = []
    for group in (NEAR, FAR):
        mine = jnp.stack([behind[k] for k in group])
        pieces += [mine, lax.ppermute(mine, "x", FLIP_A)]
    return pieces


def scatter_ring(sent, own):
    total = None
    for group, there, here in zip((SEND_FIRST, SEND_LAST), sent, own):
        here = here + lax.ppermute(there, "x", FLIP_A)
        for i, k in enumerate(group):
            part = lax.ppermute(here[i], "y", ring(k)) if k else here[i]
            total = part if total is None else total + part
    return total


def parts_of(values):
    high = values.astype(jnp.bfloat16)
    rest = values - high.astype(jnp.float32)
    mid = rest.astype(jnp.bfloat16)
    low = (rest - mid.astype(jnp.float32)).astype(jnp.bfloat16)
    return high, mid, low


def product(p, q, contract):
    return lax.dot_general(
        p, q, ((contract[:1], contract[1:]), ((), ())), preferred_element_type=jnp.float32
    )


def three_products(p, q, contract):
    return (
        product(p[0], q[0], contract)
        + product(p[0], q[1], contract)
        + product(p[1], q[0], contract)
    )


def cost_half(left_parts, left_sq, right_ref, cost_ref, place):
    cols, width = right_ref.shape
    right = right_ref[...]
    right_parts = parts_of(right)
    cross = sum(product(left_parts[p][...], right_parts[q], (1, 1)) for p, q in PASSES)
    ones = jnp.ones((8, width), jnp.bfloat16)
    right_sq = sum(product(ones, part, (1, 1)) for part in parts_of(right * right))[:1]
    at = pl.ds(pl.multiple_of(place * cols, LANES), cols)
    cost_ref[:, at] = (left_sq + right_sq - 2.0 * cross) / width


def mine_kernel(*refs):
    pieces, mine_hbm = refs[:4], refs[4]
    src_out, high_ref, mid_ref, low_ref, sq_ref, cost_ref = refs[5:11]
    src_ref, mine_ref, sem, out_sem = refs[11:]
    x, y, c = (lax.axis_index(name) for name in ("x", "y", "c"))
    a = x // 2
    size = pieces[0].shape[1]
    copies = [pltpu.make_async_copy(mine_hbm, mine_ref, sem.at[2 * NY])]
    for half, group in enumerate((NEAR, FAR)):
        for side, place in enumerate((a, 1 - a)):
            for i, k in enumerate(group):
                at = pl.multiple_of(((y + NY - k) % NY * 2 + place) * size, 8)
                copies.append(
                    pltpu.make_async_copy(
                        pieces[half * 2 + side].at[i],
                        src_ref.at[pl.ds(at, size)],
                        sem.at[(half * 2 + side) * 4 + i],
                    )
                )
    for copy in copies:
        copy.start()
    for copy in copies:
        copy.wait()
    out = pltpu.make_async_copy(src_ref, src_out, out_sem)
    out.start()
    left = src_ref[...]
    left_sq = jnp.sum(left * left, axis=1, keepdims=True)
    sq_ref[...] = left_sq
    high_ref[...], mid_ref[...], low_ref[...] = parts_of(left)
    cost_half((high_ref, mid_ref, low_ref), left_sq, mine_ref, cost_ref, c)
    out.wait()


def other_kernel(high_ref, mid_ref, low_ref, sq_ref, other_ref, same_ref, cost_ref):
    del same_ref
    place = 1 - lax.axis_index("c")
    cost_half((high_ref, mid_ref, low_ref), sq_ref[...], other_ref, cost_ref, place)


def tile(row_pieces, mine):
    size, width = row_pieces[0].shape[1:]
    rows, cols = 2 * NY * size, 2 * mine.shape[0]
    part = jax.ShapeDtypeStruct((rows, width), jnp.bfloat16)
    src_block, high, mid, low, left_sq, cost = pl.pallas_call(
        mine_kernel,
        out_shape=(
            jax.ShapeDtypeStruct((rows, width), jnp.float32),
            part,
            part,
            part,
            jax.ShapeDtypeStruct((rows, 1), jnp.float32),
            jax.ShapeDtypeStruct((rows, cols), jnp.float32),
        ),
        in_specs=[IN_HBM] * 5,
        out_specs=(IN_HBM,) + (WHOLE,) * 5,
        scratch_shapes=[
            pltpu.VMEM((rows, width), jnp.float32),
            pltpu.VMEM(mine.shape, jnp.float32),
            pltpu.SemaphoreType.DMA((2 * NY + 1,)),
            pltpu.SemaphoreType.DMA,
        ],
        compiler_params=pltpu.CompilerParams(vmem_limit_bytes=VMEM_LIMIT),
    )(*row_pieces, mine)
    other = lax.ppermute(mine, "c", SWAP)
    cost = pl.pallas_call(
        other_kernel,
        out_shape=jax.ShapeDtypeStruct((rows, cols), jnp.float32),
        in_specs=[WHOLE] * 6,
        out_specs=WHOLE,
        input_output_aliases={5: 0},
        compiler_params=pltpu.CompilerParams(vmem_limit_bytes=VMEM_LIMIT),
    )(high, mid, low, left_sq, other, cost)
    return src_block, other, cost


def half_of(high_ref, mid_ref, place):
    size = high_ref.shape[1] // 2
    at = pl.ds(pl.multiple_of(place * size, LANES), size)
    return high_ref[:, at], mid_ref[:, at]


def pull(weight_parts, src_ref, tgt):
    pulled = three_products(weight_parts, parts_of(src_ref[...]), (0, 0))
    ones = jnp.ones((src_ref.shape[0], LANES), jnp.bfloat16)
    mass = sum(product(part, ones, (0, 0)) for part in weight_parts)[:, :1]
    return mass * tgt - pulled


def send_kernel(
    src_pot_ref, tgt_pot_ref, cost_ref, src_hbm, other_hbm, sent_ref, high_ref, mid_ref,
    src_ref, tgt_ref, sem,
):
    rows, cols = cost_ref.shape
    copies = (
        pltpu.make_async_copy(src_hbm, src_ref, sem.at[0]),
        pltpu.make_async_copy(other_hbm, tgt_ref, sem.at[1]),
    )
    for copy in copies:
        copy.start()
    lane = lax.broadcasted_iota(jnp.int32, (LANES, LANES), 1)
    sub = lax.broadcasted_iota(jnp.int32, (LANES, LANES), 0)
    for i in range(rows // LANES):
        row = jnp.broadcast_to(src_pot_ref[i : i + 1, :], (LANES, LANES))
        column = jnp.sum(jnp.where(lane == sub, row, 0.0), axis=1, keepdims=True)
        at = slice(i * LANES, (i + 1) * LANES)
        for j in range(cols // LANES):
            to = slice(j * LANES, (j + 1) * LANES)
            total = column + tgt_pot_ref[j : j + 1, :] - cost_ref[at, to]
            weight = jnp.exp(total / ENTROPY_REG)
            high = weight.astype(jnp.bfloat16)
            high_ref[at, to] = high
            mid_ref[at, to] = (weight - high.astype(jnp.float32)).astype(jnp.bfloat16)
    for copy in copies:
        copy.wait()
    place = 1 - lax.axis_index("c")
    sent_ref[...] = pull(half_of(high_ref, mid_ref, place), src_ref, tgt_ref[...])


def push_kernel(high_ref, mid_ref, src_ref, mine_ref, other_ref, *out_refs):
    sent_refs, own_refs, part_ref = out_refs[:2], out_refs[2:4], out_refs[4]
    x, y, c = (lax.axis_index(name) for name in ("x", "y", "c"))
    a = x // 2
    ones = jnp.ones((mine_ref.shape[0], LANES), jnp.bfloat16)
    pushed, mass = 0.0, 0.0
    for place, ref in ((c, mine_ref), (1 - c, other_ref)):
        weight_parts = half_of(high_ref, mid_ref, place)
        pushed += three_products(weight_parts, parts_of(ref[...]), (1, 0))
        mass += sum(product(part, ones, (1, 0)) for part in weight_parts)
    part_ref[...] = mass[:, :1] * src_ref[...] - pushed
    size = own_refs[0].shape[1]
    for half, group in enumerate((SEND_FIRST, SEND_LAST)):
        for i, k in enumerate(group):
            for ref, place in ((own_refs[half], a), (sent_refs[half], 1 - a)):
                at = pl.multiple_of(((y + k) % NY * 2 + place) * size, 8)
                ref[i] = part_ref[pl.ds(at, size), :]


def keep_kernel(high_ref, mid_ref, src_ref, mine_ref, came_ref, out_ref):
    place = lax.axis_index("c")
    kept = pull(half_of(high_ref, mid_ref, place), src_ref, mine_ref[...])
    out_ref[...] = kept + came_ref[...]


def on_tile(kernel, out_shape, scratch, *args):
    return pl.pallas_call(
        kernel,
        out_shape=out_shape,
        in_specs=[WHOLE] * len(args),
        out_specs=jax.tree.map(lambda _: WHOLE, out_shape),
        scratch_shapes=scratch,
        compiler_params=pltpu.CompilerParams(vmem_limit_bytes=VMEM_LIMIT),
    )(*args)


def exchange(local, axes, groups, count):
    size = local.shape[0]
    flat = local.reshape(1, size // LANES, LANES)
    sent = jnp.broadcast_to(flat, (count, size // LANES, LANES))
    got = all_to_all(sent, axes, groups)
    peak = jnp.max(got, axis=0)
    total = jnp.sum(jnp.exp(got - peak[None]), axis=0)
    return peak + jnp.log(total)


def local_lse(scores, axis):
    peak = jnp.max(scores, axis=axis, keepdims=True)
    total = jnp.sum(jnp.exp(scores - peak), axis=axis)
    return jnp.squeeze(peak, axis) + jnp.log(total)


def per_device(src_emb, tgt_emb):
    rows, width = src_emb.shape
    z, x, y, c = (lax.axis_index(name) for name in ("z", "x", "y", "c"))
    a = x // 2
    b = (x // 2) ^ (x % 2)
    total_points = rows * NZ * NX * NY * NC
    mine = gather_blocks(tgt_emb, ("z", "x"), SIDE_GROUPS)
    row_pieces = gather_ring(src_emb)
    mine, *row_pieces[1:3] = lax.optimization_barrier((mine, *row_pieces[1:3]))
    src_block, other, cost = tile(row_pieces, mine)
    tile_rows, tile_cols = cost.shape
    tgt_pot = jnp.zeros((tile_cols,), jnp.float32)
    log_total = math.log(total_points)
    for _ in range(ITERS):
        lse = local_lse((tgt_pot.reshape(1, tile_cols) - cost) / ENTROPY_REG, 1)
        lse = exchange(lse, ("x", "y"), ROW_GROUPS, 2 * NY)
        src_pot = -ENTROPY_REG * (lse - log_total)
        lse = local_lse((src_pot.reshape(tile_rows, 1) - cost) / ENTROPY_REG, 0)
        lse = exchange(lse, ("z", "x", "c"), COL_GROUPS, 2 * NZ * NC)
        tgt_pot = -ENTROPY_REG * (lse - log_total)
    part = jax.ShapeDtypeStruct(cost.shape, jnp.bfloat16)
    half = jax.ShapeDtypeStruct(mine.shape, jnp.float32)
    sent, high, mid = pl.pallas_call(
        send_kernel,
        out_shape=(half, part, part),
        in_specs=[WHOLE] * 3 + [IN_HBM] * 2,
        out_specs=(WHOLE,) * 3,
        scratch_shapes=[
            pltpu.VMEM(src_block.shape, jnp.float32),
            pltpu.VMEM(mine.shape, jnp.float32),
            pltpu.SemaphoreType.DMA((2,)),
        ],
        compiler_params=pltpu.CompilerParams(vmem_limit_bytes=VMEM_LIMIT),
    )(src_pot, tgt_pot, cost, src_block, other)
    came = lax.ppermute(sent, "c", SWAP)
    four = jax.ShapeDtypeStruct((4, rows, width), jnp.float32)
    scratch = [pltpu.VMEM(src_block.shape, jnp.float32)]
    src_parts = on_tile(push_kernel, (four,) * 4, scratch, high, mid, src_block, mine, other)
    src_parts = list(src_parts)
    came, src_parts[0] = lax.optimization_barrier((came, src_parts[0]))
    tgt_half = on_tile(keep_kernel, half, [], high, mid, src_block, mine, came)
    tgt_sum = scatter_blocks(tgt_half, ("z", "x"), SIDE_GROUPS)
    src_sum = scatter_ring(src_parts[:2], src_parts[2:])
    src_piece = take(src_pot.reshape(-1, rows), y * 2 + a)
    tgt_piece = take(tgt_pot.reshape(-1, rows), (c * NZ + z) * 2 + b)
    return src_piece, tgt_piece, src_sum / total_points, tgt_sum / total_points


def solution(mesh):
    grid = Mesh(mesh.devices.reshape(NZ, NX, NY, NC), ("z", "x", "y", "c"))
    split = ("z", "x", "y", "c")
    return jax.shard_map(
        per_device,
        mesh=grid,
        in_specs=(P(split, None), P(split, None)),
        out_specs=(P(split), P(split), P(split, None), P(split, None)),
        check_vma=False,
    )
```

time: 252 us -> 256 us (1.016)
  the two profiles are of different devices: /device:TPU:56 before, /device:TPU:64 now
where the time goes in v5:
time: 256 us; the launch traced here: 255 us
  blocking collectives  88.6 us (35%)
  starting transfers between devices  87.4 us (34%)
  waiting for transfers between devices  33.8 us (13%)
  Pallas kernels  24.1 us (9%)
  local copies, waits for them, and re-layouts  10.7 us (4%)
  other arithmetic  9.03 us (4%)
    all_to_all x6, blocking collectives, all_to_all(): lax.all_to_all(blocks, axes, split_axis=0, concat_axis=0, axis_index_grou...  88.6 us
    ppermute x7, starting transfers between devices, gather_ring(): lax.ppermute(shard, 'y', ring(k))  27.7 us
    ppermute x7, starting transfers between devices, scatter_ring(): part = lax.ppermute(here[i], 'y', ring(k)) if k else here[i]  26.2 us
    all_to_all x2, starting transfers between devices, all_to_all(): lax.all_to_all(blocks, axes, split_axis=0, concat_axis=0, axis_index_grou...  15.3 us
    ppermute x7, waiting for transfers between devices, gather_ring(): lax.ppermute(shard, 'y', ring(k))  12 us
    pallas_call x2, Pallas kernels, on_tile(): pl.pallas_call(kernel, out_shape=out_shape, in_specs=[WHOLE] * len(args),...  10.4 us
    ppermute x2, waiting for transfers between devices, gather_ring(): pieces += [mine, lax.ppermute(mine, 'x', FLIP_A)]  9.42 us
    unnamed x26, local copies, waits for them, and re-layouts  7.74 us
  transfers between devices with their start and end apart: 22, of which 7 were waited for; matrix products, arithmetic and copies ran while one was open for 1% of the time, Pallas kernels for 5%

profile of v5, /device:TPU:64, one launch (start us, length us, event | category | flops | bytes accessed | tf_op | source)
XLA Modules:
  0.0 254.9 jit_solution(11012773565613037461)
XLA Ops:
  2.8 10.9 %all-to-all-start = ((f32[16,40,512]{2,1,0:T(8,128)}), f32[16,40,512]{2,1,0:T(8,128)}, u32[]{:S(2)}, u32[]{:S(2)}) async-start(f32[16,40,512]{2,1,0:T(8,128)} %broadcast_in_dim.14), calls=%async_computation | async-start | bytes 2621440 | tf_op jit(solution)/shard_map/all_to_all | solution.py:39
  17.2 3.8 %collective-permute-start.1 = (f32[40,512]{1,0:T(8,128)S(1)}, f32[40,512]{1,0:T(8,128)S(1)}, u32[]{:S(2)}, u32[]{:S(2)}) collective-permute-start(f32[40,512]{1,0:T(8,128)S(1)} %copy-done.12), channel_id=1, source_target_pairs={{0,14},{2,0},{4,2},{6,4},{8,6},{10,8},{12,10},{14,12},{1,15},{3,1}... | collective-permute-start | bytes 245768 | tf_op jit(solution)/shard_map/ppermute | solution.py:70
  24.1 6.3 %collective-permute-done.2 = f32[40,512]{1,0:T(8,128)S(1)} collective-permute-done((f32[40,512]{1,0:T(8,128)S(1)}, f32[40,512]{1,0:T(8,128)S(1)}, u32[]{:S(2)}, u32[]{:S(2)}) %collective-permute-start.2) | collective-permute-done | bytes 81952 | tf_op jit(solution)/shard_map/ppermute | solution.py:70
  30.4 4.0 %collective-permute-start.3 = (f32[4,40,512]{2,1,0:T(8,128)S(1)}, f32[4,40,512]{2,1,0:T(8,128)S(1)}, u32[]{:S(2)}, u32[]{:S(2)}) collective-permute-start(f32[4,40,512]{2,1,0:T(8,128)S(1)} %pad_maximum_fusion.refs_0_), channel_id=1, source_target_pairs={{0,48},{16,32},{32,16},{48,0},{1,49},{17,33},{33,17},{49,1},{2,50}... | collective-permute-start | bytes 983048 | tf_op jit(solution)/shard_map/ppermute | solution.py:74
  41.8 5.4 %collective-permute-start.6 = (f32[40,512]{1,0:T(8,128)S(1)}, f32[40,512]{1,0:T(8,128)S(1)}, u32[]{:S(2)}, u32[]{:S(2)}) collective-permute-start(f32[40,512]{1,0:T(8,128)S(1)} %copy-done.12), channel_id=1, source_target_pairs={{0,10},{2,12},{4,14},{6,0},{8,2},{10,4},{12,6},{14,8},{1,11},{3,13... | collective-permute-start | bytes 245768 | tf_op jit(solution)/shard_map/ppermute | solution.py:70
  47.2 5.3 %collective-permute-start.7 = (f32[40,512]{1,0:T(8,128)S(1)}, f32[40,512]{1,0:T(8,128)S(1)}, u32[]{:S(2)}, u32[]{:S(2)}) collective-permute-start(f32[40,512]{1,0:T(8,128)S(1)} %copy-done.12), channel_id=1, source_target_pairs={{0,8},{2,10},{4,12},{6,14},{8,0},{10,2},{12,4},{14,6},{1,9},{3,11}... | collective-permute-start | bytes 245768 | tf_op jit(solution)/shard_map/ppermute | solution.py:70
  64.8 9.4 %collective-permute-done.8.refs_3_ = f32[4,40,512]{2,1,0:T(8,128)S(1)} collective-permute-done((f32[4,40,512]{2,1,0:T(8,128)S(1)}, f32[4,40,512]{2,1,0:T(8,128)S(1)}, u32[]{:S(2)}, u32[]{:S(2)}) %collective-permute-start.8) | collective-permute-done | bytes 327712 | tf_op jit(solution)/shard_map/ppermute | solution.py:74
  77.1 6.1 %shard_map.57 = (f32[640,512]{1,0:T(8,128)S(1)}, bf16[640,512]{1,0:T(8,128)(2,1)S(1)}, bf16[640,512]{1,0:T(8,128)(2,1)S(1)}, bf16[640,512]{1,0:T(8,128)(2,1)S(1)...) custom-call(f32[4,40,512]{2,1,0:T(8,128)S(1)} %copy-done.7, f32[4,40,512]{2,1,0:T(8,128)S(1)} %copy-done.11, ...), custom_call_target="tpu_custom_call" | custom-call | tf_op jit(solution)/shard_map/pallas_call | solution.py:164
  83.3 4.0 %shard_map.58.cost_ref = f32[640,1280]{1,0:T(8,128)S(1)} custom-call(bf16[640,512]{1,0:T(8,128)(2,1)S(1)} %get-tuple-element.25.high_ref, bf16[640,512]{1,0:T(8,128)(2,1)S(1)} %get-tuple-element.26.mid_ref, bf16[640,512]{1,0:T(8,128)(2,1)S(1)} %get-tuple-element.27.low_ref, f32[640,1]{1,0:T(8,128)S(1)} %get-tuple-element.28.sq_ref, ...), custom_call_target="tpu_custom_call", output_to_operand_aliasing={{}: (5, {})} | custom-call | tf_op jit(solution)/shard_map/pallas_call | solution.py:185
  88.5 14.9 %all_to_all.40 = f32[16,5,128]{2,1,0:T(8,128)S(1)} all-to-all(f32[16,5,128]{2,1,0:T(8,128)S(1)} %broadcast_in_dim.15), channel_id=1, replica_groups={{0,2,4,6,8,10,12,14,48,50,52,54,56,58,60,62},{16,18,20,22,24,26,28,30,3..., dimensions={0} | all-to-all | bytes 81920 | tf_op jit(solution)/shard_map/all_to_all | solution.py:39
  104.6 18.7 %all_to_all.41 = f32[32,10,128]{2,1,0:T(8,128)S(1)} all-to-all(f32[32,10,128]{2,1,0:T(8,128)S(1)} %broadcast_in_dim.16), channel_id=1, replica_groups={{0,1,16,17,64,65,80,81,128,129,144,145,192,193,208,209,256,257,272,273,..., dimensions={0} | all-to-all | bytes 327680 | tf_op jit(solution)/shard_map/all_to_all | solution.py:39
  124.6 12.3 %all_to_all.42 = f32[16,5,128]{2,1,0:T(8,128)S(1)} all-to-all(f32[16,5,128]{2,1,0:T(8,128)S(1)} %broadcast_in_dim.17), channel_id=1, replica_groups={{0,2,4,6,8,10,12,14,48,50,52,54,56,58,60,62},{16,18,20,22,24,26,28,30,3..., dimensions={0} | all-to-all | bytes 81920 | tf_op jit(solution)/shard_map/all_to_all | solution.py:39
  138.2 15.2 %all_to_all.43 = f32[32,10,128]{2,1,0:T(8,128)S(1)} all-to-all(f32[32,10,128]{2,1,0:T(8,128)S(1)} %broadcast_in_dim.18), channel_id=1, replica_groups={{0,1,16,17,64,65,80,81,128,129,144,145,192,193,208,209,256,257,272,273,..., dimensions={0} | all-to-all | bytes 327680 | tf_op jit(solution)/shard_map/all_to_all | solution.py:39
  154.7 12.3 %all_to_all.44 = f32[16,5,128]{2,1,0:T(8,128)S(1)} all-to-all(f32[16,5,128]{2,1,0:T(8,128)S(1)} %broadcast_in_dim.19), channel_id=1, replica_groups={{0,2,4,6,8,10,12,14,48,50,52,54,56,58,60,62},{16,18,20,22,24,26,28,30,3..., dimensions={0} | all-to-all | bytes 81920 | tf_op jit(solution)/shard_map/all_to_all | solution.py:39
  168.2 15.3 %all_to_all.45 = f32[32,10,128]{2,1,0:T(8,128)S(1)} all-to-all(f32[32,10,128]{2,1,0:T(8,128)S(1)} %broadcast_in_dim.20), channel_id=1, replica_groups={{0,1,16,17,64,65,80,81,128,129,144,145,192,193,208,209,256,257,272,273,..., dimensions={0} | all-to-all | bytes 327680 | tf_op jit(solution)/shard_map/all_to_all | solution.py:39
  186.3 3.7 %shard_map.59 = (f32[640,512]{1,0:T(8,128)S(1)}, bf16[640,1280]{1,0:T(8,128)(2,1)S(1)}, bf16[640,1280]{1,0:T(8,128)(2,1)S(1)}) custom-call(f32[5,128]{1,0:T(8,128)S(1)} %add_multiply_fusion.1.src_pot_ref, f32[10,128]{1,0:T(8,128)S(1)} %add_multiply_fusion.tgt_pot_ref, f32[640,1280]{1,0:T(8,128)S(1)} %shard_map.58.cost_ref, f32[640,512]{1,0:T(8,128)S(1)} %copy-done.4, ...), custom_call_target="tpu_custom_call" | custom-call | tf_op jit(solution)/shard_map/pallas_call | solution.py:313
  192.1 5.7 %shard_map.60 = (f32[4,40,512]{2,1,0:T(8,128)S(1)}, f32[4,40,512]{2,1,0:T(8,128)S(1)}, f32[4,40,512]{2,1,0:T(8,128)S(1)}, f32[4,40,512]{2,1,0:T(8,128)S(1)}) custom-call(bf16[640,1280]{1,0:T(8,128)(2,1)S(1)} %get-tuple-element.31.high_ref, bf16[640,1280]{1,0:T(8,128)(2,1)S(1)} %get-tuple-element.32.mid_ref, f32[640,512]{1,0:T(8,128)S(1)} %copy-done.5, ...), custom_call_target="tpu_custom_call" | custom-call | tf_op jit(solution)/shard_map/pallas_call | solution.py:265
  197.8 4.7 %shard_map.61 = f32[640,512]{1,0:T(8,128)} custom-call(bf16[640,1280]{1,0:T(8,128)(2,1)S(1)} %get-tuple-element.31.high_ref, bf16[640,1280]{1,0:T(8,128)(2,1)S(1)} %get-tuple-element.32.mid_ref, f32[640,512]{1,0:T(8,128)S(1)} %copy-done.5, f32[640,512]{1,0:T(8,128)} %bitcast.4.refs_4_.mine_ref, f32[640,512]{1,0:T(8,128)S(1)} %collective-permute-done.10.came_ref), custom_call_target="tpu_custom_call" | custom-call | tf_op jit(solution)/shard_map/pallas_call | solution.py:265
  202.5 4.4 %all-to-all-start.7 = ((f32[16,40,512]{2,1,0:T(8,128)}), f32[16,40,512]{2,1,0:T(8,128)S(1)}, u32[]{:S(2)}, u32[]{:S(2)}) async-start(f32[16,40,512]{2,1,0:T(8,128)} %bitcast.30), calls=%async_computation.7 | async-start | bytes 2621440 | tf_op jit(solution)/shard_map/all_to_all | solution.py:39
  209.6 4.4 %collective-permute-start.11 = (f32[4,40,512]{2,1,0:T(8,128)S(1)}, f32[4,40,512]{2,1,0:T(8,128)S(1)}, u32[]{:S(2)}, u32[]{:S(2)}) collective-permute-start(f32[4,40,512]{2,1,0:T(8,128)S(1)} %get-tuple-element.36), channel_id=1, source_target_pairs={{0,48},{16,32},{32,16},{48,0},{1,49},{17,33},{33,17},{49,1},{2,50}... | collective-permute-start | bytes 983048 | tf_op jit(solution)/shard_map/ppermute | solution.py:81
  214.2 6.4 %collective-permute-done.16 = f32[4,40,512]{2,1,0:T(8,128)S(1)} collective-permute-done((f32[4,40,512]{2,1,0:T(8,128)S(1)}, f32[4,40,512]{2,1,0:T(8,128)S(1)}, u32[]{:S(2)}, u32[]{:S(2)}) %collective-permute-start.16) | collective-permute-done | bytes 327712 | tf_op jit(solution)/shard_map/ppermute | solution.py:81
  230.7 5.4 %collective-permute-start.12 = (f32[40,512]{1,0:T(8,128)S(1)}, f32[40,512]{1,0:T(8,128)S(1)}, u32[]{:S(2)}, u32[]{:S(2)}) collective-permute-start(f32[40,512]{1,0:T(8,128)S(1)} %get-tuple-element.43), channel_id=1, source_target_pairs={{0,8},{2,10},{4,12},{6,14},{8,0},{10,2},{12,4},{14,6},{1,9},{3,11}... | collective-permute-start | bytes 245768 | tf_op jit(solution)/shard_map/ppermute | solution.py:83
  238.1 6.9 %collective-permute-start.14 = (f32[40,512]{1,0:T(8,128)S(1)}, f32[40,512]{1,0:T(8,128)S(1)}, u32[]{:S(2)}, u32[]{:S(2)}) collective-permute-start(f32[40,512]{1,0:T(8,128)S(1)} %get-tuple-element.42), channel_id=1, source_target_pairs={{0,10},{2,12},{4,14},{6,0},{8,2},{10,4},{12,6},{14,8},{1,11},{3,13... | collective-permute-start | bytes 245768 | tf_op jit(solution)/shard_map/ppermute | solution.py:83
  248.2 5.3 %collective-permute-done.15 = f32[40,512]{1,0:T(8,128)S(1)} collective-permute-done((f32[40,512]{1,0:T(8,128)S(1)}, f32[40,512]{1,0:T(8,128)S(1)}, u32[]{:S(2)}, u32[]{:S(2)}) %collective-permute-start.15) | collective-permute-done | bytes 81952 | tf_op jit(solution)/shard_map/ppermute | solution.py:83
  (112 shorter events, 62.9 us)
Async XLA Ops:
  0.6 13.1 %copy-start.12 = (f32[40,512]{1,0:T(8,128)S(1)}, f32[40,512]{1,0:T(8,128)}, u32[]{:S(2)}) copy-start(f32[40,512]{1,0:T(8,128)} %param.2) | copy-start | bytes 245764
  2.8 56.3 %all-to-all-start = ((f32[16,40,512]{2,1,0:T(8,128)}), f32[16,40,512]{2,1,0:T(8,128)}, u32[]{:S(2)}, u32[]{:S(2)}) async-start(f32[16,40,512]{2,1,0:T(8,128)} %broadcast_in_dim.14), calls=%async_computation | async-start | bytes 2621440 | tf_op jit(solution)/shard_map/all_to_all | solution.py:39
  13.7 10.4 %collective-permute-start = (f32[40,512]{1,0:T(8,128)S(1)}, f32[40,512]{1,0:T(8,128)S(1)}, u32[]{:S(2)}, u32[]{:S(2)}) collective-permute-start(f32[40,512]{1,0:T(8,128)S(1)} %copy-done.12), channel_id=1, source_target_pairs={{0,2},{2,4},{4,6},{6,8},{8,10},{10,12},{12,14},{14,0},{1,3},{3,5},... | collective-permute-start | bytes 245768 | tf_op jit(solution)/shard_map/ppermute | solution.py:70
  17.2 6.9 %collective-permute-start.1 = (f32[40,512]{1,0:T(8,128)S(1)}, f32[40,512]{1,0:T(8,128)S(1)}, u32[]{:S(2)}, u32[]{:S(2)}) collective-permute-start(f32[40,512]{1,0:T(8,128)S(1)} %copy-done.12), channel_id=1, source_target_pairs={{0,14},{2,0},{4,2},{6,4},{8,6},{10,8},{12,10},{14,12},{1,15},{3,1}... | collective-permute-start | bytes 245768 | tf_op jit(solution)/shard_map/ppermute | solution.py:70
  21.0 9.3 %collective-permute-start.2 = (f32[40,512]{1,0:T(8,128)S(1)}, f32[40,512]{1,0:T(8,128)S(1)}, u32[]{:S(2)}, u32[]{:S(2)}) collective-permute-start(f32[40,512]{1,0:T(8,128)S(1)} %copy-done.12), channel_id=1, source_target_pairs={{0,4},{2,6},{4,8},{6,10},{8,12},{10,14},{12,0},{14,2},{1,5},{3,7},... | collective-permute-start | bytes 245768 | tf_op jit(solution)/shard_map/ppermute | solution.py:70
  30.4 28.0 %collective-permute-start.3 = (f32[4,40,512]{2,1,0:T(8,128)S(1)}, f32[4,40,512]{2,1,0:T(8,128)S(1)}, u32[]{:S(2)}, u32[]{:S(2)}) collective-permute-start(f32[4,40,512]{2,1,0:T(8,128)S(1)} %pad_maximum_fusion.refs_0_), channel_id=1, source_target_pairs={{0,48},{16,32},{32,16},{48,0},{1,49},{17,33},{33,17},{49,1},{2,50}... | collective-permute-start | bytes 983048 | tf_op jit(solution)/shard_map/ppermute | solution.py:74
  35.1 17.4 %collective-permute-start.4 = (f32[40,512]{1,0:T(8,128)S(1)}, f32[40,512]{1,0:T(8,128)S(1)}, u32[]{:S(2)}, u32[]{:S(2)}) collective-permute-start(f32[40,512]{1,0:T(8,128)S(1)} %copy-done.12), channel_id=1, source_target_pairs={{0,12},{2,14},{4,0},{6,2},{8,4},{10,6},{12,8},{14,10},{1,13},{3,15... | collective-permute-start | bytes 245768 | tf_op jit(solution)/shard_map/ppermute | solution.py:70
  38.4 14.2 %collective-permute-start.5 = (f32[40,512]{1,0:T(8,128)S(1)}, f32[40,512]{1,0:T(8,128)S(1)}, u32[]{:S(2)}, u32[]{:S(2)}) collective-permute-start(f32[40,512]{1,0:T(8,128)S(1)} %copy-done.12), channel_id=1, source_target_pairs={{0,6},{2,8},{4,10},{6,12},{8,14},{10,0},{12,2},{14,4},{1,7},{3,9},... | collective-permute-start | bytes 245768 | tf_op jit(solution)/shard_map/ppermute | solution.py:70
  41.8 13.2 %collective-permute-start.6 = (f32[40,512]{1,0:T(8,128)S(1)}, f32[40,512]{1,0:T(8,128)S(1)}, u32[]{:S(2)}, u32[]{:S(2)}) collective-permute-start(f32[40,512]{1,0:T(8,128)S(1)} %copy-done.12), channel_id=1, source_target_pairs={{0,10},{2,12},{4,14},{6,0},{8,2},{10,4},{12,6},{14,8},{1,11},{3,13... | collective-permute-start | bytes 245768 | tf_op jit(solution)/shard_map/ppermute | solution.py:70
  47.2 11.1 %collective-permute-start.7 = (f32[40,512]{1,0:T(8,128)S(1)}, f32[40,512]{1,0:T(8,128)S(1)}, u32[]{:S(2)}, u32[]{:S(2)}) collective-permute-start(f32[40,512]{1,0:T(8,128)S(1)} %copy-done.12), channel_id=1, source_target_pairs={{0,8},{2,10},{4,12},{6,14},{8,0},{10,2},{12,4},{14,6},{1,9},{3,11}... | collective-permute-start | bytes 245768 | tf_op jit(solution)/shard_map/ppermute | solution.py:70
  59.1 24.2 %collective-permute-start.9 = (f32[640,512]{1,0:T(8,128)}, f32[640,512]{1,0:T(8,128)S(1)}, u32[]{:S(2)}, u32[]{:S(2)}) collective-permute-start(f32[640,512]{1,0:T(8,128)} %bitcast.4.refs_4_.mine_ref), channel_id=1, source_target_pairs={{0,1},{1,0},{2,3},{3,2},{4,5},{5,4},{6,7},{7,6},{8,9},{9,8},{10,11... | collective-permute-start | bytes 3932168 | tf_op jit(solution)/shard_map/ppermute | solution.py:184
  61.0 13.2 %collective-permute-start.8 = (f32[4,40,512]{2,1,0:T(8,128)S(1)}, f32[4,40,512]{2,1,0:T(8,128)S(1)}, u32[]{:S(2)}, u32[]{:S(2)}) collective-permute-start(f32[4,40,512]{2,1,0:T(8,128)S(1)} %pad_maximum_fusion.1.refs_2_), channel_id=1, source_target_pairs={{0,48},{16,32},{32,16},{48,0},{1,49},{17,33},{33,17},{49,1},{2,50}... | collective-permute-start | bytes 983048 | tf_op jit(solution)/shard_map/ppermute | solution.py:74
  186.3 5.8 %copy-start.5 = (f32[640,512]{1,0:T(8,128)S(1)}, f32[640,512]{1,0:T(8,128)}, u32[]{:S(2)}) copy-start(f32[640,512]{1,0:T(8,128)} %copy-done.3) | copy-start | bytes 3932164
  189.9 7.9 %collective-permute-start.10 = (f32[640,512]{1,0:T(8,128)S(1)}, f32[640,512]{1,0:T(8,128)S(1)}, u32[]{:S(2)}, u32[]{:S(2)}) collective-permute-start(f32[640,512]{1,0:T(8,128)S(1)} %get-tuple-element.34), channel_id=1, source_target_pairs={{0,1},{1,0},{2,3},{3,2},{4,5},{5,4},{6,7},{7,6},{8,9},{9,8},{10,11... | collective-permute-start | bytes 3932168 | tf_op jit(solution)/shard_map/ppermute | solution.py:325
  202.5 51.7 %all-to-all-start.7 = ((f32[16,40,512]{2,1,0:T(8,128)}), f32[16,40,512]{2,1,0:T(8,128)S(1)}, u32[]{:S(2)}, u32[]{:S(2)}) async-start(f32[16,40,512]{2,1,0:T(8,128)} %bitcast.30), calls=%async_computation.7 | async-start | bytes 2621440 | tf_op jit(solution)/shard_map/all_to_all | solution.py:39
  207.0 13.6 %collective-permute-start.16 = (f32[4,40,512]{2,1,0:T(8,128)S(1)}, f32[4,40,512]{2,1,0:T(8,128)S(1)}, u32[]{:S(2)}, u32[]{:S(2)}) collective-permute-start(f32[4,40,512]{2,1,0:T(8,128)S(1)} %get-tuple-element.38), channel_id=1, source_target_pairs={{0,48},{16,32},{32,16},{48,0},{1,49},{17,33},{33,17},{49,1},{2,50}... | collective-permute-start | bytes 983048 | tf_op jit(solution)/shard_map/ppermute | solution.py:81
  209.6 21.1 %collective-permute-start.11 = (f32[4,40,512]{2,1,0:T(8,128)S(1)}, f32[4,40,512]{2,1,0:T(8,128)S(1)}, u32[]{:S(2)}, u32[]{:S(2)}) collective-permute-start(f32[4,40,512]{2,1,0:T(8,128)S(1)} %get-tuple-element.36), channel_id=1, source_target_pairs={{0,48},{16,32},{32,16},{48,0},{1,49},{17,33},{33,17},{49,1},{2,50}... | collective-permute-start | bytes 983048 | tf_op jit(solution)/shard_map/ppermute | solution.py:81
  220.7 17.4 %collective-permute-start.17 = (f32[40,512]{1,0:T(8,128)S(1)}, f32[40,512]{1,0:T(8,128)S(1)}, u32[]{:S(2)}, u32[]{:S(2)}) collective-permute-start(f32[40,512]{1,0:T(8,128)S(1)} %get-tuple-element.44), channel_id=1, source_target_pairs={{0,12},{2,14},{4,0},{6,2},{8,4},{10,6},{12,8},{14,10},{1,13},{3,15... | collective-permute-start | bytes 245768 | tf_op jit(solution)/shard_map/ppermute | solution.py:83
  223.6 21.5 %collective-permute-start.18 = (f32[40,512]{1,0:T(8,128)S(1)}, f32[40,512]{1,0:T(8,128)S(1)}, u32[]{:S(2)}, u32[]{:S(2)}) collective-permute-start(f32[40,512]{1,0:T(8,128)S(1)} %get-tuple-element.46), channel_id=1, source_target_pairs={{0,2},{2,4},{4,6},{6,8},{8,10},{10,12},{12,14},{14,0},{1,3},{3,5},... | collective-permute-start | bytes 245768 | tf_op jit(solution)/shard_map/ppermute | solution.py:83
  227.1 20.4 %collective-permute-start.19 = (f32[40,512]{1,0:T(8,128)S(1)}, f32[40,512]{1,0:T(8,128)S(1)}, u32[]{:S(2)}, u32[]{:S(2)}) collective-permute-start(f32[40,512]{1,0:T(8,128)S(1)} %get-tuple-element.45), channel_id=1, source_target_pairs={{0,14},{2,0},{4,2},{6,4},{8,6},{10,8},{12,10},{14,12},{1,15},{3,1}... | collective-permute-start | bytes 245768 | tf_op jit(solution)/shard_map/ppermute | solution.py:83
  230.7 16.8 %collective-permute-start.12 = (f32[40,512]{1,0:T(8,128)S(1)}, f32[40,512]{1,0:T(8,128)S(1)}, u32[]{:S(2)}, u32[]{:S(2)}) collective-permute-start(f32[40,512]{1,0:T(8,128)S(1)} %get-tuple-element.43), channel_id=1, source_target_pairs={{0,8},{2,10},{4,12},{6,14},{8,0},{10,2},{12,4},{14,6},{1,9},{3,11}... | collective-permute-start | bytes 245768 | tf_op jit(solution)/shard_map/ppermute | solution.py:83
  236.2 11.4 %collective-permute-start.13 = (f32[40,512]{1,0:T(8,128)S(1)}, f32[40,512]{1,0:T(8,128)S(1)}, u32[]{:S(2)}, u32[]{:S(2)}) collective-permute-start(f32[40,512]{1,0:T(8,128)S(1)} %get-tuple-element.40), channel_id=1, source_target_pairs={{0,6},{2,8},{4,10},{6,12},{8,14},{10,0},{12,2},{14,4},{1,7},{3,9},... | collective-permute-start | bytes 245768 | tf_op jit(solution)/shard_map/ppermute | solution.py:83
  238.1 10.1 %collective-permute-start.14 = (f32[40,512]{1,0:T(8,128)S(1)}, f32[40,512]{1,0:T(8,128)S(1)}, u32[]{:S(2)}, u32[]{:S(2)}) collective-permute-start(f32[40,512]{1,0:T(8,128)S(1)} %get-tuple-element.42), channel_id=1, source_target_pairs={{0,10},{2,12},{4,14},{6,0},{8,2},{10,4},{12,6},{14,8},{1,11},{3,13... | collective-permute-start | bytes 245768 | tf_op jit(solution)/shard_map/ppermute | solution.py:83
  245.1 8.4 %collective-permute-start.15 = (f32[40,512]{1,0:T(8,128)S(1)}, f32[40,512]{1,0:T(8,128)S(1)}, u32[]{:S(2)}, u32[]{:S(2)}) collective-permute-start(f32[40,512]{1,0:T(8,128)S(1)} %get-tuple-element.41), channel_id=1, source_target_pairs={{0,4},{2,6},{4,8},{6,10},{8,12},{10,14},{12,0},{14,2},{1,5},{3,7},... | collective-permute-start | bytes 245768 | tf_op jit(solution)/shard_map/ppermute | solution.py:83
  (11 other events, 21.6 us)

commit v6 on v5

--- a/solution.py
+++ b/solution.py
@@ -27,7 +27,7 @@
 ]
 
 SIDE_GROUPS = [
-    [z * NX + X_OF_AB[a, b] for z in range(NZ) for b in range(2)] for a in range(2)
+    [z * NX + X_OF_AB[a, b] for b in range(2) for z in range(NZ)] for a in range(2)
 ]
 
 
@@ -41,48 +41,16 @@
     )
 
 
-NEAR = (0, 1, 7, 2)
-FAR = (6, 3, 5, 4)
-SEND_FIRST = (4, 3, 5, 2)
-SEND_LAST = (6, 1, 7, 0)
 PASSES = ((0, 0), (0, 1), (1, 0), (1, 1), (0, 2), (2, 0))
 IN_HBM = pl.BlockSpec(memory_space=pltpu.HBM)
 WHOLE = pl.BlockSpec(memory_space=pltpu.VMEM)
 VMEM_LIMIT = 24 * 1024 * 1024
 
 
-def ring(step):
-    return [(i, (i + step) % 8) for i in range(8)]
-
-
-def gather_blocks(shard, axes, groups):
-    blocks = jnp.broadcast_to(shard[None], (len(groups[0]),) + shard.shape)
-    return all_to_all(blocks, axes, groups).reshape(-1, shard.shape[1])
-
-
 def scatter_blocks(partial, axes, groups):
     count = len(groups[0])
     blocks = partial.reshape(count, partial.shape[0] // count, partial.shape[1])
     return jnp.sum(all_to_all(blocks, axes, groups), axis=0)
-
-
-def gather_ring(shard):
-    behind = {k: lax.ppermute(shard, "y", ring(k)) if k else shard for k in NEAR + FAR}
-    pieces = []
-    for group in (NEAR, FAR):
-        mine = jnp.stack([behind[k] for k in group])
-        pieces += [mine, lax.ppermute(mine, "x", FLIP_A)]
-    return pieces
-
-
-def scatter_ring(sent, own):
-    total = None
-    for group, there, here in zip((SEND_FIRST, SEND_LAST), sent, own):
-        here = here + lax.ppermute(there, "x", FLIP_A)
-        for i, k in enumerate(group):
-            part = lax.ppermute(here[i], "y", ring(k)) if k else here[i]
-            total = part if total is None else total + part
-    return total
 
 
 def parts_of(values):
@@ -119,24 +87,18 @@
 
 
 def mine_kernel(*refs):
-    pieces, mine_hbm = refs[:4], refs[4]
-    src_out, high_ref, mid_ref, low_ref, sq_ref, cost_ref = refs[5:11]
-    src_ref, mine_ref, sem, out_sem = refs[11:]
-    x, y, c = (lax.axis_index(name) for name in ("x", "y", "c"))
+    pieces, mine_hbm = refs[:2], refs[2]
+    src_out, high_ref, mid_ref, low_ref, sq_ref, cost_ref = refs[3:9]
+    src_ref, mine_ref, sem, out_sem = refs[9:]
+    x, c = (lax.axis_index(name) for name in ("x", "c"))
     a = x // 2
-    size = pieces[0].shape[1]
-    copies = [pltpu.make_async_copy(mine_hbm, mine_ref, sem.at[2 * NY])]
-    for half, group in enumerate((NEAR, FAR)):
-        for side, place in enumerate((a, 1 - a)):
-            for i, k in enumerate(group):
-                at = pl.multiple_of(((y + NY - k) % NY * 2 + place) * size, 8)
-                copies.append(
-                    pltpu.make_async_copy(
-                        pieces[half * 2 + side].at[i],
-                        src_ref.at[pl.ds(at, size)],
-                        sem.at[(half * 2 + side) * 4 + i],
-                    )
-                )
+    half = pieces[0].shape[0]
+    copies = [pltpu.make_async_copy(mine_hbm, mine_ref, sem.at[2])]
+    for side, place in enumerate((a, 1 - a)):
+        at = pl.multiple_of(place * half, 8)
+        copies.append(
+            pltpu.make_async_copy(pieces[side], src_ref.at[pl.ds(at, half)], sem.at[side])
+        )
     for copy in copies:
         copy.start()
     for copy in copies:
@@ -158,8 +120,8 @@
 
 
 def tile(row_pieces, mine):
-    size, width = row_pieces[0].shape[1:]
-    rows, cols = 2 * NY * size, 2 * mine.shape[0]
+    width = mine.shape[1]
+    rows, cols = 2 * row_pieces[0].shape[0], 2 * mine.shape[0]
     part = jax.ShapeDtypeStruct((rows, width), jnp.bfloat16)
     src_block, high, mid, low, left_sq, cost = pl.pallas_call(
         mine_kernel,
@@ -171,12 +133,12 @@
             jax.ShapeDtypeStruct((rows, 1), jnp.float32),
             jax.ShapeDtypeStruct((rows, cols), jnp.float32),
         ),
-        in_specs=[IN_HBM] * 5,
+        in_specs=[IN_HBM] * 3,
         out_specs=(IN_HBM,) + (WHOLE,) * 5,
         scratch_shapes=[
             pltpu.VMEM((rows, width), jnp.float32),
             pltpu.VMEM(mine.shape, jnp.float32),
-            pltpu.SemaphoreType.DMA((2 * NY + 1,)),
+            pltpu.SemaphoreType.DMA((3,)),
             pltpu.SemaphoreType.DMA,
         ],
         compiler_params=pltpu.CompilerParams(vmem_limit_bytes=VMEM_LIMIT),
@@ -236,23 +198,23 @@
     sent_ref[...] = pull(half_of(high_ref, mid_ref, place), src_ref, tgt_ref[...])
 
 
+def part_in_two(values, place, sent_ref, own_ref, part_ref):
+    half = own_ref.shape[0]
+    part_ref[...] = values
+    own_ref[...] = part_ref[pl.ds(pl.multiple_of(place * half, 8), half), :]
+    sent_ref[...] = part_ref[pl.ds(pl.multiple_of((1 - place) * half, 8), half), :]
+
+
 def push_kernel(high_ref, mid_ref, src_ref, mine_ref, other_ref, *out_refs):
-    sent_refs, own_refs, part_ref = out_refs[:2], out_refs[2:4], out_refs[4]
-    x, y, c = (lax.axis_index(name) for name in ("x", "y", "c"))
-    a = x // 2
+    c = lax.axis_index("c")
+    a = lax.axis_index("x") // 2
     ones = jnp.ones((mine_ref.shape[0], LANES), jnp.bfloat16)
     pushed, mass = 0.0, 0.0
     for place, ref in ((c, mine_ref), (1 - c, other_ref)):
         weight_parts = half_of(high_ref, mid_ref, place)
         pushed += three_products(weight_parts, parts_of(ref[...]), (1, 0))
         mass += sum(product(part, ones, (1, 0)) for part in weight_parts)
-    part_ref[...] = mass[:, :1] * src_ref[...] - pushed
-    size = own_refs[0].shape[1]
-    for half, group in enumerate((SEND_FIRST, SEND_LAST)):
-        for i, k in enumerate(group):
-            for ref, place in ((own_refs[half], a), (sent_refs[half], 1 - a)):
-                at = pl.multiple_of(((y + k) % NY * 2 + place) * size, 8)
-                ref[i] = part_ref[pl.ds(at, size), :]
+    part_in_two(mass[:, :1] * src_ref[...] - pushed, a, *out_refs)
 
 
 def keep_kernel(high_ref, mid_ref, src_ref, mine_ref, came_ref, out_ref):
@@ -294,10 +256,12 @@
     a = x // 2
     b = (x // 2) ^ (x % 2)
     total_points = rows * NZ * NX * NY * NC
-    mine = gather_blocks(tgt_emb, ("z", "x"), SIDE_GROUPS)
-    row_pieces = gather_ring(src_emb)
-    mine, *row_pieces[1:3] = lax.optimization_barrier((mine, *row_pieces[1:3]))
-    src_block, other, cost = tile(row_pieces, mine)
+    side = lax.all_gather(tgt_emb, "z", axis=0, tiled=True)
+    flip = lax.ppermute(side, "x", FLIP_B)
+    near = lax.all_gather(src_emb, "y", axis=0, tiled=True)
+    far = lax.ppermute(near, "x", FLIP_A)
+    mine = jnp.where(b == 0, jnp.concatenate([side, flip]), jnp.concatenate([flip, side]))
+    src_block, other, cost = tile((near, far), mine)
     tile_rows, tile_cols = cost.shape
     tgt_pot = jnp.zeros((tile_cols,), jnp.float32)
     log_total = math.log(total_points)
@@ -323,16 +287,18 @@
         compiler_params=pltpu.CompilerParams(vmem_limit_bytes=VMEM_LIMIT),
     )(src_pot, tgt_pot, cost, src_block, other)
     came = lax.ppermute(sent, "c", SWAP)
-    four = jax.ShapeDtypeStruct((4, rows, width), jnp.float32)
+    quarter = jax.ShapeDtypeStruct(near.shape, jnp.float32)
     scratch = [pltpu.VMEM(src_block.shape, jnp.float32)]
-    src_parts = on_tile(push_kernel, (four,) * 4, scratch, high, mid, src_block, mine, other)
-    src_parts = list(src_parts)
-    came, src_parts[0] = lax.optimization_barrier((came, src_parts[0]))
+    there, here = on_tile(
+        push_kernel, (quarter, quarter), scratch, high, mid, src_block, mine, other
+    )
+    came, here = lax.optimization_barrier((came, here))
+    here = here + lax.ppermute(there, "x", FLIP_A)
+    src_sum = lax.psum_scatter(here, "y", scatter_dimension=0, tiled=True)
     tgt_half = on_tile(keep_kernel, half, [], high, mid, src_block, mine, came)
     tgt_sum = scatter_blocks(tgt_half, ("z", "x"), SIDE_GROUPS)
-    src_sum = scatter_ring(src_parts[:2], src_parts[2:])
-    src_piece = take(src_pot.reshape(-1, rows), y * 2 + a)
-    tgt_piece = take(tgt_pot.reshape(-1, rows), (c * NZ + z) * 2 + b)
+    src_piece = take(src_pot.reshape(-1, rows), a * NY + y)
+    tgt_piece = take(tgt_pot.reshape(-1, rows), (c * 2 + b) * NZ + z)
     return src_piece, tgt_piece, src_sum / total_points, tgt_sum / total_points
 
 

time: 256 us -> 287 us (1.12)
  the two profiles are of different devices: /device:TPU:64 before, /device:TPU:56 now
where the time goes in v6:
time: 287 us; the launch traced here: 285 us
  blocking collectives  146 us (51%)
  waiting for transfers between devices  70.5 us (25%)
  Pallas kernels  19.9 us (7%)
  starting transfers between devices  18.3 us (6%)
  between operations  14.4 us (5%)
  other arithmetic  10.9 us (4%)
  local copies, waits for them, and re-layouts  4.57 us (2%)
    all_to_all x6, blocking collectives, all_to_all(): lax.all_to_all(blocks, axes, split_axis=0, concat_axis=0, axis_index_grou...  88.1 us
    reduce_scatter x1, waiting for transfers between devices, per_device(): src_sum = lax.psum_scatter(here, 'y', scatter_dimension=0, tiled=True)  33.7 us
    all_gather x1, blocking collectives, per_device(): side = lax.all_gather(tgt_emb, 'z', axis=0, tiled=True)  32.4 us
    all_gather x1, blocking collectives, per_device(): near = lax.all_gather(src_emb, 'y', axis=0, tiled=True)  25.8 us
    ppermute x1, waiting for transfers between devices, per_device(): here = here + lax.ppermute(there, 'x', FLIP_A)  17.9 us
    ppermute x1, waiting for transfers between devices, per_device(): far = lax.ppermute(near, 'x', FLIP_A)  9.5 us
    ppermute x1, waiting for transfers between devices, per_device(): flip = lax.ppermute(side, 'x', FLIP_B)  9.41 us
    pallas_call x2, Pallas kernels, on_tile(): pl.pallas_call(kernel, out_shape=out_shape, in_specs=[WHOLE] * len(args),...  7.7 us
  transfers between devices with their start and end apart: 7, of which 4 were waited for; matrix products, arithmetic and copies ran while one was open for 1% of the time, Pallas kernels for 3%

profile of v6, /device:TPU:56, one launch (start us, length us, event | category | flops | bytes accessed | tf_op | source)
XLA Modules:
  0.0 284.8 jit_solution(15246692368639176287)
XLA Ops:
  7.2 32.4 %all_gather.7 = f32[320,512]{1,0:T(8,128)S(1)} all-gather(f32[40,512]{1,0:T(8,128)} %param.3), channel_id=1, replica_groups=mesh['z'=8,'x'=4,'y'=8,'c'=2] {'z'}, dimensions={0}, use_global_device_ids=true | all-gather | bytes 737280 | tf_op jit(solution)/shard_map/all_gather | solution.py:259
  39.6 3.4 %collective-permute-start.1 = (f32[320,512]{1,0:T(8,128)S(1)}, f32[320,512]{1,0:T(8,128)S(1)}, u32[]{:S(2)}, u32[]{:S(2)}) collective-permute-start(f32[320,512]{1,0:T(8,128)S(1)} %all_gather.7), channel_id=1, source_target_pairs={{0,16},{16,0},{32,48},{48,32},{1,17},{17,1},{33,49},{49,33},{2,18}... | collective-permute-start | bytes 1966088 | tf_op jit(solution)/shard_map/ppermute | solution.py:260
  43.0 9.4 %collective-permute-done.1 = f32[320,512]{1,0:T(8,128)S(1)} collective-permute-done((f32[320,512]{1,0:T(8,128)S(1)}, f32[320,512]{1,0:T(8,128)S(1)}, u32[]{:S(2)}, u32[]{:S(2)}) %collective-permute-start.1) | collective-permute-done | bytes 655392 | tf_op jit(solution)/shard_map/ppermute | solution.py:260
  52.6 1.9 collective-permute-start.2
  54.5 25.8 %all_gather.6.refs_0_ = f32[320,512]{1,0:T(8,128)S(1)} all-gather(f32[40,512]{1,0:T(8,128)S(1)} %copy-done.7), channel_id=1, replica_groups=mesh['z'=8,'x'=4,'y'=8,'c'=2] {'y'}, dimensions={0}, use_global_device_ids=true | all-gather | bytes 737280 | tf_op jit(solution)/shard_map/all_gather | solution.py:261
  80.3 4.7 %collective-permute-start = (f32[320,512]{1,0:T(8,128)S(1)}, f32[320,512]{1,0:T(8,128)S(1)}, u32[]{:S(2)}, u32[]{:S(2)}) collective-permute-start(f32[320,512]{1,0:T(8,128)S(1)} %all_gather.6.refs_0_), channel_id=1, source_target_pairs={{0,48},{16,32},{32,16},{48,0},{1,49},{17,33},{33,17},{49,1},{2,50}... | collective-permute-start | bytes 1966088 | tf_op jit(solution)/shard_map/ppermute | solution.py:262
  85.0 9.5 %collective-permute-done.refs_1_ = f32[320,512]{1,0:T(8,128)S(1)} collective-permute-done((f32[320,512]{1,0:T(8,128)S(1)}, f32[320,512]{1,0:T(8,128)S(1)}, u32[]{:S(2)}, u32[]{:S(2)}) %collective-permute-start) | collective-permute-done | bytes 655392 | tf_op jit(solution)/shard_map/ppermute | solution.py:262
  94.5 4.6 %shard_map.57 = (f32[640,512]{1,0:T(8,128)S(1)}, bf16[640,512]{1,0:T(8,128)(2,1)S(1)}, bf16[640,512]{1,0:T(8,128)(2,1)S(1)}, bf16[640,512]{1,0:T(8,128)(2,1)S(1)...) custom-call(f32[320,512]{1,0:T(8,128)S(1)} %all_gather.6.refs_0_, f32[320,512]{1,0:T(8,128)S(1)} %collective-permute-done.refs_1_, ...), custom_call_target="tpu_custom_call" | custom-call | tf_op jit(solution)/shard_map/pallas_call | solution.py:126
  100.2 4.0 %shard_map.58.cost_ref = f32[640,1280]{1,0:T(8,128)S(1)} custom-call(bf16[640,512]{1,0:T(8,128)(2,1)S(1)} %get-tuple-element.17.high_ref, bf16[640,512]{1,0:T(8,128)(2,1)S(1)} %get-tuple-element.18.mid_ref, bf16[640,512]{1,0:T(8,128)(2,1)S(1)} %get-tuple-element.19.low_ref, f32[640,1]{1,0:T(8,128)S(1)} %get-tuple-element.20.sq_ref, ...), custom_call_target="tpu_custom_call", output_to_operand_aliasing={{}: (5, {})} | custom-call | tf_op jit(solution)/shard_map/pallas_call | solution.py:147
  105.3 16.8 %all_to_all.35 = f32[16,5,128]{2,1,0:T(8,128)S(1)} all-to-all(f32[16,5,128]{2,1,0:T(8,128)S(1)} %broadcast_in_dim.12), channel_id=1, replica_groups={{0,2,4,6,8,10,12,14,48,50,52,54,56,58,60,62},{16,18,20,22,24,26,28,30,3..., dimensions={0} | all-to-all | bytes 81920 | tf_op jit(solution)/shard_map/all_to_all | solution.py:39
  123.4 16.1 %all_to_all.36 = f32[32,10,128]{2,1,0:T(8,128)S(1)} all-to-all(f32[32,10,128]{2,1,0:T(8,128)S(1)} %broadcast_in_dim.13), channel_id=1, replica_groups={{0,1,16,17,64,65,80,81,128,129,144,145,192,193,208,209,256,257,272,273,..., dimensions={0} | all-to-all | bytes 327680 | tf_op jit(solution)/shard_map/all_to_all | solution.py:39
  140.8 12.5 %all_to_all.37 = f32[16,5,128]{2,1,0:T(8,128)S(1)} all-to-all(f32[16,5,128]{2,1,0:T(8,128)S(1)} %broadcast_in_dim.14), channel_id=1, replica_groups={{0,2,4,6,8,10,12,14,48,50,52,54,56,58,60,62},{16,18,20,22,24,26,28,30,3..., dimensions={0} | all-to-all | bytes 81920 | tf_op jit(solution)/shard_map/all_to_all | solution.py:39
  154.6 15.2 %all_to_all.38 = f32[32,10,128]{2,1,0:T(8,128)S(1)} all-to-all(f32[32,10,128]{2,1,0:T(8,128)S(1)} %broadcast_in_dim.15), channel_id=1, replica_groups={{0,1,16,17,64,65,80,81,128,129,144,145,192,193,208,209,256,257,272,273,..., dimensions={0} | all-to-all | bytes 327680 | tf_op jit(solution)/shard_map/all_to_all | solution.py:39
  171.1 12.2 %all_to_all.39 = f32[16,5,128]{2,1,0:T(8,128)S(1)} all-to-all(f32[16,5,128]{2,1,0:T(8,128)S(1)} %broadcast_in_dim.16), channel_id=1, replica_groups={{0,2,4,6,8,10,12,14,48,50,52,54,56,58,60,62},{16,18,20,22,24,26,28,30,3..., dimensions={0} | all-to-all | bytes 81920 | tf_op jit(solution)/shard_map/all_to_all | solution.py:39
  184.6 15.2 %all_to_all.40 = f32[32,10,128]{2,1,0:T(8,128)S(1)} all-to-all(f32[32,10,128]{2,1,0:T(8,128)S(1)} %broadcast_in_dim.17), channel_id=1, replica_groups={{0,1,16,17,64,65,80,81,128,129,144,145,192,193,208,209,256,257,272,273,..., dimensions={0} | all-to-all | bytes 327680 | tf_op jit(solution)/shard_map/all_to_all | solution.py:39
  202.7 3.7 %shard_map.59 = (f32[640,512]{1,0:T(8,128)S(1)}, bf16[640,1280]{1,0:T(8,128)(2,1)S(1)}, bf16[640,1280]{1,0:T(8,128)(2,1)S(1)}) custom-call(f32[5,128]{1,0:T(8,128)S(1)} %add_multiply_fusion.1.src_pot_ref, f32[10,128]{1,0:T(8,128)S(1)} %add_multiply_fusion.tgt_pot_ref, f32[640,1280]{1,0:T(8,128)S(1)} %shard_map.58.cost_ref, f32[640,512]{1,0:T(8,128)S(1)} %copy-done.6, ...), custom_call_target="tpu_custom_call" | custom-call | tf_op jit(solution)/shard_map/pallas_call | solution.py:277
  206.4 2.1 collective-permute-start.3
  208.5 4.3 %shard_map.60 = (f32[320,512]{1,0:T(8,128)S(1)}, f32[320,512]{1,0:T(8,128)S(1)}) custom-call(bf16[640,1280]{1,0:T(8,128)(2,1)S(1)} %get-tuple-element.24.high_ref, bf16[640,1280]{1,0:T(8,128)(2,1)S(1)} %get-tuple-element.25.mid_ref, f32[640,512]{1,0:T(8,128)S(1)} %copy-done.6, f32[640,512]{1,0:T(8,128)S(1)} %copy-done.1, f32[640,512]{1,0:T(8,128)S(1)} %copy-done.4), custom_call_target="tpu_custom_call" | custom-call | tf_op jit(solution)/shard_map/pallas_call | solution.py:227
  212.9 3.4 %shard_map.61 = f32[640,512]{1,0:T(8,128)} custom-call(bf16[640,1280]{1,0:T(8,128)(2,1)S(1)} %get-tuple-element.24.high_ref, bf16[640,1280]{1,0:T(8,128)(2,1)S(1)} %get-tuple-element.25.mid_ref, f32[640,512]{1,0:T(8,128)S(1)} %copy-done.6, f32[640,512]{1,0:T(8,128)S(1)} %copy-done.1, f32[640,512]{1,0:T(8,128)S(1)} %collective-permute-done.3.came_ref), custom_call_target="tpu_custom_call" | custom-call | tf_op jit(solution)/shard_map/pallas_call | solution.py:227
  216.3 3.7 %all-to-all-start.6 = ((f32[16,40,512]{2,1,0:T(8,128)}), f32[16,40,512]{2,1,0:T(8,128)S(1)}, u32[]{:S(2)}, u32[]{:S(2)}) async-start(f32[16,40,512]{2,1,0:T(8,128)} %bitcast.13), calls=%async_computation.7 | async-start | bytes 2621440 | tf_op jit(solution)/shard_map/all_to_all | solution.py:39
  220.0 2.4 collective-permute-start.4
  222.4 17.9 %collective-permute-done.4 = f32[320,512]{1,0:T(8,128)S(1)} collective-permute-done((f32[320,512]{1,0:T(8,128)S(1)}, f32[320,512]{1,0:T(8,128)S(1)}, u32[]{:S(2)}, u32[]{:S(2)}) %collective-permute-start.4) | collective-permute-done | bytes 655392 | tf_op jit(solution)/shard_map/ppermute | solution.py:296
  242.0 33.7 %reduce-scatter.2.cloned.1.call-done = f32[40,512]{1,0:T(8,128)} async-done(((f32[320,512]{1,0:T(8,128)}), f32[40,512]{1,0:T(8,128)}) %reduce-scatter.2.cloned.1.call-update) | async-done | bytes 81936 | tf_op jit(solution)/shard_map/reduce_scatter | solution.py:297
  275.7 1.5 broadcast_multiply_fusion.1
  (70 shorter events, 14.0 us)
Async XLA Ops:
  7.2 47.3 %copy-start.7 = (f32[40,512]{1,0:T(8,128)S(1)}, f32[40,512]{1,0:T(8,128)}, u32[]{:S(2)}) copy-start(f32[40,512]{1,0:T(8,128)} %param.2) | copy-start | bytes 245764
  39.6 12.8 %collective-permute-start.1 = (f32[320,512]{1,0:T(8,128)S(1)}, f32[320,512]{1,0:T(8,128)S(1)}, u32[]{:S(2)}, u32[]{:S(2)}) collective-permute-start(f32[320,512]{1,0:T(8,128)S(1)} %all_gather.7), channel_id=1, source_target_pairs={{0,16},{16,0},{32,48},{48,32},{1,17},{17,1},{33,49},{49,33},{2,18}... | collective-permute-start | bytes 1966088 | tf_op jit(solution)/shard_map/ppermute | solution.py:260
  52.6 47.6 %copy-start = (f32[640,512]{1,0:T(8,128)}, f32[640,512]{1,0:T(8,128)S(1)}, u32[]{:S(2)}) copy-start(f32[640,512]{1,0:T(8,128)S(1)} %maximum_select_fusion.refs_2_.mine_ref) | copy-start | bytes 3932164
  52.6 47.6 %collective-permute-start.2 = (f32[640,512]{1,0:T(8,128)S(1)}, f32[640,512]{1,0:T(8,128)S(1)}, u32[]{:S(2)}, u32[]{:S(2)}) collective-permute-start(f32[640,512]{1,0:T(8,128)S(1)} %maximum_select_fusion.refs_2_.mine_ref), channel_id=1, source_target_pairs={{0,1},{1,0},{2,3},{3,2},{4,5},{5,4},{6,7},{7,6},{8,9},{9,8},{10,11... | collective-permute-start | bytes 3932168 | tf_op jit(solution)/shard_map/ppermute | solution.py:146
  80.3 14.2 %collective-permute-start = (f32[320,512]{1,0:T(8,128)S(1)}, f32[320,512]{1,0:T(8,128)S(1)}, u32[]{:S(2)}, u32[]{:S(2)}) collective-permute-start(f32[320,512]{1,0:T(8,128)S(1)} %all_gather.6.refs_0_), channel_id=1, source_target_pairs={{0,48},{16,32},{32,16},{48,0},{1,49},{17,33},{33,17},{49,1},{2,50}... | collective-permute-start | bytes 1966088 | tf_op jit(solution)/shard_map/ppermute | solution.py:262
  99.1 1.1 copy-start.5
  100.2 4.0 %copy-start.2 = (f32[640,512]{1,0:T(8,128)}, f32[640,512]{1,0:T(8,128)S(1)}, u32[]{:S(2)}) copy-start(f32[640,512]{1,0:T(8,128)S(1)} %collective-permute-done.2.other_ref.other_hbm) | copy-start | bytes 3932164
  199.9 8.6 %copy-start.1 = (f32[640,512]{1,0:T(8,128)S(1)}, f32[640,512]{1,0:T(8,128)}, u32[]{:S(2)}) copy-start(f32[640,512]{1,0:T(8,128)} %copy-done) | copy-start | bytes 3932164
  200.0 1.4 copy-start.3
  201.4 1.3 copy-start.6
  202.7 5.8 %copy-start.4 = (f32[640,512]{1,0:T(8,128)S(1)}, f32[640,512]{1,0:T(8,128)}, u32[]{:S(2)}) copy-start(f32[640,512]{1,0:T(8,128)} %copy-done.2) | copy-start | bytes 3932164
  206.4 6.5 %collective-permute-start.3 = (f32[640,512]{1,0:T(8,128)S(1)}, f32[640,512]{1,0:T(8,128)S(1)}, u32[]{:S(2)}, u32[]{:S(2)}) collective-permute-start(f32[640,512]{1,0:T(8,128)S(1)} %get-tuple-element.23), channel_id=1, source_target_pairs={{0,1},{1,0},{2,3},{3,2},{4,5},{5,4},{6,7},{7,6},{8,9},{9,8},{10,11... | collective-permute-start | bytes 3932168 | tf_op jit(solution)/shard_map/ppermute | solution.py:289
  216.3 61.0 %all-to-all-start.6 = ((f32[16,40,512]{2,1,0:T(8,128)}), f32[16,40,512]{2,1,0:T(8,128)S(1)}, u32[]{:S(2)}, u32[]{:S(2)}) async-start(f32[16,40,512]{2,1,0:T(8,128)} %bitcast.13), calls=%async_computation.7 | async-start | bytes 2621440 | tf_op jit(solution)/shard_map/all_to_all | solution.py:39
  220.0 55.7 %reduce-scatter.2.cloned.1.call-start = ((), (), s32[]{:S(2)}) async-start(), calls=%async_computation.8 | async-start | bytes 737280 | tf_op jit(solution)/shard_map/reduce_scatter | solution.py:297
  220.0 20.3 %collective-permute-start.4 = (f32[320,512]{1,0:T(8,128)S(1)}, f32[320,512]{1,0:T(8,128)S(1)}, u32[]{:S(2)}, u32[]{:S(2)}) collective-permute-start(f32[320,512]{1,0:T(8,128)S(1)} %get-tuple-element.28), channel_id=1, source_target_pairs={{0,48},{16,32},{32,16},{48,0},{1,49},{17,33},{33,17},{49,1},{2,50}... | collective-permute-start | bytes 1966088 | tf_op jit(solution)/shard_map/ppermute | solution.py:296
Sparse Core Ops, SparseCore 0:
  241.4 34.2 reduce-scatter.1

commit v7 on v6

--- a/solution.py
+++ b/solution.py
@@ -41,10 +41,24 @@
     )
 
 
+STEPS = (4, 3, 5, 2, 6, 1, 7)
 PASSES = ((0, 0), (0, 1), (1, 0), (1, 1), (0, 2), (2, 0))
 IN_HBM = pl.BlockSpec(memory_space=pltpu.HBM)
 WHOLE = pl.BlockSpec(memory_space=pltpu.VMEM)
 VMEM_LIMIT = 24 * 1024 * 1024
+
+
+def gather_blocks(shard, axes, groups):
+    blocks = jnp.broadcast_to(shard[None], (len(groups[0]),) + shard.shape)
+    return all_to_all(blocks, axes, groups).reshape(-1, shard.shape[1])
+
+
+def scatter_ring(pieces, a):
+    total = pieces[-1]
+    for k, piece in zip(STEPS, pieces):
+        moves = [(i, (i + k) % NY) for i in range(NY)]
+        total = total + lax.ppermute(piece, "y", moves)
+    return take(total, a) + lax.ppermute(take(total, 1 - a), "x", FLIP_A)
 
 
 def scatter_blocks(partial, axes, groups):
@@ -198,23 +212,21 @@
     sent_ref[...] = pull(half_of(high_ref, mid_ref, place), src_ref, tgt_ref[...])
 
 
-def part_in_two(values, place, sent_ref, own_ref, part_ref):
-    half = own_ref.shape[0]
-    part_ref[...] = values
-    own_ref[...] = part_ref[pl.ds(pl.multiple_of(place * half, 8), half), :]
-    sent_ref[...] = part_ref[pl.ds(pl.multiple_of((1 - place) * half, 8), half), :]
-
-
 def push_kernel(high_ref, mid_ref, src_ref, mine_ref, other_ref, *out_refs):
-    c = lax.axis_index("c")
-    a = lax.axis_index("x") // 2
+    out_refs, part_ref = out_refs[:-1], out_refs[-1]
+    y, c = lax.axis_index("y"), lax.axis_index("c")
     ones = jnp.ones((mine_ref.shape[0], LANES), jnp.bfloat16)
     pushed, mass = 0.0, 0.0
     for place, ref in ((c, mine_ref), (1 - c, other_ref)):
         weight_parts = half_of(high_ref, mid_ref, place)
         pushed += three_products(weight_parts, parts_of(ref[...]), (1, 0))
         mass += sum(product(part, ones, (1, 0)) for part in weight_parts)
-    part_in_two(mass[:, :1] * src_ref[...] - pushed, a, *out_refs)
+    part_ref[...] = mass[:, :1] * src_ref[...] - pushed
+    size = out_refs[0].shape[1]
+    for k, ref in zip(STEPS + (0,), out_refs):
+        for a in range(2):
+            at = pl.multiple_of((a * NY + (y + k) % NY) * size, 8)
+            ref[a] = part_ref[pl.ds(at, size), :]
 
 
 def keep_kernel(high_ref, mid_ref, src_ref, mine_ref, came_ref, out_ref):
@@ -256,11 +268,10 @@
     a = x // 2
     b = (x // 2) ^ (x % 2)
     total_points = rows * NZ * NX * NY * NC
-    side = lax.all_gather(tgt_emb, "z", axis=0, tiled=True)
-    flip = lax.ppermute(side, "x", FLIP_B)
+    mine = gather_blocks(tgt_emb, ("z", "x"), SIDE_GROUPS)
     near = lax.all_gather(src_emb, "y", axis=0, tiled=True)
     far = lax.ppermute(near, "x", FLIP_A)
-    mine = jnp.where(b == 0, jnp.concatenate([side, flip]), jnp.concatenate([flip, side]))
+    mine, far = lax.optimization_barrier((mine, far))
     src_block, other, cost = tile((near, far), mine)
     tile_rows, tile_cols = cost.shape
     tgt_pot = jnp.zeros((tile_cols,), jnp.float32)
@@ -287,16 +298,14 @@
         compiler_params=pltpu.CompilerParams(vmem_limit_bytes=VMEM_LIMIT),
     )(src_pot, tgt_pot, cost, src_block, other)
     came = lax.ppermute(sent, "c", SWAP)
-    quarter = jax.ShapeDtypeStruct(near.shape, jnp.float32)
+    pair = jax.ShapeDtypeStruct((2, rows, width), jnp.float32)
     scratch = [pltpu.VMEM(src_block.shape, jnp.float32)]
-    there, here = on_tile(
-        push_kernel, (quarter, quarter), scratch, high, mid, src_block, mine, other
-    )
-    came, here = lax.optimization_barrier((came, here))
-    here = here + lax.ppermute(there, "x", FLIP_A)
-    src_sum = lax.psum_scatter(here, "y", scatter_dimension=0, tiled=True)
+    pieces = on_tile(push_kernel, (pair,) * NY, scratch, high, mid, src_block, mine, other)
+    pieces = list(pieces)
+    came, pieces[0] = lax.optimization_barrier((came, pieces[0]))
     tgt_half = on_tile(keep_kernel, half, [], high, mid, src_block, mine, came)
     tgt_sum = scatter_blocks(tgt_half, ("z", "x"), SIDE_GROUPS)
+    src_sum = scatter_ring(pieces, a)
     src_piece = take(src_pot.reshape(-1, rows), a * NY + y)
     tgt_piece = take(tgt_pot.reshape(-1, rows), (c * 2 + b) * NZ + z)
     return src_piece, tgt_piece, src_sum / total_points, tgt_sum / total_points

time: 287 us -> 242 us (0.84)
  waiting for transfers between devices: 70.5 us -> 30 us
  starting transfers between devices: 18.3 us -> 50.4 us
  blocking collectives: 146 us -> 116 us
  between operations: 14.4 us -> 1.14 us
  local copies, waits for them, and re-layouts: 4.57 us -> 9.43 us
  Pallas kernels: 19.9 us -> 23.4 us
    reduce_scatter x1 -> x0, waiting for transfers between devices: 33.7 us -> none  [per_device(): src_sum = lax.psum_scatter(here, 'y', scatter_dimension=0, tiled=True)]
    all_gather x1 -> x0, blocking collectives: 32.4 us -> none  [per_device(): side = lax.all_gather(tgt_emb, 'z', axis=0, tiled=True)]
    ppermute x2 -> x8, starting transfers between devices: 5.8 us -> 27.2 us  [the longest x7 24.6 us: scatter_ring(): total = total + lax.ppermute(piece, 'y', moves)]
    all_to_all x1 -> x2, starting transfers between devices: 3.7 us -> 15.1 us  [all_to_all(): lax.all_to_all(blocks, axes, split_axis=0, concat_axis=0, axis_index_grou...]
    ppermute x2 -> x8, waiting for transfers between devices: 27.3 us -> 19.3 us  [the longest x7 14.9 us: scatter_ring(): total = total + lax.ppermute(piece, 'y', moves)]
    unnamed x16 -> x22, local copies, waits for them, and re-layouts: 3.81 us -> 6.49 us
  transfers between devices with their start and end apart: 7 -> 13, of which waited for: 4 -> 5; matrix products, arithmetic and copies ran while one was open for 1% -> 1% of each run, Pallas kernels for 3% -> 5%
where the time goes in v7:
time: 242 us; the launch traced here: 239 us
  blocking collectives  116 us (48%)
  starting transfers between devices  50.4 us (21%)
  waiting for transfers between devices  30 us (12%)
  Pallas kernels  23.4 us (10%)
  local copies, waits for them, and re-layouts  9.43 us (4%)
  other arithmetic  8.97 us (4%)
    all_to_all x6, blocking collectives, all_to_all(): lax.all_to_all(blocks, axes, split_axis=0, concat_axis=0, axis_index_grou...  90.3 us
    all_gather x1, blocking collectives, per_device(): near = lax.all_gather(src_emb, 'y', axis=0, tiled=True)  25.7 us
    ppermute x7, starting transfers between devices, scatter_ring(): total = total + lax.ppermute(piece, 'y', moves)  24.6 us
    all_to_all x2, starting transfers between devices, all_to_all(): lax.all_to_all(blocks, axes, split_axis=0, concat_axis=0, axis_index_grou...  15.1 us
    ppermute x7, waiting for transfers between devices, scatter_ring(): total = total + lax.ppermute(piece, 'y', moves)  14.9 us
    ppermute x1, waiting for transfers between devices, per_device(): far = lax.ppermute(near, 'x', FLIP_A)  10.7 us
    pallas_call x2, Pallas kernels, on_tile(): pl.pallas_call(kernel, out_shape=out_shape, in_specs=[WHOLE] * len(args),...  10.4 us
    unnamed x22, local copies, waits for them, and re-layouts  6.49 us
  transfers between devices with their start and end apart: 13, of which 5 were waited for; matrix products, arithmetic and copies ran while one was open for 1% of the time, Pallas kernels for 5%

profile of v7, /device:TPU:56, one launch (start us, length us, event | category | flops | bytes accessed | tf_op | source)
XLA Modules:
  0.0 239.4 jit_solution(7698219923854813730)
XLA Ops:
  2.8 11.4 %all-to-all-start = ((f32[16,40,512]{2,1,0:T(8,128)}), f32[16,40,512]{2,1,0:T(8,128)}, u32[]{:S(2)}, u32[]{:S(2)}) async-start(f32[16,40,512]{2,1,0:T(8,128)} %broadcast_in_dim.14), calls=%async_computation | async-start | bytes 2621440 | tf_op jit(solution)/shard_map/all_to_all | solution.py:39
  14.2 25.7 %all_gather.3.refs_0_ = f32[320,512]{1,0:T(8,128)S(1)} all-gather(f32[40,512]{1,0:T(8,128)S(1)} %copy-done.10), channel_id=1, replica_groups=mesh['z'=8,'x'=4,'y'=8,'c'=2] {'y'}, dimensions={0}, use_global_device_ids=true | all-gather | bytes 737280 | tf_op jit(solution)/shard_map/all_gather | solution.py:272
  39.9 4.0 %collective-permute-start = (f32[320,512]{1,0:T(8,128)S(1)}, f32[320,512]{1,0:T(8,128)S(1)}, u32[]{:S(2)}, u32[]{:S(2)}) collective-permute-start(f32[320,512]{1,0:T(8,128)S(1)} %all_gather.3.refs_0_), channel_id=1, source_target_pairs={{0,48},{16,32},{32,16},{48,0},{1,49},{17,33},{33,17},{49,1},{2,50}... | collective-permute-start | bytes 1966088 | tf_op jit(solution)/shard_map/ppermute | solution.py:273
  44.8 10.7 %collective-permute-done.refs_1_ = f32[320,512]{1,0:T(8,128)S(1)} collective-permute-done((f32[320,512]{1,0:T(8,128)S(1)}, f32[320,512]{1,0:T(8,128)S(1)}, u32[]{:S(2)}, u32[]{:S(2)}) %collective-permute-start) | collective-permute-done | bytes 655392 | tf_op jit(solution)/shard_map/ppermute | solution.py:273
  60.4 5.4 %shard_map.57 = (f32[640,512]{1,0:T(8,128)S(1)}, bf16[640,512]{1,0:T(8,128)(2,1)S(1)}, bf16[640,512]{1,0:T(8,128)(2,1)S(1)}, bf16[640,512]{1,0:T(8,128)(2,1)S(1)...) custom-call(f32[320,512]{1,0:T(8,128)S(1)} %copy-done.7, f32[320,512]{1,0:T(8,128)S(1)} %copy-done.9, ...), custom_call_target="tpu_custom_call" | custom-call | tf_op jit(solution)/shard_map/pallas_call | solution.py:140
  65.9 4.0 %shard_map.58.cost_ref = f32[640,1280]{1,0:T(8,128)S(1)} custom-call(bf16[640,512]{1,0:T(8,128)(2,1)S(1)} %get-tuple-element.27.high_ref, bf16[640,512]{1,0:T(8,128)(2,1)S(1)} %get-tuple-element.28.mid_ref, bf16[640,512]{1,0:T(8,128)(2,1)S(1)} %get-tuple-element.29.low_ref, f32[640,1]{1,0:T(8,128)S(1)} %get-tuple-element.30.sq_ref, ...), custom_call_target="tpu_custom_call", output_to_operand_aliasing={{}: (5, {})} | custom-call | tf_op jit(solution)/shard_map/pallas_call | solution.py:161
  71.1 15.6 %all_to_all.40 = f32[16,5,128]{2,1,0:T(8,128)S(1)} all-to-all(f32[16,5,128]{2,1,0:T(8,128)S(1)} %broadcast_in_dim.15), channel_id=1, replica_groups={{0,2,4,6,8,10,12,14,48,50,52,54,56,58,60,62},{16,18,20,22,24,26,28,30,3..., dimensions={0} | all-to-all | bytes 81920 | tf_op jit(solution)/shard_map/all_to_all | solution.py:39
  87.9 19.5 %all_to_all.41 = f32[32,10,128]{2,1,0:T(8,128)S(1)} all-to-all(f32[32,10,128]{2,1,0:T(8,128)S(1)} %broadcast_in_dim.16), channel_id=1, replica_groups={{0,1,16,17,64,65,80,81,128,129,144,145,192,193,208,209,256,257,272,273,..., dimensions={0} | all-to-all | bytes 327680 | tf_op jit(solution)/shard_map/all_to_all | solution.py:39
  108.8 12.5 %all_to_all.42 = f32[16,5,128]{2,1,0:T(8,128)S(1)} all-to-all(f32[16,5,128]{2,1,0:T(8,128)S(1)} %broadcast_in_dim.17), channel_id=1, replica_groups={{0,2,4,6,8,10,12,14,48,50,52,54,56,58,60,62},{16,18,20,22,24,26,28,30,3..., dimensions={0} | all-to-all | bytes 81920 | tf_op jit(solution)/shard_map/all_to_all | solution.py:39
  122.5 15.2 %all_to_all.43 = f32[32,10,128]{2,1,0:T(8,128)S(1)} all-to-all(f32[32,10,128]{2,1,0:T(8,128)S(1)} %broadcast_in_dim.18), channel_id=1, replica_groups={{0,1,16,17,64,65,80,81,128,129,144,145,192,193,208,209,256,257,272,273,..., dimensions={0} | all-to-all | bytes 327680 | tf_op jit(solution)/shard_map/all_to_all | solution.py:39
  139.1 12.2 %all_to_all.44 = f32[16,5,128]{2,1,0:T(8,128)S(1)} all-to-all(f32[16,5,128]{2,1,0:T(8,128)S(1)} %broadcast_in_dim.19), channel_id=1, replica_groups={{0,2,4,6,8,10,12,14,48,50,52,54,56,58,60,62},{16,18,20,22,24,26,28,30,3..., dimensions={0} | all-to-all | bytes 81920 | tf_op jit(solution)/shard_map/all_to_all | solution.py:39
  152.6 15.2 %all_to_all.45 = f32[32,10,128]{2,1,0:T(8,128)S(1)} all-to-all(f32[32,10,128]{2,1,0:T(8,128)S(1)} %broadcast_in_dim.20), channel_id=1, replica_groups={{0,1,16,17,64,65,80,81,128,129,144,145,192,193,208,209,256,257,272,273,..., dimensions={0} | all-to-all | bytes 327680 | tf_op jit(solution)/shard_map/all_to_all | solution.py:39
  170.6 3.7 %shard_map.59 = (f32[640,512]{1,0:T(8,128)S(1)}, bf16[640,1280]{1,0:T(8,128)(2,1)S(1)}, bf16[640,1280]{1,0:T(8,128)(2,1)S(1)}) custom-call(f32[5,128]{1,0:T(8,128)S(1)} %add_multiply_fusion.1.src_pot_ref, f32[10,128]{1,0:T(8,128)S(1)} %add_multiply_fusion.tgt_pot_ref, f32[640,1280]{1,0:T(8,128)S(1)} %shard_map.58.cost_ref, f32[640,512]{1,0:T(8,128)S(1)} %copy-done.4, ...), custom_call_target="tpu_custom_call" | custom-call | tf_op jit(solution)/shard_map/pallas_call | solution.py:288
  176.4 5.7 %shard_map.60 = (f32[2,40,512]{2,1,0:T(8,128)S(1)}, f32[2,40,512]{2,1,0:T(8,128)S(1)}, f32[2,40,512]{2,1,0:T(8,128)S(1)}, f32[2,40,512]{2,1,0:T(8,128)S(1)}, f32...) custom-call(bf16[640,1280]{1,0:T(8,128)(2,1)S(1)} %get-tuple-element., ...), custom_call_target="tpu_custom_call" | custom-call | tf_op jit(solution)/shard_map/pallas_call | solution.py:239
  182.1 4.7 %shard_map.61 = f32[640,512]{1,0:T(8,128)} custom-call(bf16[640,1280]{1,0:T(8,128)(2,1)S(1)} %get-tuple-element.33.high_ref, bf16[640,1280]{1,0:T(8,128)(2,1)S(1)} %get-tuple-element.34.mid_ref, f32[640,512]{1,0:T(8,128)S(1)} %copy-done.5, f32[640,512]{1,0:T(8,128)} %bitcast.refs_2_.mine_ref, f32[640,512]{1,0:T(8,128)S(1)} %collective-permute-done.2.came_ref), custom_call_target="tpu_custom_call" | custom-call | tf_op jit(solution)/shard_map/pallas_call | solution.py:239
  186.8 3.7 %all-to-all-start.7 = ((f32[16,40,512]{2,1,0:T(8,128)}), f32[16,40,512]{2,1,0:T(8,128)S(1)}, u32[]{:S(2)}, u32[]{:S(2)}) async-start(f32[16,40,512]{2,1,0:T(8,128)} %bitcast.16), calls=%async_computation.7 | async-start | bytes 2621440 | tf_op jit(solution)/shard_map/all_to_all | solution.py:39
  190.5 4.4 %collective-permute-start.4 = (f32[2,40,512]{2,1,0:T(8,128)S(1)}, f32[2,40,512]{2,1,0:T(8,128)S(1)}, u32[]{:S(2)}, u32[]{:S(2)}) collective-permute-start(f32[2,40,512]{2,1,0:T(8,128)S(1)} %get-tuple-element.39), channel_id=1, source_target_pairs={{0,6},{2,8},{4,10},{6,12},{8,14},{10,0},{12,2},{14,4},{1,7},{3,9},... | collective-permute-start | bytes 491528 | tf_op jit(solution)/shard_map/ppermute | solution.py:60
  194.9 3.3 %collective-permute-start.5 = (f32[2,40,512]{2,1,0:T(8,128)S(1)}, f32[2,40,512]{2,1,0:T(8,128)S(1)}, u32[]{:S(2)}, u32[]{:S(2)}) collective-permute-start(f32[2,40,512]{2,1,0:T(8,128)S(1)} %get-tuple-element.40), channel_id=1, source_target_pairs={{0,10},{2,12},{4,14},{6,0},{8,2},{10,4},{12,6},{14,8},{1,11},{3,13... | collective-permute-start | bytes 491528 | tf_op jit(solution)/shard_map/ppermute | solution.py:60
  198.2 5.6 %collective-permute-start.6 = (f32[2,40,512]{2,1,0:T(8,128)S(1)}, f32[2,40,512]{2,1,0:T(8,128)S(1)}, u32[]{:S(2)}, u32[]{:S(2)}) collective-permute-start(f32[2,40,512]{2,1,0:T(8,128)S(1)} %get-tuple-element.41), channel_id=1, source_target_pairs={{0,4},{2,6},{4,8},{6,10},{8,12},{10,14},{12,0},{14,2},{1,5},{3,7},... | collective-permute-start | bytes 491528 | tf_op jit(solution)/shard_map/ppermute | solution.py:60
  205.7 5.6 %collective-permute-start.8 = (f32[2,40,512]{2,1,0:T(8,128)S(1)}, f32[2,40,512]{2,1,0:T(8,128)S(1)}, u32[]{:S(2)}, u32[]{:S(2)}) collective-permute-start(f32[2,40,512]{2,1,0:T(8,128)S(1)} %get-tuple-element.43), channel_id=1, source_target_pairs={{0,2},{2,4},{4,6},{6,8},{8,10},{10,12},{12,14},{14,0},{1,3},{3,5},... | collective-permute-start | bytes 491528 | tf_op jit(solution)/shard_map/ppermute | solution.py:60
  217.0 3.4 %collective-permute-done.7 = f32[2,40,512]{2,1,0:T(8,128)S(1)} collective-permute-done((f32[2,40,512]{2,1,0:T(8,128)S(1)}, f32[2,40,512]{2,1,0:T(8,128)S(1)}, u32[]{:S(2)}, u32[]{:S(2)}) %collective-permute-start.7) | collective-permute-done | bytes 163872 | tf_op jit(solution)/shard_map/ppermute | solution.py:60
  220.3 10.0 %collective-permute-done.9 = f32[2,40,512]{2,1,0:T(8,128)S(1)} collective-permute-done((f32[2,40,512]{2,1,0:T(8,128)S(1)}, f32[2,40,512]{2,1,0:T(8,128)S(1)}, u32[]{:S(2)}, u32[]{:S(2)}) %collective-permute-start.9) | collective-permute-done | bytes 163872 | tf_op jit(solution)/shard_map/ppermute | solution.py:60
  230.5 2.6 %collective-permute-start.10 = (f32[40,512]{1,0:T(8,128)S(1)}, f32[40,512]{1,0:T(8,128)S(1)}, u32[]{:S(2)}, u32[]{:S(2)}) collective-permute-start(f32[40,512]{1,0:T(8,128)S(1)} %dynamic-slice_bitcast_fusion), channel_id=1, source_target_pairs={{0,48},{16,32},{32,16},{48,0},{1,49},{17,33},{33,17},{49,1},{2,50}... | collective-permute-start | bytes 245768 | tf_op jit(solution)/shard_map/ppermute | solution.py:61
  233.6 4.4 %collective-permute-done.10 = f32[40,512]{1,0:T(8,128)S(1)} collective-permute-done((f32[40,512]{1,0:T(8,128)S(1)}, f32[40,512]{1,0:T(8,128)S(1)}, u32[]{:S(2)}, u32[]{:S(2)}) %collective-permute-start.10) | collective-permute-done | bytes 81952 | tf_op jit(solution)/shard_map/ppermute | solution.py:61
  (87 shorter events, 29.7 us)
Async XLA Ops:
  0.6 13.6 %copy-start.10 = (f32[40,512]{1,0:T(8,128)S(1)}, f32[40,512]{1,0:T(8,128)}, u32[]{:S(2)}) copy-start(f32[40,512]{1,0:T(8,128)} %param.2) | copy-start | bytes 245764
  2.8 53.5 %all-to-all-start = ((f32[16,40,512]{2,1,0:T(8,128)}), f32[16,40,512]{2,1,0:T(8,128)}, u32[]{:S(2)}, u32[]{:S(2)}) async-start(f32[16,40,512]{2,1,0:T(8,128)} %broadcast_in_dim.14), calls=%async_computation | async-start | bytes 2621440 | tf_op jit(solution)/shard_map/all_to_all | solution.py:39
  39.9 15.6 %collective-permute-start = (f32[320,512]{1,0:T(8,128)S(1)}, f32[320,512]{1,0:T(8,128)S(1)}, u32[]{:S(2)}, u32[]{:S(2)}) collective-permute-start(f32[320,512]{1,0:T(8,128)S(1)} %all_gather.3.refs_0_), channel_id=1, source_target_pairs={{0,48},{16,32},{32,16},{48,0},{1,49},{17,33},{33,17},{49,1},{2,50}... | collective-permute-start | bytes 1966088 | tf_op jit(solution)/shard_map/ppermute | solution.py:273
  43.9 0.8 copy-start.6
  55.5 0.8 copy-start.8
  56.3 9.5 %collective-permute-start.1 = (f32[640,512]{1,0:T(8,128)}, f32[640,512]{1,0:T(8,128)S(1)}, u32[]{:S(2)}, u32[]{:S(2)}) collective-permute-start(f32[640,512]{1,0:T(8,128)} %bitcast.refs_2_.mine_ref), channel_id=1, source_target_pairs={{0,1},{1,0},{2,3},{3,2},{4,5},{5,4},{6,7},{7,6},{8,9},{9,8},{10,11... | collective-permute-start | bytes 3932168 | tf_op jit(solution)/shard_map/ppermute | solution.py:160
  58.3 1.1 copy-start.7
  59.3 1.1 copy-start.9
  65.9 4.0 %copy-start.3 = (f32[640,512]{1,0:T(8,128)}, f32[640,512]{1,0:T(8,128)S(1)}, u32[]{:S(2)}) copy-start(f32[640,512]{1,0:T(8,128)S(1)} %get-tuple-element.32.src_hbm.src_ref) | copy-start | bytes 3932164
  65.9 4.0 %copy-start = (f32[640,512]{1,0:T(8,128)}, f32[640,512]{1,0:T(8,128)S(1)}, u32[]{:S(2)}) copy-start(f32[640,512]{1,0:T(8,128)S(1)} %collective-permute-done.1.other_ref.other_hbm) | copy-start | bytes 3932164
  167.9 1.3 copy-start.1
  169.2 1.3 copy-start.4
  170.5 5.8 %copy-start.2 = (f32[640,512]{1,0:T(8,128)S(1)}, f32[640,512]{1,0:T(8,128)}, u32[]{:S(2)}) copy-start(f32[640,512]{1,0:T(8,128)} %copy-done) | copy-start | bytes 3932164
  170.6 5.8 %copy-start.5 = (f32[640,512]{1,0:T(8,128)S(1)}, f32[640,512]{1,0:T(8,128)}, u32[]{:S(2)}) copy-start(f32[640,512]{1,0:T(8,128)} %copy-done.3) | copy-start | bytes 3932164
  174.2 7.9 %collective-permute-start.2 = (f32[640,512]{1,0:T(8,128)S(1)}, f32[640,512]{1,0:T(8,128)S(1)}, u32[]{:S(2)}, u32[]{:S(2)}) collective-permute-start(f32[640,512]{1,0:T(8,128)S(1)} %get-tuple-element.36), channel_id=1, source_target_pairs={{0,1},{1,0},{2,3},{3,2},{4,5},{5,4},{6,7},{7,6},{8,9},{9,8},{10,11... | collective-permute-start | bytes 3932168 | tf_op jit(solution)/shard_map/ppermute | solution.py:300
  186.8 51.9 %all-to-all-start.7 = ((f32[16,40,512]{2,1,0:T(8,128)}), f32[16,40,512]{2,1,0:T(8,128)S(1)}, u32[]{:S(2)}, u32[]{:S(2)}) async-start(f32[16,40,512]{2,1,0:T(8,128)} %bitcast.16), calls=%async_computation.7 | async-start | bytes 2621440 | tf_op jit(solution)/shard_map/all_to_all | solution.py:39
  190.5 20.9 %collective-permute-start.4 = (f32[2,40,512]{2,1,0:T(8,128)S(1)}, f32[2,40,512]{2,1,0:T(8,128)S(1)}, u32[]{:S(2)}, u32[]{:S(2)}) collective-permute-start(f32[2,40,512]{2,1,0:T(8,128)S(1)} %get-tuple-element.39), channel_id=1, source_target_pairs={{0,6},{2,8},{4,10},{6,12},{8,14},{10,0},{12,2},{14,4},{1,7},{3,9},... | collective-permute-start | bytes 491528 | tf_op jit(solution)/shard_map/ppermute | solution.py:60
  194.9 19.9 %collective-permute-start.5 = (f32[2,40,512]{2,1,0:T(8,128)S(1)}, f32[2,40,512]{2,1,0:T(8,128)S(1)}, u32[]{:S(2)}, u32[]{:S(2)}) collective-permute-start(f32[2,40,512]{2,1,0:T(8,128)S(1)} %get-tuple-element.40), channel_id=1, source_target_pairs={{0,10},{2,12},{4,14},{6,0},{8,2},{10,4},{12,6},{14,8},{1,11},{3,13... | collective-permute-start | bytes 491528 | tf_op jit(solution)/shard_map/ppermute | solution.py:60
  198.2 18.8 %collective-permute-start.6 = (f32[2,40,512]{2,1,0:T(8,128)S(1)}, f32[2,40,512]{2,1,0:T(8,128)S(1)}, u32[]{:S(2)}, u32[]{:S(2)}) collective-permute-start(f32[2,40,512]{2,1,0:T(8,128)S(1)} %get-tuple-element.41), channel_id=1, source_target_pairs={{0,4},{2,6},{4,8},{6,10},{8,12},{10,14},{12,0},{14,2},{1,5},{3,7},... | collective-permute-start | bytes 491528 | tf_op jit(solution)/shard_map/ppermute | solution.py:60
  203.8 16.5 %collective-permute-start.7 = (f32[2,40,512]{2,1,0:T(8,128)S(1)}, f32[2,40,512]{2,1,0:T(8,128)S(1)}, u32[]{:S(2)}, u32[]{:S(2)}) collective-permute-start(f32[2,40,512]{2,1,0:T(8,128)S(1)} %get-tuple-element.42), channel_id=1, source_target_pairs={{0,12},{2,14},{4,0},{6,2},{8,4},{10,6},{12,8},{14,10},{1,13},{3,15... | collective-permute-start | bytes 491528 | tf_op jit(solution)/shard_map/ppermute | solution.py:60
  205.7 14.6 %collective-permute-start.8 = (f32[2,40,512]{2,1,0:T(8,128)S(1)}, f32[2,40,512]{2,1,0:T(8,128)S(1)}, u32[]{:S(2)}, u32[]{:S(2)}) collective-permute-start(f32[2,40,512]{2,1,0:T(8,128)S(1)} %get-tuple-element.43), channel_id=1, source_target_pairs={{0,2},{2,4},{4,6},{6,8},{8,10},{10,12},{12,14},{14,0},{1,3},{3,5},... | collective-permute-start | bytes 491528 | tf_op jit(solution)/shard_map/ppermute | solution.py:60
  211.4 19.0 %collective-permute-start.9 = (f32[2,40,512]{2,1,0:T(8,128)S(1)}, f32[2,40,512]{2,1,0:T(8,128)S(1)}, u32[]{:S(2)}, u32[]{:S(2)}) collective-permute-start(f32[2,40,512]{2,1,0:T(8,128)S(1)} %get-tuple-element.44), channel_id=1, source_target_pairs={{0,14},{2,0},{4,2},{6,4},{8,6},{10,8},{12,10},{14,12},{1,15},{3,1}... | collective-permute-start | bytes 491528 | tf_op jit(solution)/shard_map/ppermute | solution.py:60
  214.8 15.6 %collective-permute-start.3 = (f32[2,40,512]{2,1,0:T(8,128)S(1)}, f32[2,40,512]{2,1,0:T(8,128)S(1)}, u32[]{:S(2)}, u32[]{:S(2)}) collective-permute-start(f32[2,40,512]{2,1,0:T(8,128)S(1)} %get-tuple-element.38), channel_id=1, source_target_pairs={{0,8},{2,10},{4,12},{6,14},{8,0},{10,2},{12,4},{14,6},{1,9},{3,11}... | collective-permute-start | bytes 491528 | tf_op jit(solution)/shard_map/ppermute | solution.py:60
  230.5 7.5 %collective-permute-start.10 = (f32[40,512]{1,0:T(8,128)S(1)}, f32[40,512]{1,0:T(8,128)S(1)}, u32[]{:S(2)}, u32[]{:S(2)}) collective-permute-start(f32[40,512]{1,0:T(8,128)S(1)} %dynamic-slice_bitcast_fusion), channel_id=1, source_target_pairs={{0,48},{16,32},{32,16},{48,0},{1,49},{17,33},{33,17},{49,1},{2,50}... | collective-permute-start | bytes 245768 | tf_op jit(solution)/shard_map/ppermute | solution.py:61

commit v8 on v7

--- a/solution.py
+++ b/solution.py
@@ -182,22 +182,18 @@
     return mass * tgt - pulled
 
 
-def send_kernel(
-    src_pot_ref, tgt_pot_ref, cost_ref, src_hbm, other_hbm, sent_ref, high_ref, mid_ref,
-    src_ref, tgt_ref, sem,
-):
-    rows, cols = cost_ref.shape
-    copies = (
-        pltpu.make_async_copy(src_hbm, src_ref, sem.at[0]),
-        pltpu.make_async_copy(other_hbm, tgt_ref, sem.at[1]),
-    )
-    for copy in copies:
-        copy.start()
+def columns_of(row):
     lane = lax.broadcasted_iota(jnp.int32, (LANES, LANES), 1)
     sub = lax.broadcasted_iota(jnp.int32, (LANES, LANES), 0)
+    square = jnp.where(lane == sub, jnp.broadcast_to(row, (LANES, LANES)), 0.0)
+    return jnp.sum(square, axis=1, keepdims=True)
+
+
+def weight_kernel(src_pot_ref, tgt_pot_ref, cost_ref, high_ref, mid_ref, sum_ref):
+    rows, cols = cost_ref.shape
+    sums = [0.0] * (cols // LANES)
     for i in range(rows // LANES):
-        row = jnp.broadcast_to(src_pot_ref[i : i + 1, :], (LANES, LANES))
-        column = jnp.sum(jnp.where(lane == sub, row, 0.0), axis=1, keepdims=True)
+        column = columns_of(src_pot_ref[i : i + 1, :])
         at = slice(i * LANES, (i + 1) * LANES)
         for j in range(cols // LANES):
             to = slice(j * LANES, (j + 1) * LANES)
@@ -206,21 +202,31 @@
             high = weight.astype(jnp.bfloat16)
             high_ref[at, to] = high
             mid_ref[at, to] = (weight - high.astype(jnp.float32)).astype(jnp.bfloat16)
-    for copy in copies:
-        copy.wait()
+            sums[j] += jnp.sum(weight, axis=0, keepdims=True)
+    for j, value in enumerate(sums):
+        sum_ref[j : j + 1, :] = value
+
+
+def send_kernel(high_ref, mid_ref, src_ref, other_ref, sent_ref):
     place = 1 - lax.axis_index("c")
-    sent_ref[...] = pull(half_of(high_ref, mid_ref, place), src_ref, tgt_ref[...])
-
-
-def push_kernel(high_ref, mid_ref, src_ref, mine_ref, other_ref, *out_refs):
-    out_refs, part_ref = out_refs[:-1], out_refs[-1]
+    sent_ref[...] = pull(half_of(high_ref, mid_ref, place), src_ref, other_ref[...])
+
+
+def push_kernel(high_ref, mid_ref, scale_ref, src_ref, mine_ref, other_ref, *out_refs):
+    out_refs, (part_ref, tgt_ref, wide_ref) = out_refs[:-3], out_refs[-3:]
     y, c = lax.axis_index("y"), lax.axis_index("c")
-    ones = jnp.ones((mine_ref.shape[0], LANES), jnp.bfloat16)
+    count = scale_ref.shape[0] // 2
     pushed, mass = 0.0, 0.0
     for place, ref in ((c, mine_ref), (1 - c, other_ref)):
+        for i in range(count):
+            low, high = scale_ref[i : i + 1, :], scale_ref[count + i : count + i + 1, :]
+            column = columns_of(jnp.where(place == 0, low, high))
+            at = slice(i * LANES, (i + 1) * LANES)
+            tgt_ref[at, :] = ref[at, :] * column
+            wide_ref[at, :] = jnp.broadcast_to(column, (LANES, LANES))
         weight_parts = half_of(high_ref, mid_ref, place)
-        pushed += three_products(weight_parts, parts_of(ref[...]), (1, 0))
-        mass += sum(product(part, ones, (1, 0)) for part in weight_parts)
+        pushed += three_products(weight_parts, parts_of(tgt_ref[...]), (1, 0))
+        mass += three_products(weight_parts, parts_of(wide_ref[...]), (1, 0))
     part_ref[...] = mass[:, :1] * src_ref[...] - pushed
     size = out_refs[0].shape[1]
     for k, ref in zip(STEPS + (0,), out_refs):
@@ -246,11 +252,14 @@
     )(*args)
 
 
-def exchange(local, axes, groups, count):
-    size = local.shape[0]
-    flat = local.reshape(1, size // LANES, LANES)
-    sent = jnp.broadcast_to(flat, (count, size // LANES, LANES))
-    got = all_to_all(sent, axes, groups)
+def gather_lanes(local, axes, groups):
+    count = len(groups[0])
+    flat = local.reshape(1, local.size // LANES, LANES)
+    return all_to_all(jnp.broadcast_to(flat, (count,) + flat.shape[1:]), axes, groups)
+
+
+def exchange(local, axes, groups):
+    got = gather_lanes(local, axes, groups)
     peak = jnp.max(got, axis=0)
     total = jnp.sum(jnp.exp(got - peak[None]), axis=0)
     return peak + jnp.log(total)
@@ -274,41 +283,55 @@
     mine, far = lax.optimization_barrier((mine, far))
     src_block, other, cost = tile((near, far), mine)
     tile_rows, tile_cols = cost.shape
-    tgt_pot = jnp.zeros((tile_cols,), jnp.float32)
     log_total = math.log(total_points)
-    for _ in range(ITERS):
-        lse = local_lse((tgt_pot.reshape(1, tile_cols) - cost) / ENTROPY_REG, 1)
-        lse = exchange(lse, ("x", "y"), ROW_GROUPS, 2 * NY)
-        src_pot = -ENTROPY_REG * (lse - log_total)
-        lse = local_lse((src_pot.reshape(tile_rows, 1) - cost) / ENTROPY_REG, 0)
-        lse = exchange(lse, ("z", "x", "c"), COL_GROUPS, 2 * NZ * NC)
-        tgt_pot = -ENTROPY_REG * (lse - log_total)
+    row_axes, col_axes = ("x", "y"), ("z", "x", "c")
+    lse = exchange(local_lse(-cost / ENTROPY_REG, 1), row_axes, ROW_GROUPS)
+    src_pot = -ENTROPY_REG * (lse - log_total)
+    scores = (src_pot.reshape(tile_rows, 1) - cost) / ENTROPY_REG
+    lse = exchange(local_lse(scores, 0), col_axes, COL_GROUPS)
+    tgt_pot = -ENTROPY_REG * (lse - log_total)
+
+    def weights():
+        total = src_pot.reshape(tile_rows, 1) + tgt_pot.reshape(1, tile_cols) - cost
+        return jnp.exp(total / ENTROPY_REG)
+
+    for iteration in range(1, ITERS):
+        row_sums = gather_lanes(jnp.sum(weights(), axis=1), row_axes, ROW_GROUPS)
+        row_sums = jnp.sum(row_sums, axis=0)
+        src_pot = src_pot - ENTROPY_REG * (jnp.log(row_sums) - log_total)
+        if iteration < ITERS - 1:
+            col_sums = gather_lanes(jnp.sum(weights(), axis=0), col_axes, COL_GROUPS)
+            col_sums = jnp.sum(col_sums, axis=0)
+            tgt_pot = tgt_pot - ENTROPY_REG * (jnp.log(col_sums) - log_total)
     part = jax.ShapeDtypeStruct(cost.shape, jnp.bfloat16)
     half = jax.ShapeDtypeStruct(mine.shape, jnp.float32)
-    sent, high, mid = pl.pallas_call(
-        send_kernel,
-        out_shape=(half, part, part),
-        in_specs=[WHOLE] * 3 + [IN_HBM] * 2,
-        out_specs=(WHOLE,) * 3,
-        scratch_shapes=[
-            pltpu.VMEM(src_block.shape, jnp.float32),
-            pltpu.VMEM(mine.shape, jnp.float32),
-            pltpu.SemaphoreType.DMA((2,)),
-        ],
-        compiler_params=pltpu.CompilerParams(vmem_limit_bytes=VMEM_LIMIT),
-    )(src_pot, tgt_pot, cost, src_block, other)
+    lanes = jax.ShapeDtypeStruct(tgt_pot.shape, jnp.float32)
+    high, mid, col_sums = on_tile(
+        weight_kernel, (part, part, lanes), [], src_pot, tgt_pot, cost
+    )
+    col_sums = gather_lanes(col_sums, col_axes, COL_GROUPS)
+    sent = on_tile(send_kernel, half, [], high, mid, src_block, other)
     came = lax.ppermute(sent, "c", SWAP)
+    tgt_half = on_tile(keep_kernel, half, [], high, mid, src_block, mine, came)
+    tgt_half, col_sums = lax.optimization_barrier((tgt_half, col_sums))
+    tgt_sum = scatter_blocks(tgt_half, ("z", "x"), SIDE_GROUPS)
+    col_sums = jnp.sum(col_sums, axis=0)
+    tgt_pot = tgt_pot - ENTROPY_REG * (jnp.log(col_sums) - log_total)
     pair = jax.ShapeDtypeStruct((2, rows, width), jnp.float32)
-    scratch = [pltpu.VMEM(src_block.shape, jnp.float32)]
-    pieces = on_tile(push_kernel, (pair,) * NY, scratch, high, mid, src_block, mine, other)
-    pieces = list(pieces)
-    came, pieces[0] = lax.optimization_barrier((came, pieces[0]))
-    tgt_half = on_tile(keep_kernel, half, [], high, mid, src_block, mine, came)
-    tgt_sum = scatter_blocks(tgt_half, ("z", "x"), SIDE_GROUPS)
+    scratch = [
+        pltpu.VMEM(src_block.shape, jnp.float32),
+        pltpu.VMEM(mine.shape, jnp.float32),
+        pltpu.VMEM((mine.shape[0], LANES), jnp.float32),
+    ]
+    pieces = on_tile(
+        push_kernel, (pair,) * NY, scratch,
+        high, mid, total_points / col_sums, src_block, mine, other,
+    )
     src_sum = scatter_ring(pieces, a)
     src_piece = take(src_pot.reshape(-1, rows), a * NY + y)
     tgt_piece = take(tgt_pot.reshape(-1, rows), (c * 2 + b) * NZ + z)
-    return src_piece, tgt_piece, src_sum / total_points, tgt_sum / total_points
+    col_sum = take(col_sums.reshape(-1, rows), (c * 2 + b) * NZ + z)
+    return src_piece, tgt_piece, src_sum / total_points, tgt_sum / col_sum[:, None]
 
 
 def solution(mesh):

time: 242 us -> 244 us (level)
  blocking collectives: 116 us -> 88.6 us
  starting transfers between devices: 50.4 us -> 65.4 us
  local copies, waits for them, and re-layouts: 9.43 us -> 16.5 us
  other arithmetic: 8.97 us -> 12.1 us
    all_to_all x6 -> x4, blocking collectives: 90.3 us -> 62.8 us  [all_to_all(): lax.all_to_all(blocks, axes, split_axis=0, concat_axis=0, axis_index_grou...]
    all_to_all x2 -> x4, waiting for transfers between devices: 0.01 us -> 12 us  [all_to_all(): lax.all_to_all(blocks, axes, split_axis=0, concat_axis=0, axis_index_grou...]
    all_to_all x2 -> x4, starting transfers between devices: 15.1 us -> 25.7 us  [all_to_all(): lax.all_to_all(blocks, axes, split_axis=0, concat_axis=0, axis_index_grou...]
    ppermute x7, waiting for transfers between devices: 14.9 us -> 4.4 us  [scatter_ring(): total = total + lax.ppermute(piece, 'y', moves)]
    reduce_sum x0 -> x7, other arithmetic: none -> 5.61 us  [the longest x2 3.23 us: per_device(): row_sums = gather_lanes(jnp.sum(weights(), axis=1), row_axes, ROW_GROUPS)]
    unnamed x22 -> x62, local copies, waits for them, and re-layouts: 6.49 us -> 12.1 us
    ppermute x7, starting transfers between devices: 24.6 us -> 29.3 us  [scatter_ring(): total = total + lax.ppermute(piece, 'y', moves)]
    pallas_call x2 -> x4, Pallas kernels: 10.4 us -> 14.8 us  [on_tile(): pl.pallas_call(kernel, out_shape=out_shape, in_specs=[WHOLE] * len(args),...]
  transfers between devices with their start and end apart: 13 -> 15, of which waited for: 5 -> 7; matrix products, arithmetic and copies ran while one was open for 1% -> 2% of each run, Pallas kernels for 5% -> 7%
where the time goes in v8:
time: 244 us; the launch traced here: 240 us
  blocking collectives  88.6 us (36%)
  starting transfers between devices  65.4 us (27%)
  waiting for transfers between devices  31.5 us (13%)
  Pallas kernels  24.2 us (10%)
  local copies, waits for them, and re-layouts  16.5 us (7%)
  other arithmetic  12.1 us (5%)
    all_to_all x4, blocking collectives, all_to_all(): lax.all_to_all(blocks, axes, split_axis=0, concat_axis=0, axis_index_grou...  62.8 us
    ppermute x7, starting transfers between devices, scatter_ring(): total = total + lax.ppermute(piece, 'y', moves)  29.3 us
    all_gather x1, blocking collectives, per_device(): near = lax.all_gather(src_emb, 'y', axis=0, tiled=True)  25.7 us
    all_to_all x4, starting transfers between devices, all_to_all(): lax.all_to_all(blocks, axes, split_axis=0, concat_axis=0, axis_index_grou...  25.7 us
    pallas_call x4, Pallas kernels, on_tile(): pl.pallas_call(kernel, out_shape=out_shape, in_specs=[WHOLE] * len(args),...  14.8 us
    unnamed x62, local copies, waits for them, and re-layouts  12.1 us
    all_to_all x4, waiting for transfers between devices, all_to_all(): lax.all_to_all(blocks, axes, split_axis=0, concat_axis=0, axis_index_grou...  12 us
    ppermute x1, waiting for transfers between devices, per_device(): far = lax.ppermute(near, 'x', FLIP_A)  10.7 us
  transfers between devices with their start and end apart: 15, of which 7 were waited for; matrix products, arithmetic and copies ran while one was open for 2% of the time, Pallas kernels for 7%

profile of v8, /device:TPU:56, one launch (start us, length us, event | category | flops | bytes accessed | tf_op | source)
XLA Modules:
  0.0 239.5 jit_solution(1930147379983122602)
XLA Ops:
  2.8 11.4 %all-to-all-start = ((f32[16,40,512]{2,1,0:T(8,128)}), f32[16,40,512]{2,1,0:T(8,128)}, u32[]{:S(2)}, u32[]{:S(2)}) async-start(f32[16,40,512]{2,1,0:T(8,128)} %broadcast_in_dim.20), calls=%async_computation | async-start | bytes 2621440 | tf_op jit(solution)/shard_map/all_to_all | solution.py:39
  14.2 25.7 %all_gather.3.refs_0_ = f32[320,512]{1,0:T(8,128)S(1)} all-gather(f32[40,512]{1,0:T(8,128)S(1)} %copy-done.20), channel_id=1, replica_groups=mesh['z'=8,'x'=4,'y'=8,'c'=2] {'y'}, dimensions={0}, use_global_device_ids=true | all-gather | bytes 737280 | tf_op jit(solution)/shard_map/all_gather | solution.py:281
  39.9 4.0 %collective-permute-start = (f32[320,512]{1,0:T(8,128)S(1)}, f32[320,512]{1,0:T(8,128)S(1)}, u32[]{:S(2)}, u32[]{:S(2)}) collective-permute-start(f32[320,512]{1,0:T(8,128)S(1)} %all_gather.3.refs_0_), channel_id=1, source_target_pairs={{0,48},{16,32},{32,16},{48,0},{1,49},{17,33},{33,17},{49,1},{2,50}... | collective-permute-start | bytes 1966088 | tf_op jit(solution)/shard_map/ppermute | solution.py:282
  44.8 10.7 %collective-permute-done.refs_1_ = f32[320,512]{1,0:T(8,128)S(1)} collective-permute-done((f32[320,512]{1,0:T(8,128)S(1)}, f32[320,512]{1,0:T(8,128)S(1)}, u32[]{:S(2)}, u32[]{:S(2)}) %collective-permute-start) | collective-permute-done | bytes 655392 | tf_op jit(solution)/shard_map/ppermute | solution.py:282
  60.4 5.4 %shard_map.57 = (f32[640,512]{1,0:T(8,128)S(1)}, bf16[640,512]{1,0:T(8,128)(2,1)S(1)}, bf16[640,512]{1,0:T(8,128)(2,1)S(1)}, bf16[640,512]{1,0:T(8,128)(2,1)S(1)...) custom-call(f32[320,512]{1,0:T(8,128)S(1)} %copy-done.15, f32[320,512]{1,0:T(8,128)S(1)} %copy-done.17, ...), custom_call_target="tpu_custom_call" | custom-call | tf_op jit(solution)/shard_map/pallas_call | solution.py:140
  65.9 4.0 %shard_map.58.cost_ref = f32[640,1280]{1,0:T(8,128)S(1)} custom-call(bf16[640,512]{1,0:T(8,128)(2,1)S(1)} %get-tuple-element.27.high_ref, bf16[640,512]{1,0:T(8,128)(2,1)S(1)} %get-tuple-element.28.mid_ref, bf16[640,512]{1,0:T(8,128)(2,1)S(1)} %get-tuple-element.29.low_ref, f32[640,1]{1,0:T(8,128)S(1)} %get-tuple-element.30.sq_ref, ...), custom_call_target="tpu_custom_call", output_to_operand_aliasing={{}: (5, {})} | custom-call | tf_op jit(solution)/shard_map/pallas_call | solution.py:161
  70.9 15.6 %all_to_all.40 = f32[16,5,128]{2,1,0:T(8,128)S(1)} all-to-all(f32[16,5,128]{2,1,0:T(8,128)S(1)} %broadcast_in_dim.21), channel_id=1, replica_groups={{0,2,4,6,8,10,12,14,48,50,52,54,56,58,60,62},{16,18,20,22,24,26,28,30,3..., dimensions={0} | all-to-all | bytes 81920 | tf_op jit(solution)/shard_map/all_to_all | solution.py:39
  88.3 19.5 %all_to_all.41 = f32[32,10,128]{2,1,0:T(8,128)S(1)} all-to-all(f32[32,10,128]{2,1,0:T(8,128)S(1)} %broadcast_in_dim.22), channel_id=1, replica_groups={{0,1,16,17,64,65,80,81,128,129,144,145,192,193,208,209,256,257,272,273,..., dimensions={0} | all-to-all | bytes 327680 | tf_op jit(solution)/shard_map/all_to_all | solution.py:39
  110.2 12.5 %all_to_all.42 = f32[16,5,128]{2,1,0:T(8,128)S(1)} all-to-all(f32[16,5,128]{2,1,0:T(8,128)S(1)} %broadcast_in_dim.24), channel_id=1, replica_groups={{0,2,4,6,8,10,12,14,48,50,52,54,56,58,60,62},{16,18,20,22,24,26,28,30,3..., dimensions={0} | all-to-all | bytes 81920 | tf_op jit(solution)/shard_map/all_to_all | solution.py:39
  123.6 15.2 %all_to_all.43 = f32[32,10,128]{2,1,0:T(8,128)S(1)} all-to-all(f32[32,10,128]{2,1,0:T(8,128)S(1)} %broadcast_in_dim.26), channel_id=1, replica_groups={{0,1,16,17,64,65,80,81,128,129,144,145,192,193,208,209,256,257,272,273,..., dimensions={0} | all-to-all | bytes 327680 | tf_op jit(solution)/shard_map/all_to_all | solution.py:39
  142.4 5.3 %all-to-all-start.5 = ((f32[16,5,128]{2,1,0:T(8,128)}), f32[16,5,128]{2,1,0:T(8,128)S(1)}, u32[]{:S(2)}, u32[]{:S(2)}) async-start(f32[16,5,128]{2,1,0:T(8,128)} %broadcast_in_dim.55), calls=%async_computation.5 | async-start | bytes 131072 | tf_op jit(solution)/shard_map/all_to_all | solution.py:39
  147.8 7.8 %all-to-all-done.5 = f32[16,5,128]{2,1,0:T(8,128)S(1)} async-done(((f32[16,5,128]{2,1,0:T(8,128)}), f32[16,5,128]{2,1,0:T(8,128)S(1)}, u32[]{:S(2)}, u32[]{:S(2)}) %all-to-all-start.5) | async-done | bytes 40992 | tf_op jit(solution)/shard_map/all_to_all | solution.py:39
  162.3 4.6 %all-to-all-start.6 = ((f32[32,10,128]{2,1,0:T(8,128)}), f32[32,10,128]{2,1,0:T(8,128)}, u32[]{:S(2)}, u32[]{:S(2)}) async-start(f32[32,10,128]{2,1,0:T(8,128)} %broadcast_in_dim.56), calls=%async_computation.6 | async-start | bytes 524288 | tf_op jit(solution)/shard_map/all_to_all | solution.py:39
  169.8 4.2 %shard_map.61 = f32[640,512]{1,0:T(8,128)S(1)} custom-call(bf16[640,1280]{1,0:T(8,128)(2,1)S(1)} %copy-done.1, bf16[640,1280]{1,0:T(8,128)(2,1)S(1)} %copy-done.4, f32[640,512]{1,0:T(8,128)S(1)} %copy-done.11, f32[640,512]{1,0:T(8,128)} %bitcast.refs_2_.mine_ref, f32[640,512]{1,0:T(8,128)} %collective-permute-done.2.came_ref), custom_call_target="tpu_custom_call" | custom-call | tf_op jit(solution)/shard_map/pallas_call | solution.py:245
  175.1 4.2 %all-to-all-done.6 = f32[32,10,128]{2,1,0:T(8,128)} async-done(((f32[32,10,128]{2,1,0:T(8,128)}), f32[32,10,128]{2,1,0:T(8,128)}, u32[]{:S(2)}, u32[]{:S(2)}) %all-to-all-start.6) | async-done | bytes 163872 | tf_op jit(solution)/shard_map/all_to_all | solution.py:39
  179.2 4.4 %all-to-all-start.7 = ((f32[16,40,512]{2,1,0:T(8,128)}), f32[16,40,512]{2,1,0:T(8,128)}, u32[]{:S(2)}, u32[]{:S(2)}) async-start(f32[16,40,512]{2,1,0:T(8,128)} %bitcast.29), calls=%async_computation.7 | async-start | bytes 2621440 | tf_op jit(solution)/shard_map/all_to_all | solution.py:39
  187.3 7.1 %shard_map.62 = (f32[2,40,512]{2,1,0:T(8,128)S(1)}, f32[2,40,512]{2,1,0:T(8,128)S(1)}, f32[2,40,512]{2,1,0:T(8,128)}, f32[2,40,512]{2,1,0:T(8,128)}, f32[2,40,51...) custom-call(bf16[640,1280]{1,0:T(8,128)(2,1)S(1)} %copy-done.2, ...), custom_call_target="tpu_custom_call" | custom-call | tf_op jit(solution)/shard_map/pallas_call | solution.py:245
  194.4 4.4 %collective-permute-start.3 = (f32[2,40,512]{2,1,0:T(8,128)S(1)}, f32[2,40,512]{2,1,0:T(8,128)S(1)}, u32[]{:S(2)}, u32[]{:S(2)}) collective-permute-start(f32[2,40,512]{2,1,0:T(8,128)S(1)} %get-tuple-element.38), channel_id=1, source_target_pairs={{0,8},{2,10},{4,12},{6,14},{8,0},{10,2},{12,4},{14,6},{1,9},{3,11}... | collective-permute-start | bytes 491528 | tf_op jit(solution)/shard_map/ppermute | solution.py:60
  198.8 4.3 %collective-permute-start.4 = (f32[2,40,512]{2,1,0:T(8,128)S(1)}, f32[2,40,512]{2,1,0:T(8,128)S(1)}, u32[]{:S(2)}, u32[]{:S(2)}) collective-permute-start(f32[2,40,512]{2,1,0:T(8,128)S(1)} %get-tuple-element.39), channel_id=1, source_target_pairs={{0,6},{2,8},{4,10},{6,12},{8,14},{10,0},{12,2},{14,4},{1,7},{3,9},... | collective-permute-start | bytes 491528 | tf_op jit(solution)/shard_map/ppermute | solution.py:60
  203.1 3.4 %collective-permute-start.5 = (f32[2,40,512]{2,1,0:T(8,128)}, f32[2,40,512]{2,1,0:T(8,128)S(1)}, u32[]{:S(2)}, u32[]{:S(2)}) collective-permute-start(f32[2,40,512]{2,1,0:T(8,128)} %get-tuple-element.40), channel_id=1, source_target_pairs={{0,10},{2,12},{4,14},{6,0},{8,2},{10,4},{12,6},{14,8},{1,11},{3,13... | collective-permute-start | bytes 491528 | tf_op jit(solution)/shard_map/ppermute | solution.py:60
  206.5 4.7 %collective-permute-start.6 = (f32[2,40,512]{2,1,0:T(8,128)}, f32[2,40,512]{2,1,0:T(8,128)S(1)}, u32[]{:S(2)}, u32[]{:S(2)}) collective-permute-start(f32[2,40,512]{2,1,0:T(8,128)} %get-tuple-element.41), channel_id=1, source_target_pairs={{0,4},{2,6},{4,8},{6,10},{8,12},{10,14},{12,0},{14,2},{1,5},{3,7},... | collective-permute-start | bytes 491528 | tf_op jit(solution)/shard_map/ppermute | solution.py:60
  213.9 4.4 %collective-permute-start.8 = (f32[2,40,512]{2,1,0:T(8,128)}, f32[2,40,512]{2,1,0:T(8,128)S(1)}, u32[]{:S(2)}, u32[]{:S(2)}) collective-permute-start(f32[2,40,512]{2,1,0:T(8,128)} %get-tuple-element.43), channel_id=1, source_target_pairs={{0,2},{2,4},{4,6},{6,8},{8,10},{10,12},{12,14},{14,0},{1,3},{3,5},... | collective-permute-start | bytes 491528 | tf_op jit(solution)/shard_map/ppermute | solution.py:60
  220.4 5.5 %collective-permute-start.9 = (f32[2,40,512]{2,1,0:T(8,128)}, f32[2,40,512]{2,1,0:T(8,128)S(1)}, u32[]{:S(2)}, u32[]{:S(2)}) collective-permute-start(f32[2,40,512]{2,1,0:T(8,128)} %get-tuple-element.44), channel_id=1, source_target_pairs={{0,14},{2,0},{4,2},{6,4},{8,6},{10,8},{12,10},{14,12},{1,15},{3,1}... | collective-permute-start | bytes 491528 | tf_op jit(solution)/shard_map/ppermute | solution.py:60
  232.3 4.5 %collective-permute-done.10 = f32[40,512]{1,0:T(8,128)S(1)} collective-permute-done((f32[40,512]{1,0:T(8,128)S(1)}, f32[40,512]{1,0:T(8,128)S(1)}, u32[]{:S(2)}, u32[]{:S(2)}) %collective-permute-start.10) | collective-permute-done | bytes 81952 | tf_op jit(solution)/shard_map/ppermute | solution.py:61
  (120 shorter events, 45.5 us)
Async XLA Ops:
  0.6 13.6 %copy-start.20 = (f32[40,512]{1,0:T(8,128)S(1)}, f32[40,512]{1,0:T(8,128)}, u32[]{:S(2)}) copy-start(f32[40,512]{1,0:T(8,128)} %param.2) | copy-start | bytes 245764
  2.8 53.5 %all-to-all-start = ((f32[16,40,512]{2,1,0:T(8,128)}), f32[16,40,512]{2,1,0:T(8,128)}, u32[]{:S(2)}, u32[]{:S(2)}) async-start(f32[16,40,512]{2,1,0:T(8,128)} %broadcast_in_dim.20), calls=%async_computation | async-start | bytes 2621440 | tf_op jit(solution)/shard_map/all_to_all | solution.py:39
  39.9 15.6 %collective-permute-start = (f32[320,512]{1,0:T(8,128)S(1)}, f32[320,512]{1,0:T(8,128)S(1)}, u32[]{:S(2)}, u32[]{:S(2)}) collective-permute-start(f32[320,512]{1,0:T(8,128)S(1)} %all_gather.3.refs_0_), channel_id=1, source_target_pairs={{0,48},{16,32},{32,16},{48,0},{1,49},{17,33},{33,17},{49,1},{2,50}... | collective-permute-start | bytes 1966088 | tf_op jit(solution)/shard_map/ppermute | solution.py:282
  56.3 9.5 %collective-permute-start.1 = (f32[640,512]{1,0:T(8,128)}, f32[640,512]{1,0:T(8,128)S(1)}, u32[]{:S(2)}, u32[]{:S(2)}) collective-permute-start(f32[640,512]{1,0:T(8,128)} %bitcast.refs_2_.mine_ref), channel_id=1, source_target_pairs={{0,1},{1,0},{2,3},{3,2},{4,5},{5,4},{6,7},{7,6},{8,9},{9,8},{10,11... | collective-permute-start | bytes 3932168 | tf_op jit(solution)/shard_map/ppermute | solution.py:160
  108.6 14.2 %copy-start.19 = (f32[640]{0:T(1024)S(1)}, f32[640]{0:T(1024)}, u32[]{:S(2)}) copy-start(f32[640]{0:T(1024)} %copy-done.18) | copy-start | bytes 7684
  139.4 8.4 %copy-start.23 = (f32[10,128]{1,0:T(8,128)S(1)}, f32[10,128]{1,0:T(8,128)}, u32[]{:S(2)}) copy-start(f32[10,128]{1,0:T(8,128)} %reduce_sum.117) | copy-start | bytes 15364
  139.4 16.2 %copy-start.25 = (f32[5,128]{1,0:T(8,128)S(1)}, f32[5,128]{1,0:T(8,128)}, u32[]{:S(2)}) copy-start(f32[5,128]{1,0:T(8,128)} %copy-done.24) | copy-start | bytes 7684
  139.4 16.2 %copy-start.28 = (f32[5,128]{1,0:T(8,128)S(1)}, f32[5,128]{1,0:T(8,128)}, u32[]{:S(2)}) copy-start(f32[5,128]{1,0:T(8,128)} %copy-done.27) | copy-start | bytes 7684
  139.4 16.2 %copy-start.30 = (f32[5,128]{1,0:T(8,128)S(1)}, f32[5,128]{1,0:T(8,128)}, u32[]{:S(2)}) copy-start(f32[5,128]{1,0:T(8,128)} %copy-done.29) | copy-start | bytes 7684
  142.4 13.1 %all-to-all-start.5 = ((f32[16,5,128]{2,1,0:T(8,128)}), f32[16,5,128]{2,1,0:T(8,128)S(1)}, u32[]{:S(2)}, u32[]{:S(2)}) async-start(f32[16,5,128]{2,1,0:T(8,128)} %broadcast_in_dim.55), calls=%async_computation.5 | async-start | bytes 131072 | tf_op jit(solution)/shard_map/all_to_all | solution.py:39
  157.3 9.6 %copy-start.11 = (f32[640,512]{1,0:T(8,128)S(1)}, f32[640,512]{1,0:T(8,128)}, u32[]{:S(2)}) copy-start(f32[640,512]{1,0:T(8,128)} %copy-done.9) | copy-start | bytes 3932164
  159.6 7.3 %collective-permute-start.2 = (f32[640,512]{1,0:T(8,128)S(1)}, f32[640,512]{1,0:T(8,128)}, u32[]{:S(2)}, u32[]{:S(2)}) collective-permute-start(f32[640,512]{1,0:T(8,128)S(1)} %shard_map.60), channel_id=1, source_target_pairs={{0,1},{1,0},{2,3},{3,2},{4,5},{5,4},{6,7},{7,6},{8,9},{9,8},{10,11... | collective-permute-start | bytes 3932168 | tf_op jit(solution)/shard_map/ppermute | solution.py:314
  162.3 16.9 %all-to-all-start.6 = ((f32[32,10,128]{2,1,0:T(8,128)}), f32[32,10,128]{2,1,0:T(8,128)}, u32[]{:S(2)}, u32[]{:S(2)}) async-start(f32[32,10,128]{2,1,0:T(8,128)} %broadcast_in_dim.56), calls=%async_computation.6 | async-start | bytes 524288 | tf_op jit(solution)/shard_map/all_to_all | solution.py:39
  169.8 14.9 %copy-start.5 = (bf16[640,1280]{1,0:T(8,128)(2,1)S(1)}, bf16[640,1280]{1,0:T(8,128)(2,1)}, u32[]{:S(2)}) copy-start(bf16[640,1280]{1,0:T(8,128)(2,1)} %copy-done.3) | copy-start | bytes 4915204
  175.1 9.6 %copy-start.2 = (bf16[640,1280]{1,0:T(8,128)(2,1)S(1)}, bf16[640,1280]{1,0:T(8,128)(2,1)}, u32[]{:S(2)}) copy-start(bf16[640,1280]{1,0:T(8,128)(2,1)} %copy-done) | copy-start | bytes 4915204
  179.2 58.1 %all-to-all-start.7 = ((f32[16,40,512]{2,1,0:T(8,128)}), f32[16,40,512]{2,1,0:T(8,128)}, u32[]{:S(2)}, u32[]{:S(2)}) async-start(f32[16,40,512]{2,1,0:T(8,128)} %bitcast.29), calls=%async_computation.7 | async-start | bytes 2621440 | tf_op jit(solution)/shard_map/all_to_all | solution.py:39
  194.4 19.5 %collective-permute-start.3 = (f32[2,40,512]{2,1,0:T(8,128)S(1)}, f32[2,40,512]{2,1,0:T(8,128)S(1)}, u32[]{:S(2)}, u32[]{:S(2)}) collective-permute-start(f32[2,40,512]{2,1,0:T(8,128)S(1)} %get-tuple-element.38), channel_id=1, source_target_pairs={{0,8},{2,10},{4,12},{6,14},{8,0},{10,2},{12,4},{14,6},{1,9},{3,11}... | collective-permute-start | bytes 491528 | tf_op jit(solution)/shard_map/ppermute | solution.py:60
  198.8 21.5 %collective-permute-start.4 = (f32[2,40,512]{2,1,0:T(8,128)S(1)}, f32[2,40,512]{2,1,0:T(8,128)S(1)}, u32[]{:S(2)}, u32[]{:S(2)}) collective-permute-start(f32[2,40,512]{2,1,0:T(8,128)S(1)} %get-tuple-element.39), channel_id=1, source_target_pairs={{0,6},{2,8},{4,10},{6,12},{8,14},{10,0},{12,2},{14,4},{1,7},{3,9},... | collective-permute-start | bytes 491528 | tf_op jit(solution)/shard_map/ppermute | solution.py:60
  203.1 23.7 %collective-permute-start.5 = (f32[2,40,512]{2,1,0:T(8,128)}, f32[2,40,512]{2,1,0:T(8,128)S(1)}, u32[]{:S(2)}, u32[]{:S(2)}) collective-permute-start(f32[2,40,512]{2,1,0:T(8,128)} %get-tuple-element.40), channel_id=1, source_target_pairs={{0,10},{2,12},{4,14},{6,0},{8,2},{10,4},{12,6},{14,8},{1,11},{3,13... | collective-permute-start | bytes 491528 | tf_op jit(solution)/shard_map/ppermute | solution.py:60
  206.5 20.3 %collective-permute-start.6 = (f32[2,40,512]{2,1,0:T(8,128)}, f32[2,40,512]{2,1,0:T(8,128)S(1)}, u32[]{:S(2)}, u32[]{:S(2)}) collective-permute-start(f32[2,40,512]{2,1,0:T(8,128)} %get-tuple-element.41), channel_id=1, source_target_pairs={{0,4},{2,6},{4,8},{6,10},{8,12},{10,14},{12,0},{14,2},{1,5},{3,7},... | collective-permute-start | bytes 491528 | tf_op jit(solution)/shard_map/ppermute | solution.py:60
  211.2 15.6 %collective-permute-start.7 = (f32[2,40,512]{2,1,0:T(8,128)}, f32[2,40,512]{2,1,0:T(8,128)S(1)}, u32[]{:S(2)}, u32[]{:S(2)}) collective-permute-start(f32[2,40,512]{2,1,0:T(8,128)} %get-tuple-element.42), channel_id=1, source_target_pairs={{0,12},{2,14},{4,0},{6,2},{8,4},{10,6},{12,8},{14,10},{1,13},{3,15... | collective-permute-start | bytes 491528 | tf_op jit(solution)/shard_map/ppermute | solution.py:60
  213.9 14.5 %collective-permute-start.8 = (f32[2,40,512]{2,1,0:T(8,128)}, f32[2,40,512]{2,1,0:T(8,128)S(1)}, u32[]{:S(2)}, u32[]{:S(2)}) collective-permute-start(f32[2,40,512]{2,1,0:T(8,128)} %get-tuple-element.43), channel_id=1, source_target_pairs={{0,2},{2,4},{4,6},{6,8},{8,10},{10,12},{12,14},{14,0},{1,3},{3,5},... | collective-permute-start | bytes 491528 | tf_op jit(solution)/shard_map/ppermute | solution.py:60
  220.4 8.7 %collective-permute-start.9 = (f32[2,40,512]{2,1,0:T(8,128)}, f32[2,40,512]{2,1,0:T(8,128)S(1)}, u32[]{:S(2)}, u32[]{:S(2)}) collective-permute-start(f32[2,40,512]{2,1,0:T(8,128)} %get-tuple-element.44), channel_id=1, source_target_pairs={{0,14},{2,0},{4,2},{6,4},{8,6},{10,8},{12,10},{14,12},{1,15},{3,1}... | collective-permute-start | bytes 491528 | tf_op jit(solution)/shard_map/ppermute | solution.py:60
  229.2 7.5 %collective-permute-start.10 = (f32[40,512]{1,0:T(8,128)S(1)}, f32[40,512]{1,0:T(8,128)S(1)}, u32[]{:S(2)}, u32[]{:S(2)}) collective-permute-start(f32[40,512]{1,0:T(8,128)S(1)} %dynamic-slice_bitcast_fusion), channel_id=1, source_target_pairs={{0,48},{16,32},{32,16},{48,0},{1,49},{17,33},{33,17},{49,1},{2,50}... | collective-permute-start | bytes 245768 | tf_op jit(solution)/shard_map/ppermute | solution.py:61
  (22 other events, 40.9 us)

commit v9 on v8

--- a/solution.py
+++ b/solution.py
@@ -53,12 +53,9 @@
     return all_to_all(blocks, axes, groups).reshape(-1, shard.shape[1])
 
 
-def scatter_ring(pieces, a):
-    total = pieces[-1]
-    for k, piece in zip(STEPS, pieces):
-        moves = [(i, (i + k) % NY) for i in range(NY)]
-        total = total + lax.ppermute(piece, "y", moves)
-    return take(total, a) + lax.ppermute(take(total, 1 - a), "x", FLIP_A)
+def sum_pieces(pieces, b):
+    total = sum(pieces)
+    return take(total, b) + lax.ppermute(take(total, 1 - b), "x", FLIP_B)
 
 
 def scatter_blocks(partial, axes, groups):
@@ -207,14 +204,24 @@
         sum_ref[j : j + 1, :] = value
 
 
-def send_kernel(high_ref, mid_ref, src_ref, other_ref, sent_ref):
-    place = 1 - lax.axis_index("c")
-    sent_ref[...] = pull(half_of(high_ref, mid_ref, place), src_ref, other_ref[...])
+def pull_kernel(high_ref, mid_ref, src_ref, mine_ref, other_ref, sent_ref, kept_ref):
+    c = lax.axis_index("c")
+    sent_ref[...] = pull(half_of(high_ref, mid_ref, 1 - c), src_ref, other_ref[...])
+    kept_ref[...] = pull(half_of(high_ref, mid_ref, c), src_ref, mine_ref[...])
+
+
+def order_kernel(kept_ref, came_ref, *out_refs):
+    z = lax.axis_index("z")
+    size = out_refs[0].shape[1]
+    for k, ref in zip(STEPS + (0,), out_refs):
+        for b in range(2):
+            at = pl.ds(pl.multiple_of((b * NZ + (z + k) % NZ) * size, 8), size)
+            ref[b] = kept_ref[at, :] + came_ref[at, :]
 
 
 def push_kernel(high_ref, mid_ref, scale_ref, src_ref, mine_ref, other_ref, *out_refs):
-    out_refs, (part_ref, tgt_ref, wide_ref) = out_refs[:-3], out_refs[-3:]
-    y, c = lax.axis_index("y"), lax.axis_index("c")
+    out_ref, tgt_ref, wide_ref = out_refs
+    c = lax.axis_index("c")
     count = scale_ref.shape[0] // 2
     pushed, mass = 0.0, 0.0
     for place, ref in ((c, mine_ref), (1 - c, other_ref)):
@@ -227,18 +234,7 @@
         weight_parts = half_of(high_ref, mid_ref, place)
         pushed += three_products(weight_parts, parts_of(tgt_ref[...]), (1, 0))
         mass += three_products(weight_parts, parts_of(wide_ref[...]), (1, 0))
-    part_ref[...] = mass[:, :1] * src_ref[...] - pushed
-    size = out_refs[0].shape[1]
-    for k, ref in zip(STEPS + (0,), out_refs):
-        for a in range(2):
-            at = pl.multiple_of((a * NY + (y + k) % NY) * size, 8)
-            ref[a] = part_ref[pl.ds(at, size), :]
-
-
-def keep_kernel(high_ref, mid_ref, src_ref, mine_ref, came_ref, out_ref):
-    place = lax.axis_index("c")
-    kept = pull(half_of(high_ref, mid_ref, place), src_ref, mine_ref[...])
-    out_ref[...] = kept + came_ref[...]
+    out_ref[...] = mass[:, :1] * src_ref[...] - pushed
 
 
 def on_tile(kernel, out_shape, scratch, *args):
@@ -285,24 +281,16 @@
     tile_rows, tile_cols = cost.shape
     log_total = math.log(total_points)
     row_axes, col_axes = ("x", "y"), ("z", "x", "c")
-    lse = exchange(local_lse(-cost / ENTROPY_REG, 1), row_axes, ROW_GROUPS)
-    src_pot = -ENTROPY_REG * (lse - log_total)
-    scores = (src_pot.reshape(tile_rows, 1) - cost) / ENTROPY_REG
-    lse = exchange(local_lse(scores, 0), col_axes, COL_GROUPS)
-    tgt_pot = -ENTROPY_REG * (lse - log_total)
-
-    def weights():
-        total = src_pot.reshape(tile_rows, 1) + tgt_pot.reshape(1, tile_cols) - cost
-        return jnp.exp(total / ENTROPY_REG)
-
-    for iteration in range(1, ITERS):
-        row_sums = gather_lanes(jnp.sum(weights(), axis=1), row_axes, ROW_GROUPS)
-        row_sums = jnp.sum(row_sums, axis=0)
-        src_pot = src_pot - ENTROPY_REG * (jnp.log(row_sums) - log_total)
+    tgt_pot = jnp.zeros((tile_cols,), jnp.float32)
+    for iteration in range(ITERS):
+        scores = (tgt_pot.reshape(1, tile_cols) - cost) / ENTROPY_REG
+        lse = exchange(local_lse(scores, 1), row_axes, ROW_GROUPS)
+        src_pot = -ENTROPY_REG * (lse - log_total)
         if iteration < ITERS - 1:
-            col_sums = gather_lanes(jnp.sum(weights(), axis=0), col_axes, COL_GROUPS)
-            col_sums = jnp.sum(col_sums, axis=0)
-            tgt_pot = tgt_pot - ENTROPY_REG * (jnp.log(col_sums) - log_total)
+            scores = (src_pot.reshape(tile_rows, 1) - cost) / ENTROPY_REG
+            lse = exchange(local_lse(scores, 0), col_axes, COL_GROUPS)
+            tgt_pot = -ENTROPY_REG * (lse - log_total)
+
     part = jax.ShapeDtypeStruct(cost.shape, jnp.bfloat16)
     half = jax.ShapeDtypeStruct(mine.shape, jnp.float32)
     lanes = jax.ShapeDtypeStruct(tgt_pot.shape, jnp.float32)
@@ -310,24 +298,29 @@
         weight_kernel, (part, part, lanes), [], src_pot, tgt_pot, cost
     )
     col_sums = gather_lanes(col_sums, col_axes, COL_GROUPS)
-    sent = on_tile(send_kernel, half, [], high, mid, src_block, other)
+    sent, kept = on_tile(
+        pull_kernel, (half, half), [], high, mid, src_block, mine, other
+    )
     came = lax.ppermute(sent, "c", SWAP)
-    tgt_half = on_tile(keep_kernel, half, [], high, mid, src_block, mine, came)
-    tgt_half, col_sums = lax.optimization_barrier((tgt_half, col_sums))
-    tgt_sum = scatter_blocks(tgt_half, ("z", "x"), SIDE_GROUPS)
+    pair = jax.ShapeDtypeStruct((2, rows, width), jnp.float32)
+    pieces = list(on_tile(order_kernel, (pair,) * NZ, [], kept, came))
+    for i, k in enumerate(STEPS):
+        moves = [(place, (place + k) % NZ) for place in range(NZ)]
+        pieces[i] = lax.ppermute(pieces[i], "z", moves)
+    pieces[0], col_sums = lax.optimization_barrier((pieces[0], col_sums))
+    tgt_sum = sum_pieces(pieces, b)
     col_sums = jnp.sum(col_sums, axis=0)
     tgt_pot = tgt_pot - ENTROPY_REG * (jnp.log(col_sums) - log_total)
-    pair = jax.ShapeDtypeStruct((2, rows, width), jnp.float32)
+    block = jax.ShapeDtypeStruct(src_block.shape, jnp.float32)
     scratch = [
-        pltpu.VMEM(src_block.shape, jnp.float32),
         pltpu.VMEM(mine.shape, jnp.float32),
         pltpu.VMEM((mine.shape[0], LANES), jnp.float32),
     ]
-    pieces = on_tile(
-        push_kernel, (pair,) * NY, scratch,
+    src_part = on_tile(
+        push_kernel, block, scratch,
         high, mid, total_points / col_sums, src_block, mine, other,
     )
-    src_sum = scatter_ring(pieces, a)
+    src_sum = scatter_blocks(src_part, row_axes, ROW_GROUPS)
     src_piece = take(src_pot.reshape(-1, rows), a * NY + y)
     tgt_piece = take(tgt_pot.reshape(-1, rows), (c * 2 + b) * NZ + z)
     col_sum = take(col_sums.reshape(-1, rows), (c * 2 + b) * NZ + z)

time: 244 us -> 251 us (1.029); the launches traced: 240 us -> 249 us
  blocking collectives: 88.6 us -> 101 us
  waiting for transfers between devices: 31.5 us -> 26 us
    all_to_all x4 -> x5, blocking collectives: 62.8 us -> 75.3 us  [all_to_all(): lax.all_to_all(blocks, axes, split_axis=0, concat_axis=0, axis_index_grou...]
    all_to_all x4 -> x3, waiting for transfers between devices: 12 us -> 0.01 us  [all_to_all(): lax.all_to_all(blocks, axes, split_axis=0, concat_axis=0, axis_index_grou...]
    ppermute x8, waiting for transfers between devices: 8.87 us -> 15.3 us  [the longest x7 13 us: per_device(): pieces[i] = lax.ppermute(pieces[i], 'z', moves)]
    ppermute x8, starting transfers between devices: 31.9 us -> 36.1 us  [the longest x7 32.7 us: per_device(): pieces[i] = lax.ppermute(pieces[i], 'z', moves)]
    all_to_all x4 -> x3, starting transfers between devices: 25.7 us -> 21.6 us  [all_to_all(): lax.all_to_all(blocks, axes, split_axis=0, concat_axis=0, axis_index_grou...]
    reduce_sum x5 -> x0, other arithmetic: 3.98 us -> none  [the longest x2 3.23 us: per_device(): row_sums = gather_lanes(jnp.sum(weights(), axis=1), row_axes, ROW_GROUPS)]
    unnamed x62 -> x48, local copies, waits for them, and re-layouts: 12.1 us -> 14.3 us
  transfers between devices with their start and end apart: 15 -> 14, of which waited for: 7 -> 6; matrix products, arithmetic and copies ran while one was open for 2% -> 2% of each run, Pallas kernels for 7% -> 3%
where the time goes in v9:
time: 251 us; the launch traced here: 249 us
  blocking collectives  101 us (40%)
  starting transfers between devices  65.8 us (26%)
  waiting for transfers between devices  26 us (10%)
  Pallas kernels  25.6 us (10%)
  local copies, waits for them, and re-layouts  17.9 us (7%)
  other arithmetic  11.7 us (5%)
    all_to_all x5, blocking collectives, all_to_all(): lax.all_to_all(blocks, axes, split_axis=0, concat_axis=0, axis_index_grou...  75.3 us
    ppermute x7, starting transfers between devices, per_device(): pieces[i] = lax.ppermute(pieces[i], 'z', moves)  32.7 us
    all_gather x1, blocking collectives, per_device(): near = lax.all_gather(src_emb, 'y', axis=0, tiled=True)  25.7 us
    all_to_all x3, starting transfers between devices, all_to_all(): lax.all_to_all(blocks, axes, split_axis=0, concat_axis=0, axis_index_grou...  21.6 us
    pallas_call x4, Pallas kernels, on_tile(): pl.pallas_call(kernel, out_shape=out_shape, in_specs=[WHOLE] * len(args),...  16.1 us
    unnamed x48, local copies, waits for them, and re-layouts  14.3 us
    ppermute x7, waiting for transfers between devices, per_device(): pieces[i] = lax.ppermute(pieces[i], 'z', moves)  13 us
    ppermute x1, waiting for transfers between devices, per_device(): far = lax.ppermute(near, 'x', FLIP_A)  10.7 us
  transfers between devices with their start and end apart: 14, of which 6 were waited for; matrix products, arithmetic and copies ran while one was open for 2% of the time, Pallas kernels for 3%

profile of v9, /device:TPU:56, one launch (start us, length us, event | category | flops | bytes accessed | tf_op | source)
XLA Modules:
  0.0 249.3 jit_solution(14208605258604403636)
XLA Ops:
  2.8 11.4 %all-to-all-start = ((f32[16,40,512]{2,1,0:T(8,128)}), f32[16,40,512]{2,1,0:T(8,128)}, u32[]{:S(2)}, u32[]{:S(2)}) async-start(f32[16,40,512]{2,1,0:T(8,128)} %broadcast_in_dim.14), calls=%async_computation | async-start | bytes 2621440 | tf_op jit(solution)/shard_map/all_to_all | solution.py:39
  14.2 25.7 %all_gather.3.refs_0_ = f32[320,512]{1,0:T(8,128)S(1)} all-gather(f32[40,512]{1,0:T(8,128)S(1)} %copy-done.21), channel_id=1, replica_groups=mesh['z'=8,'x'=4,'y'=8,'c'=2] {'y'}, dimensions={0}, use_global_device_ids=true | all-gather | bytes 737280 | tf_op jit(solution)/shard_map/all_gather | solution.py:277
  39.9 4.0 %collective-permute-start = (f32[320,512]{1,0:T(8,128)S(1)}, f32[320,512]{1,0:T(8,128)S(1)}, u32[]{:S(2)}, u32[]{:S(2)}) collective-permute-start(f32[320,512]{1,0:T(8,128)S(1)} %all_gather.3.refs_0_), channel_id=1, source_target_pairs={{0,48},{16,32},{32,16},{48,0},{1,49},{17,33},{33,17},{49,1},{2,50}... | collective-permute-start | bytes 1966088 | tf_op jit(solution)/shard_map/ppermute | solution.py:278
  44.8 10.7 %collective-permute-done.refs_1_ = f32[320,512]{1,0:T(8,128)S(1)} collective-permute-done((f32[320,512]{1,0:T(8,128)S(1)}, f32[320,512]{1,0:T(8,128)S(1)}, u32[]{:S(2)}, u32[]{:S(2)}) %collective-permute-start) | collective-permute-done | bytes 655392 | tf_op jit(solution)/shard_map/ppermute | solution.py:278
  60.4 5.4 %shard_map.57 = (f32[640,512]{1,0:T(8,128)S(1)}, bf16[640,512]{1,0:T(8,128)(2,1)S(1)}, bf16[640,512]{1,0:T(8,128)(2,1)S(1)}, bf16[640,512]{1,0:T(8,128)(2,1)S(1)...) custom-call(f32[320,512]{1,0:T(8,128)S(1)} %copy-done.12, f32[320,512]{1,0:T(8,128)S(1)} %copy-done.16, ...), custom_call_target="tpu_custom_call" | custom-call | tf_op jit(solution)/shard_map/pallas_call | solution.py:137
  65.9 4.1 %shard_map.58.cost_ref = f32[640,1280]{1,0:T(8,128)S(1)} custom-call(bf16[640,512]{1,0:T(8,128)(2,1)S(1)} %get-tuple-element.29.high_ref, bf16[640,512]{1,0:T(8,128)(2,1)S(1)} %get-tuple-element.30.mid_ref, bf16[640,512]{1,0:T(8,128)(2,1)S(1)} %get-tuple-element.31.low_ref, f32[640,1]{1,0:T(8,128)S(1)} %get-tuple-element.32.sq_ref, ...), custom_call_target="tpu_custom_call", output_to_operand_aliasing={{}: (5, {})} | custom-call | tf_op jit(solution)/shard_map/pallas_call | solution.py:158
  71.2 15.6 %all_to_all.40 = f32[16,5,128]{2,1,0:T(8,128)S(1)} all-to-all(f32[16,5,128]{2,1,0:T(8,128)S(1)} %broadcast_in_dim.15), channel_id=1, replica_groups={{0,2,4,6,8,10,12,14,48,50,52,54,56,58,60,62},{16,18,20,22,24,26,28,30,3..., dimensions={0} | all-to-all | bytes 81920 | tf_op jit(solution)/shard_map/all_to_all | solution.py:39
  88.0 19.5 %all_to_all.41 = f32[32,10,128]{2,1,0:T(8,128)S(1)} all-to-all(f32[32,10,128]{2,1,0:T(8,128)S(1)} %broadcast_in_dim.16), channel_id=1, replica_groups={{0,1,16,17,64,65,80,81,128,129,144,145,192,193,208,209,256,257,272,273,..., dimensions={0} | all-to-all | bytes 327680 | tf_op jit(solution)/shard_map/all_to_all | solution.py:39
  110.2 12.7 %all_to_all.42 = f32[16,5,128]{2,1,0:T(8,128)S(1)} all-to-all(f32[16,5,128]{2,1,0:T(8,128)S(1)} %broadcast_in_dim.17), channel_id=1, replica_groups={{0,2,4,6,8,10,12,14,48,50,52,54,56,58,60,62},{16,18,20,22,24,26,28,30,3..., dimensions={0} | all-to-all | bytes 81920 | tf_op jit(solution)/shard_map/all_to_all | solution.py:39
  124.1 15.2 %all_to_all.43 = f32[32,10,128]{2,1,0:T(8,128)S(1)} all-to-all(f32[32,10,128]{2,1,0:T(8,128)S(1)} %broadcast_in_dim.18), channel_id=1, replica_groups={{0,1,16,17,64,65,80,81,128,129,144,145,192,193,208,209,256,257,272,273,..., dimensions={0} | all-to-all | bytes 327680 | tf_op jit(solution)/shard_map/all_to_all | solution.py:39
  142.0 12.2 %all_to_all.44 = f32[16,5,128]{2,1,0:T(8,128)S(1)} all-to-all(f32[16,5,128]{2,1,0:T(8,128)S(1)} %broadcast_in_dim.19), channel_id=1, replica_groups={{0,2,4,6,8,10,12,14,48,50,52,54,56,58,60,62},{16,18,20,22,24,26,28,30,3..., dimensions={0} | all-to-all | bytes 81920 | tf_op jit(solution)/shard_map/all_to_all | solution.py:39
  156.0 6.5 %shard_map.60 = (f32[640,512]{1,0:T(8,128)}, f32[640,512]{1,0:T(8,128)S(1)}) custom-call(bf16[640,1280]{1,0:T(8,128)(2,1)S(1)} %get-tuple-element.34.high_ref, bf16[640,1280]{1,0:T(8,128)(2,1)S(1)} %get-tuple-element.35.mid_ref, f32[640,512]{1,0:T(8,128)S(1)} %copy-done.8, f32[640,512]{1,0:T(8,128)} %bitcast.refs_2_.mine_ref, f32[640,512]{1,0:T(8,128)S(1)} %copy-done.1), custom_call_target="tpu_custom_call" | custom-call | tf_op jit(solution)/shard_map/pallas_call | solution.py:241
  166.5 4.6 %all-to-all-start.6 = ((f32[32,10,128]{2,1,0:T(8,128)}), f32[32,10,128]{2,1,0:T(8,128)}, u32[]{:S(2)}, u32[]{:S(2)}) async-start(f32[32,10,128]{2,1,0:T(8,128)} %broadcast_in_dim.20), calls=%async_computation.6 | async-start | bytes 524288 | tf_op jit(solution)/shard_map/all_to_all | solution.py:39
  177.2 7.7 %collective-permute-start.3 = (f32[2,40,512]{2,1,0:T(8,128)}, f32[2,40,512]{2,1,0:T(8,128)}, u32[]{:S(2)}, u32[]{:S(2)}) collective-permute-start(f32[2,40,512]{2,1,0:T(8,128)} %get-tuple-element.39), channel_id=1, source_target_pairs={{0,256},{64,320},{128,384},{192,448},{256,0},{320,64},{384,128},{4... | collective-permute-start | bytes 491528 | tf_op jit(solution)/shard_map/ppermute | solution.py:309
  184.9 6.7 %collective-permute-done.3 = f32[2,40,512]{2,1,0:T(8,128)} collective-permute-done((f32[2,40,512]{2,1,0:T(8,128)}, f32[2,40,512]{2,1,0:T(8,128)}, u32[]{:S(2)}, u32[]{:S(2)}) %collective-permute-start.3) | collective-permute-done | bytes 163872 | tf_op jit(solution)/shard_map/ppermute | solution.py:309
  195.5 6.2 %shard_map.62 = f32[640,512]{1,0:T(8,128)S(1)} custom-call(bf16[640,1280]{1,0:T(8,128)(2,1)S(1)} %copy-done.4, bf16[640,1280]{1,0:T(8,128)(2,1)S(1)} %copy-done.6, f32[10,128]{1,0:T(8,128)S(1)} %broadcast_divide_fusion.scale_ref, f32[640,512]{1,0:T(8,128)S(1)} %copy-done.9, f32[640,512]{1,0:T(8,128)} %bitcast.refs_2_.mine_ref, f32[640,512]{1,0:T(8,128)S(1)} %copy-done.2), custom_call_target="tpu_custom_call" | custom-call | tf_op jit(solution)/shard_map/pallas_call | solution.py:241
  202.7 5.6 %all-to-all-start.7 = ((f32[16,40,512]{2,1,0:T(8,128)}), f32[16,40,512]{2,1,0:T(8,128)S(1)}, u32[]{:S(2)}, u32[]{:S(2)}) async-start(f32[16,40,512]{2,1,0:T(8,128)} %bitcast.31), calls=%async_computation.7 | async-start | bytes 2621440 | tf_op jit(solution)/shard_map/all_to_all | solution.py:39
  208.3 5.4 %collective-permute-start.4 = (f32[2,40,512]{2,1,0:T(8,128)}, f32[2,40,512]{2,1,0:T(8,128)S(1)}, u32[]{:S(2)}, u32[]{:S(2)}) collective-permute-start(f32[2,40,512]{2,1,0:T(8,128)} %copy-done.20), channel_id=1, source_target_pairs={{0,192},{64,256},{128,320},{192,384},{256,448},{320,0},{384,64},{4... | collective-permute-start | bytes 491528 | tf_op jit(solution)/shard_map/ppermute | solution.py:309
  213.7 4.6 %collective-permute-start.5 = (f32[2,40,512]{2,1,0:T(8,128)}, f32[2,40,512]{2,1,0:T(8,128)S(1)}, u32[]{:S(2)}, u32[]{:S(2)}) collective-permute-start(f32[2,40,512]{2,1,0:T(8,128)} %copy-done.19), channel_id=1, source_target_pairs={{0,320},{64,384},{128,448},{192,0},{256,64},{320,128},{384,192},{4... | collective-permute-start | bytes 491528 | tf_op jit(solution)/shard_map/ppermute | solution.py:309
  218.3 4.7 %collective-permute-start.6 = (f32[2,40,512]{2,1,0:T(8,128)}, f32[2,40,512]{2,1,0:T(8,128)S(1)}, u32[]{:S(2)}, u32[]{:S(2)}) collective-permute-start(f32[2,40,512]{2,1,0:T(8,128)} %copy-done.18), channel_id=1, source_target_pairs={{0,128},{64,192},{128,256},{192,320},{256,384},{320,448},{384,0},{... | collective-permute-start | bytes 491528 | tf_op jit(solution)/shard_map/ppermute | solution.py:309
  226.3 3.4 %collective-permute-start.8 = (f32[2,40,512]{2,1,0:T(8,128)S(1)}, f32[2,40,512]{2,1,0:T(8,128)S(1)}, u32[]{:S(2)}, u32[]{:S(2)}) collective-permute-start(f32[2,40,512]{2,1,0:T(8,128)S(1)} %get-tuple-element.47), channel_id=1, source_target_pairs={{0,64},{64,128},{128,192},{192,256},{256,320},{320,384},{384,448},... | collective-permute-start | bytes 491528 | tf_op jit(solution)/shard_map/ppermute | solution.py:309
  229.7 3.7 %collective-permute-start.9 = (f32[2,40,512]{2,1,0:T(8,128)S(1)}, f32[2,40,512]{2,1,0:T(8,128)S(1)}, u32[]{:S(2)}, u32[]{:S(2)}) collective-permute-start(f32[2,40,512]{2,1,0:T(8,128)S(1)} %get-tuple-element.48), channel_id=1, source_target_pairs={{0,448},{64,0},{128,64},{192,128},{256,192},{320,256},{384,320},{4... | collective-permute-start | bytes 491528 | tf_op jit(solution)/shard_map/ppermute | solution.py:309
  234.2 3.6 %collective-permute-done.7 = f32[2,40,512]{2,1,0:T(8,128)S(1)} collective-permute-done((f32[2,40,512]{2,1,0:T(8,128)}, f32[2,40,512]{2,1,0:T(8,128)S(1)}, u32[]{:S(2)}, u32[]{:S(2)}) %collective-permute-start.7) | collective-permute-done | bytes 163872 | tf_op jit(solution)/shard_map/ppermute | solution.py:309
  241.5 3.4 %collective-permute-start.10 = (f32[40,512]{1,0:T(8,128)S(1)}, f32[40,512]{1,0:T(8,128)S(1)}, u32[]{:S(2)}, u32[]{:S(2)}) collective-permute-start(f32[40,512]{1,0:T(8,128)S(1)} %dynamic-slice_bitcast_fusion), channel_id=1, source_target_pairs={{0,16},{16,0},{32,48},{48,32},{1,17},{17,1},{33,49},{49,33},{2,18}... | collective-permute-start | bytes 245768 | tf_op jit(solution)/shard_map/ppermute | solution.py:58
  (113 shorter events, 45.4 us)
Async XLA Ops:
  0.6 13.6 %copy-start.21 = (f32[40,512]{1,0:T(8,128)S(1)}, f32[40,512]{1,0:T(8,128)}, u32[]{:S(2)}) copy-start(f32[40,512]{1,0:T(8,128)} %param.2) | copy-start | bytes 245764
  2.8 53.5 %all-to-all-start = ((f32[16,40,512]{2,1,0:T(8,128)}), f32[16,40,512]{2,1,0:T(8,128)}, u32[]{:S(2)}, u32[]{:S(2)}) async-start(f32[16,40,512]{2,1,0:T(8,128)} %broadcast_in_dim.14), calls=%async_computation | async-start | bytes 2621440 | tf_op jit(solution)/shard_map/all_to_all | solution.py:39
  39.9 15.6 %collective-permute-start = (f32[320,512]{1,0:T(8,128)S(1)}, f32[320,512]{1,0:T(8,128)S(1)}, u32[]{:S(2)}, u32[]{:S(2)}) collective-permute-start(f32[320,512]{1,0:T(8,128)S(1)} %all_gather.3.refs_0_), channel_id=1, source_target_pairs={{0,48},{16,32},{32,16},{48,0},{1,49},{17,33},{33,17},{49,1},{2,50}... | collective-permute-start | bytes 1966088 | tf_op jit(solution)/shard_map/ppermute | solution.py:278
  56.3 9.5 %collective-permute-start.1 = (f32[640,512]{1,0:T(8,128)}, f32[640,512]{1,0:T(8,128)S(1)}, u32[]{:S(2)}, u32[]{:S(2)}) collective-permute-start(f32[640,512]{1,0:T(8,128)} %bitcast.refs_2_.mine_ref), channel_id=1, source_target_pairs={{0,1},{1,0},{2,3},{3,2},{4,5},{5,4},{6,7},{7,6},{8,9},{9,8},{10,11... | collective-permute-start | bytes 3932168 | tf_op jit(solution)/shard_map/ppermute | solution.py:157
  65.8 4.1 %copy-start.7 = (f32[640,512]{1,0:T(8,128)}, f32[640,512]{1,0:T(8,128)S(1)}, u32[]{:S(2)}) copy-start(f32[640,512]{1,0:T(8,128)S(1)} %get-tuple-element.36.src_ref) | copy-start | bytes 3932164
  65.9 4.1 %copy-start = (f32[640,512]{1,0:T(8,128)}, f32[640,512]{1,0:T(8,128)S(1)}, u32[]{:S(2)}) copy-start(f32[640,512]{1,0:T(8,128)S(1)} %collective-permute-done.1.other_ref) | copy-start | bytes 3932164
  154.2 1.4 copy-start.1
  154.3 1.7 copy-start.8
  155.6 6.9 %copy-start.3 = (bf16[640,1280]{1,0:T(8,128)(2,1)}, bf16[640,1280]{1,0:T(8,128)(2,1)S(1)}, u32[]{:S(2)}) copy-start(bf16[640,1280]{1,0:T(8,128)(2,1)S(1)} %get-tuple-element.34.high_ref) | copy-start | bytes 4915204
  155.6 6.9 %copy-start.5 = (bf16[640,1280]{1,0:T(8,128)(2,1)}, bf16[640,1280]{1,0:T(8,128)(2,1)S(1)}, u32[]{:S(2)}) copy-start(bf16[640,1280]{1,0:T(8,128)(2,1)S(1)} %get-tuple-element.35.mid_ref) | copy-start | bytes 4915204
  163.6 29.1 %copy-start.2 = (f32[640,512]{1,0:T(8,128)S(1)}, f32[640,512]{1,0:T(8,128)}, u32[]{:S(2)}) copy-start(f32[640,512]{1,0:T(8,128)} %copy-done) | copy-start | bytes 3932164
  163.6 29.1 %copy-start.4 = (bf16[640,1280]{1,0:T(8,128)(2,1)S(1)}, bf16[640,1280]{1,0:T(8,128)(2,1)}, u32[]{:S(2)}) copy-start(bf16[640,1280]{1,0:T(8,128)(2,1)} %copy-done.3) | copy-start | bytes 4915204
  163.6 7.5 %collective-permute-start.2 = (f32[640,512]{1,0:T(8,128)}, f32[640,512]{1,0:T(8,128)}, u32[]{:S(2)}, u32[]{:S(2)}) collective-permute-start(f32[640,512]{1,0:T(8,128)} %get-tuple-element.38), channel_id=1, source_target_pairs={{0,1},{1,0},{2,3},{3,2},{4,5},{5,4},{6,7},{7,6},{8,9},{9,8},{10,11... | collective-permute-start | bytes 3932168 | tf_op jit(solution)/shard_map/ppermute | solution.py:304
  166.5 18.4 %all-to-all-start.6 = ((f32[32,10,128]{2,1,0:T(8,128)}), f32[32,10,128]{2,1,0:T(8,128)}, u32[]{:S(2)}, u32[]{:S(2)}) async-start(f32[32,10,128]{2,1,0:T(8,128)} %broadcast_in_dim.20), calls=%async_computation.6 | async-start | bytes 524288 | tf_op jit(solution)/shard_map/all_to_all | solution.py:39
  177.2 14.5 %collective-permute-start.3 = (f32[2,40,512]{2,1,0:T(8,128)}, f32[2,40,512]{2,1,0:T(8,128)}, u32[]{:S(2)}, u32[]{:S(2)}) collective-permute-start(f32[2,40,512]{2,1,0:T(8,128)} %get-tuple-element.39), channel_id=1, source_target_pairs={{0,256},{64,320},{128,384},{192,448},{256,0},{320,64},{384,128},{4... | collective-permute-start | bytes 491528 | tf_op jit(solution)/shard_map/ppermute | solution.py:309
  192.7 1.4 copy-start.6
  202.7 45.8 %all-to-all-start.7 = ((f32[16,40,512]{2,1,0:T(8,128)}), f32[16,40,512]{2,1,0:T(8,128)S(1)}, u32[]{:S(2)}, u32[]{:S(2)}) async-start(f32[16,40,512]{2,1,0:T(8,128)} %bitcast.31), calls=%async_computation.7 | async-start | bytes 2621440 | tf_op jit(solution)/shard_map/all_to_all | solution.py:39
  208.3 21.3 %collective-permute-start.4 = (f32[2,40,512]{2,1,0:T(8,128)}, f32[2,40,512]{2,1,0:T(8,128)S(1)}, u32[]{:S(2)}, u32[]{:S(2)}) collective-permute-start(f32[2,40,512]{2,1,0:T(8,128)} %copy-done.20), channel_id=1, source_target_pairs={{0,192},{64,256},{128,320},{192,384},{256,448},{320,0},{384,64},{4... | collective-permute-start | bytes 491528 | tf_op jit(solution)/shard_map/ppermute | solution.py:309
  213.7 20.4 %collective-permute-start.5 = (f32[2,40,512]{2,1,0:T(8,128)}, f32[2,40,512]{2,1,0:T(8,128)S(1)}, u32[]{:S(2)}, u32[]{:S(2)}) collective-permute-start(f32[2,40,512]{2,1,0:T(8,128)} %copy-done.19), channel_id=1, source_target_pairs={{0,320},{64,384},{128,448},{192,0},{256,64},{320,128},{384,192},{4... | collective-permute-start | bytes 491528 | tf_op jit(solution)/shard_map/ppermute | solution.py:309
  218.3 15.9 %collective-permute-start.6 = (f32[2,40,512]{2,1,0:T(8,128)}, f32[2,40,512]{2,1,0:T(8,128)S(1)}, u32[]{:S(2)}, u32[]{:S(2)}) collective-permute-start(f32[2,40,512]{2,1,0:T(8,128)} %copy-done.18), channel_id=1, source_target_pairs={{0,128},{64,192},{128,256},{192,320},{256,384},{320,448},{384,0},{... | collective-permute-start | bytes 491528 | tf_op jit(solution)/shard_map/ppermute | solution.py:309
  223.0 14.8 %collective-permute-start.7 = (f32[2,40,512]{2,1,0:T(8,128)}, f32[2,40,512]{2,1,0:T(8,128)S(1)}, u32[]{:S(2)}, u32[]{:S(2)}) collective-permute-start(f32[2,40,512]{2,1,0:T(8,128)} %copy-done.17), channel_id=1, source_target_pairs={{0,384},{64,448},{128,0},{192,64},{256,128},{320,192},{384,256},{4... | collective-permute-start | bytes 491528 | tf_op jit(solution)/shard_map/ppermute | solution.py:309
  226.3 12.0 %collective-permute-start.8 = (f32[2,40,512]{2,1,0:T(8,128)S(1)}, f32[2,40,512]{2,1,0:T(8,128)S(1)}, u32[]{:S(2)}, u32[]{:S(2)}) collective-permute-start(f32[2,40,512]{2,1,0:T(8,128)S(1)} %get-tuple-element.47), channel_id=1, source_target_pairs={{0,64},{64,128},{128,192},{192,256},{256,320},{320,384},{384,448},... | collective-permute-start | bytes 491528 | tf_op jit(solution)/shard_map/ppermute | solution.py:309
  229.7 10.7 %collective-permute-start.9 = (f32[2,40,512]{2,1,0:T(8,128)S(1)}, f32[2,40,512]{2,1,0:T(8,128)S(1)}, u32[]{:S(2)}, u32[]{:S(2)}) collective-permute-start(f32[2,40,512]{2,1,0:T(8,128)S(1)} %get-tuple-element.48), channel_id=1, source_target_pairs={{0,448},{64,0},{128,64},{192,128},{256,192},{320,256},{384,320},{4... | collective-permute-start | bytes 491528 | tf_op jit(solution)/shard_map/ppermute | solution.py:309
  241.5 6.3 %collective-permute-start.10 = (f32[40,512]{1,0:T(8,128)S(1)}, f32[40,512]{1,0:T(8,128)S(1)}, u32[]{:S(2)}, u32[]{:S(2)}) collective-permute-start(f32[40,512]{1,0:T(8,128)S(1)} %dynamic-slice_bitcast_fusion), channel_id=1, source_target_pairs={{0,16},{16,0},{32,48},{48,32},{1,17},{17,1},{33,49},{49,33},{2,18}... | collective-permute-start | bytes 245768 | tf_op jit(solution)/shard_map/ppermute | solution.py:58
  (14 other events, 12.5 us)

commit v10 on v7

--- a/solution.py
+++ b/solution.py
@@ -196,12 +196,12 @@
     lane = lax.broadcasted_iota(jnp.int32, (LANES, LANES), 1)
     sub = lax.broadcasted_iota(jnp.int32, (LANES, LANES), 0)
     for i in range(rows // LANES):
-        row = jnp.broadcast_to(src_pot_ref[i : i + 1, :], (LANES, LANES))
+        at = slice(i * LANES, (i + 1) * LANES)
+        row = jnp.broadcast_to(src_pot_ref[:, at], (LANES, LANES))
         column = jnp.sum(jnp.where(lane == sub, row, 0.0), axis=1, keepdims=True)
-        at = slice(i * LANES, (i + 1) * LANES)
         for j in range(cols // LANES):
             to = slice(j * LANES, (j + 1) * LANES)
-            total = column + tgt_pot_ref[j : j + 1, :] - cost_ref[at, to]
+            total = column + tgt_pot_ref[:, to] - cost_ref[at, to]
             weight = jnp.exp(total / ENTROPY_REG)
             high = weight.astype(jnp.bfloat16)
             high_ref[at, to] = high
@@ -247,10 +247,8 @@
 
 
 def exchange(local, axes, groups, count):
-    size = local.shape[0]
-    flat = local.reshape(1, size // LANES, LANES)
-    sent = jnp.broadcast_to(flat, (count, size // LANES, LANES))
-    got = all_to_all(sent, axes, groups)
+    flat = local.reshape(1, 1, local.size)
+    got = all_to_all(jnp.broadcast_to(flat, (count, 1, local.size)), axes, groups)
     peak = jnp.max(got, axis=0)
     total = jnp.sum(jnp.exp(got - peak[None]), axis=0)
     return peak + jnp.log(total)

time: 242 us -> 237 us (0.979)
  blocking collectives: 116 us -> 96.4 us
  waiting for transfers between devices: 30 us -> 39.8 us
  starting transfers between devices: 50.4 us -> 54.4 us
    all_to_all x6 -> x5, blocking collectives: 90.3 us -> 70.7 us  [all_to_all(): lax.all_to_all(blocks, axes, split_axis=0, concat_axis=0, axis_index_grou...]
    all_to_all x2 -> x3, waiting for transfers between devices: 0.01 us -> 10.3 us  [all_to_all(): lax.all_to_all(blocks, axes, split_axis=0, concat_axis=0, axis_index_grou...]
    all_to_all x2 -> x3, starting transfers between devices: 15.1 us -> 19 us  [all_to_all(): lax.all_to_all(blocks, axes, split_axis=0, concat_axis=0, axis_index_grou...]
  transfers between devices with their start and end apart: 13 -> 14, of which waited for: 5 -> 6; matrix products, arithmetic and copies ran while one was open for 1% -> 1% of each run, Pallas kernels for 5% -> 5%
where the time goes in v10:
time: 237 us; the launch traced here: 235 us
  blocking collectives  96.4 us (41%)
  starting transfers between devices  54.4 us (23%)
  waiting for transfers between devices  39.8 us (17%)
  Pallas kernels  23.4 us (10%)
  local copies, waits for them, and re-layouts  10.9 us (5%)
  other arithmetic  9.14 us (4%)
    all_to_all x5, blocking collectives, all_to_all(): lax.all_to_all(blocks, axes, split_axis=0, concat_axis=0, axis_index_grou...  70.7 us
    all_gather x1, blocking collectives, per_device(): near = lax.all_gather(src_emb, 'y', axis=0, tiled=True)  25.7 us
    ppermute x7, starting transfers between devices, scatter_ring(): total = total + lax.ppermute(piece, 'y', moves)  24.8 us
    all_to_all x3, starting transfers between devices, all_to_all(): lax.all_to_all(blocks, axes, split_axis=0, concat_axis=0, axis_index_grou...  19 us
    ppermute x7, waiting for transfers between devices, scatter_ring(): total = total + lax.ppermute(piece, 'y', moves)  14.4 us
    ppermute x1, waiting for transfers between devices, per_device(): far = lax.ppermute(near, 'x', FLIP_A)  10.7 us
    pallas_call x2, Pallas kernels, on_tile(): pl.pallas_call(kernel, out_shape=out_shape, in_specs=[WHOLE] * len(args),...  10.4 us
    all_to_all x3, waiting for transfers between devices, all_to_all(): lax.all_to_all(blocks, axes, split_axis=0, concat_axis=0, axis_index_grou...  10.3 us
  transfers between devices with their start and end apart: 14, of which 6 were waited for; matrix products, arithmetic and copies ran while one was open for 1% of the time, Pallas kernels for 5%

profile of v10, /device:TPU:56, one launch (start us, length us, event | category | flops | bytes accessed | tf_op | source)
XLA Modules:
  0.0 235.2 jit_solution(14213818121406032292)
XLA Ops:
  2.8 11.4 %all-to-all-start = ((f32[16,40,512]{2,1,0:T(8,128)}), f32[16,40,512]{2,1,0:T(8,128)}, u32[]{:S(2)}, u32[]{:S(2)}) async-start(f32[16,40,512]{2,1,0:T(8,128)} %broadcast_in_dim.14), calls=%async_computation | async-start | bytes 2621440 | tf_op jit(solution)/shard_map/all_to_all | solution.py:39
  14.2 25.7 %all_gather.3.refs_0_ = f32[320,512]{1,0:T(8,128)S(1)} all-gather(f32[40,512]{1,0:T(8,128)S(1)} %copy-done.10), channel_id=1, replica_groups=mesh['z'=8,'x'=4,'y'=8,'c'=2] {'y'}, dimensions={0}, use_global_device_ids=true | all-gather | bytes 737280 | tf_op jit(solution)/shard_map/all_gather | solution.py:270
  39.9 4.0 %collective-permute-start = (f32[320,512]{1,0:T(8,128)S(1)}, f32[320,512]{1,0:T(8,128)S(1)}, u32[]{:S(2)}, u32[]{:S(2)}) collective-permute-start(f32[320,512]{1,0:T(8,128)S(1)} %all_gather.3.refs_0_), channel_id=1, source_target_pairs={{0,48},{16,32},{32,16},{48,0},{1,49},{17,33},{33,17},{49,1},{2,50}... | collective-permute-start | bytes 1966088 | tf_op jit(solution)/shard_map/ppermute | solution.py:271
  44.8 10.7 %collective-permute-done.refs_1_ = f32[320,512]{1,0:T(8,128)S(1)} collective-permute-done((f32[320,512]{1,0:T(8,128)S(1)}, f32[320,512]{1,0:T(8,128)S(1)}, u32[]{:S(2)}, u32[]{:S(2)}) %collective-permute-start) | collective-permute-done | bytes 655392 | tf_op jit(solution)/shard_map/ppermute | solution.py:271
  60.4 5.4 %shard_map.57 = (f32[640,512]{1,0:T(8,128)S(1)}, bf16[640,512]{1,0:T(8,128)(2,1)S(1)}, bf16[640,512]{1,0:T(8,128)(2,1)S(1)}, bf16[640,512]{1,0:T(8,128)(2,1)S(1)...) custom-call(f32[320,512]{1,0:T(8,128)S(1)} %copy-done.7, f32[320,512]{1,0:T(8,128)S(1)} %copy-done.9, ...), custom_call_target="tpu_custom_call" | custom-call | tf_op jit(solution)/shard_map/pallas_call | solution.py:140
  65.9 4.0 %shard_map.58.cost_ref = f32[640,1280]{1,0:T(8,128)S(1)} custom-call(bf16[640,512]{1,0:T(8,128)(2,1)S(1)} %get-tuple-element.27.high_ref, bf16[640,512]{1,0:T(8,128)(2,1)S(1)} %get-tuple-element.28.mid_ref, bf16[640,512]{1,0:T(8,128)(2,1)S(1)} %get-tuple-element.29.low_ref, f32[640,1]{1,0:T(8,128)S(1)} %get-tuple-element.30.sq_ref, ...), custom_call_target="tpu_custom_call", output_to_operand_aliasing={{}: (5, {})} | custom-call | tf_op jit(solution)/shard_map/pallas_call | solution.py:161
  71.1 15.4 %all_to_all.40 = f32[16,1,640]{2,1,0:T(1,128)S(1)} all-to-all(f32[16,1,640]{2,1,0:T(1,128)S(1)} %broadcast_in_dim.15), channel_id=1, replica_groups={{0,2,4,6,8,10,12,14,48,50,52,54,56,58,60,62},{16,18,20,22,24,26,28,30,3..., dimensions={0} | all-to-all | bytes 81920 | tf_op jit(solution)/shard_map/all_to_all | solution.py:39
  87.8 17.5 %all_to_all.41 = f32[32,1,1280]{2,1,0:T(1,128)S(1)} all-to-all(f32[32,1,1280]{2,1,0:T(1,128)S(1)} %broadcast_in_dim.16), channel_id=1, replica_groups={{0,1,16,17,64,65,80,81,128,129,144,145,192,193,208,209,256,257,272,273,..., dimensions={0} | all-to-all | bytes 327680 | tf_op jit(solution)/shard_map/all_to_all | solution.py:39
  106.7 12.4 %all_to_all.42 = f32[16,1,640]{2,1,0:T(1,128)S(1)} all-to-all(f32[16,1,640]{2,1,0:T(1,128)S(1)} %broadcast_in_dim.17), channel_id=1, replica_groups={{0,2,4,6,8,10,12,14,48,50,52,54,56,58,60,62},{16,18,20,22,24,26,28,30,3..., dimensions={0} | all-to-all | bytes 81920 | tf_op jit(solution)/shard_map/all_to_all | solution.py:39
  120.4 13.1 %all_to_all.43 = f32[32,1,1280]{2,1,0:T(1,128)S(1)} all-to-all(f32[32,1,1280]{2,1,0:T(1,128)S(1)} %broadcast_in_dim.18), channel_id=1, replica_groups={{0,1,16,17,64,65,80,81,128,129,144,145,192,193,208,209,256,257,272,273,..., dimensions={0} | all-to-all | bytes 327680 | tf_op jit(solution)/shard_map/all_to_all | solution.py:39
  135.0 12.3 %all_to_all.44 = f32[16,1,640]{2,1,0:T(1,128)S(1)} all-to-all(f32[16,1,640]{2,1,0:T(1,128)S(1)} %broadcast_in_dim.19), channel_id=1, replica_groups={{0,2,4,6,8,10,12,14,48,50,52,54,56,58,60,62},{16,18,20,22,24,26,28,30,3..., dimensions={0} | all-to-all | bytes 81920 | tf_op jit(solution)/shard_map/all_to_all | solution.py:39
  149.2 3.9 %all-to-all-start.6 = ((f32[32,1,1280]{2,1,0:T(1,128)}), f32[32,1,1280]{2,1,0:T(1,128)S(1)}, u32[]{:S(2)}, u32[]{:S(2)}) async-start(f32[32,1,1280]{2,1,0:T(1,128)} %broadcast_in_dim.20), calls=%async_computation.6 | async-start | bytes 327680 | tf_op jit(solution)/shard_map/all_to_all | solution.py:39
  153.1 10.3 %all-to-all-done.6 = f32[32,1,1280]{2,1,0:T(1,128)S(1)} async-done(((f32[32,1,1280]{2,1,0:T(1,128)}), f32[32,1,1280]{2,1,0:T(1,128)S(1)}, u32[]{:S(2)}, u32[]{:S(2)}) %all-to-all-start.6) | async-done | bytes 163872 | tf_op jit(solution)/shard_map/all_to_all | solution.py:39
  166.2 3.7 %shard_map.59 = (f32[640,512]{1,0:T(8,128)S(1)}, bf16[640,1280]{1,0:T(8,128)(2,1)S(1)}, bf16[640,1280]{1,0:T(8,128)(2,1)S(1)}) custom-call(f32[1,640]{1,0:T(1,128)S(1)} %mul.68.src_pot_ref, f32[1,1280]{1,0:T(1,128)S(1)} %mul.69.tgt_pot_ref, f32[640,1280]{1,0:T(8,128)S(1)} %shard_map.58.cost_ref, f32[640,512]{1,0:T(8,128)S(1)} %copy-done.4, ...), custom_call_target="tpu_custom_call" | custom-call | tf_op jit(solution)/shard_map/pallas_call | solution.py:286
  172.0 5.6 %shard_map.60 = (f32[2,40,512]{2,1,0:T(8,128)S(1)}, f32[2,40,512]{2,1,0:T(8,128)S(1)}, f32[2,40,512]{2,1,0:T(8,128)S(1)}, f32[2,40,512]{2,1,0:T(8,128)S(1)}, f32...) custom-call(bf16[640,1280]{1,0:T(8,128)(2,1)S(1)} %get-tuple-element., ...), custom_call_target="tpu_custom_call" | custom-call | tf_op jit(solution)/shard_map/pallas_call | solution.py:239
  177.7 4.7 %shard_map.61 = f32[640,512]{1,0:T(8,128)} custom-call(bf16[640,1280]{1,0:T(8,128)(2,1)S(1)} %get-tuple-element.33.high_ref, bf16[640,1280]{1,0:T(8,128)(2,1)S(1)} %get-tuple-element.34.mid_ref, f32[640,512]{1,0:T(8,128)S(1)} %copy-done.5, f32[640,512]{1,0:T(8,128)} %bitcast.refs_2_.mine_ref, f32[640,512]{1,0:T(8,128)S(1)} %collective-permute-done.2.came_ref), custom_call_target="tpu_custom_call" | custom-call | tf_op jit(solution)/shard_map/pallas_call | solution.py:239
  182.4 3.7 %all-to-all-start.7 = ((f32[16,40,512]{2,1,0:T(8,128)}), f32[16,40,512]{2,1,0:T(8,128)S(1)}, u32[]{:S(2)}, u32[]{:S(2)}) async-start(f32[16,40,512]{2,1,0:T(8,128)} %bitcast.5), calls=%async_computation.7 | async-start | bytes 2621440 | tf_op jit(solution)/shard_map/all_to_all | solution.py:39
  186.1 4.5 %collective-permute-start.4 = (f32[2,40,512]{2,1,0:T(8,128)S(1)}, f32[2,40,512]{2,1,0:T(8,128)S(1)}, u32[]{:S(2)}, u32[]{:S(2)}) collective-permute-start(f32[2,40,512]{2,1,0:T(8,128)S(1)} %get-tuple-element.39), channel_id=1, source_target_pairs={{0,6},{2,8},{4,10},{6,12},{8,14},{10,0},{12,2},{14,4},{1,7},{3,9},... | collective-permute-start | bytes 491528 | tf_op jit(solution)/shard_map/ppermute | solution.py:60
  190.6 3.2 %collective-permute-start.5 = (f32[2,40,512]{2,1,0:T(8,128)S(1)}, f32[2,40,512]{2,1,0:T(8,128)S(1)}, u32[]{:S(2)}, u32[]{:S(2)}) collective-permute-start(f32[2,40,512]{2,1,0:T(8,128)S(1)} %get-tuple-element.40), channel_id=1, source_target_pairs={{0,10},{2,12},{4,14},{6,0},{8,2},{10,4},{12,6},{14,8},{1,11},{3,13... | collective-permute-start | bytes 491528 | tf_op jit(solution)/shard_map/ppermute | solution.py:60
  193.8 5.6 %collective-permute-start.6 = (f32[2,40,512]{2,1,0:T(8,128)S(1)}, f32[2,40,512]{2,1,0:T(8,128)S(1)}, u32[]{:S(2)}, u32[]{:S(2)}) collective-permute-start(f32[2,40,512]{2,1,0:T(8,128)S(1)} %get-tuple-element.41), channel_id=1, source_target_pairs={{0,4},{2,6},{4,8},{6,10},{8,12},{10,14},{12,0},{14,2},{1,5},{3,7},... | collective-permute-start | bytes 491528 | tf_op jit(solution)/shard_map/ppermute | solution.py:60
  201.4 5.8 %collective-permute-start.8 = (f32[2,40,512]{2,1,0:T(8,128)S(1)}, f32[2,40,512]{2,1,0:T(8,128)S(1)}, u32[]{:S(2)}, u32[]{:S(2)}) collective-permute-start(f32[2,40,512]{2,1,0:T(8,128)S(1)} %get-tuple-element.43), channel_id=1, source_target_pairs={{0,2},{2,4},{4,6},{6,8},{8,10},{10,12},{12,14},{14,0},{1,3},{3,5},... | collective-permute-start | bytes 491528 | tf_op jit(solution)/shard_map/ppermute | solution.py:60
  213.0 3.1 %collective-permute-done.7 = f32[2,40,512]{2,1,0:T(8,128)S(1)} collective-permute-done((f32[2,40,512]{2,1,0:T(8,128)S(1)}, f32[2,40,512]{2,1,0:T(8,128)S(1)}, u32[]{:S(2)}, u32[]{:S(2)}) %collective-permute-start.7) | collective-permute-done | bytes 163872 | tf_op jit(solution)/shard_map/ppermute | solution.py:60
  216.1 10.1 %collective-permute-done.9 = f32[2,40,512]{2,1,0:T(8,128)S(1)} collective-permute-done((f32[2,40,512]{2,1,0:T(8,128)S(1)}, f32[2,40,512]{2,1,0:T(8,128)S(1)}, u32[]{:S(2)}, u32[]{:S(2)}) %collective-permute-start.9) | collective-permute-done | bytes 163872 | tf_op jit(solution)/shard_map/ppermute | solution.py:60
  229.4 4.5 %collective-permute-done.10 = f32[40,512]{1,0:T(8,128)S(1)} collective-permute-done((f32[40,512]{1,0:T(8,128)S(1)}, f32[40,512]{1,0:T(8,128)S(1)}, u32[]{:S(2)}, u32[]{:S(2)}) %collective-permute-start.10) | collective-permute-done | bytes 81952 | tf_op jit(solution)/shard_map/ppermute | solution.py:61
  (91 shorter events, 33.6 us)
Async XLA Ops:
  0.6 13.6 %copy-start.10 = (f32[40,512]{1,0:T(8,128)S(1)}, f32[40,512]{1,0:T(8,128)}, u32[]{:S(2)}) copy-start(f32[40,512]{1,0:T(8,128)} %param.2) | copy-start | bytes 245764
  2.8 53.5 %all-to-all-start = ((f32[16,40,512]{2,1,0:T(8,128)}), f32[16,40,512]{2,1,0:T(8,128)}, u32[]{:S(2)}, u32[]{:S(2)}) async-start(f32[16,40,512]{2,1,0:T(8,128)} %broadcast_in_dim.14), calls=%async_computation | async-start | bytes 2621440 | tf_op jit(solution)/shard_map/all_to_all | solution.py:39
  39.9 15.6 %collective-permute-start = (f32[320,512]{1,0:T(8,128)S(1)}, f32[320,512]{1,0:T(8,128)S(1)}, u32[]{:S(2)}, u32[]{:S(2)}) collective-permute-start(f32[320,512]{1,0:T(8,128)S(1)} %all_gather.3.refs_0_), channel_id=1, source_target_pairs={{0,48},{16,32},{32,16},{48,0},{1,49},{17,33},{33,17},{49,1},{2,50}... | collective-permute-start | bytes 1966088 | tf_op jit(solution)/shard_map/ppermute | solution.py:271
  43.9 0.8 copy-start.6
  56.3 9.5 %collective-permute-start.1 = (f32[640,512]{1,0:T(8,128)}, f32[640,512]{1,0:T(8,128)S(1)}, u32[]{:S(2)}, u32[]{:S(2)}) collective-permute-start(f32[640,512]{1,0:T(8,128)} %bitcast.refs_2_.mine_ref), channel_id=1, source_target_pairs={{0,1},{1,0},{2,3},{3,2},{4,5},{5,4},{6,7},{7,6},{8,9},{9,8},{10,11... | collective-permute-start | bytes 3932168 | tf_op jit(solution)/shard_map/ppermute | solution.py:160
  58.3 1.1 copy-start.7
  59.3 1.1 copy-start.9
  65.9 4.0 %copy-start.3 = (f32[640,512]{1,0:T(8,128)}, f32[640,512]{1,0:T(8,128)S(1)}, u32[]{:S(2)}) copy-start(f32[640,512]{1,0:T(8,128)S(1)} %get-tuple-element.32.src_hbm.src_ref) | copy-start | bytes 3932164
  65.9 4.0 %copy-start = (f32[640,512]{1,0:T(8,128)}, f32[640,512]{1,0:T(8,128)S(1)}, u32[]{:S(2)}) copy-start(f32[640,512]{1,0:T(8,128)S(1)} %collective-permute-done.1.other_ref.other_hbm) | copy-start | bytes 3932164
  149.2 14.1 %all-to-all-start.6 = ((f32[32,1,1280]{2,1,0:T(1,128)}), f32[32,1,1280]{2,1,0:T(1,128)S(1)}, u32[]{:S(2)}, u32[]{:S(2)}) async-start(f32[32,1,1280]{2,1,0:T(1,128)} %broadcast_in_dim.20), calls=%async_computation.6 | async-start | bytes 327680 | tf_op jit(solution)/shard_map/all_to_all | solution.py:39
  163.6 1.3 copy-start.1
  164.9 1.3 copy-start.4
  166.2 5.8 %copy-start.2 = (f32[640,512]{1,0:T(8,128)S(1)}, f32[640,512]{1,0:T(8,128)}, u32[]{:S(2)}) copy-start(f32[640,512]{1,0:T(8,128)} %copy-done) | copy-start | bytes 3932164
  166.2 5.8 %copy-start.5 = (f32[640,512]{1,0:T(8,128)S(1)}, f32[640,512]{1,0:T(8,128)}, u32[]{:S(2)}) copy-start(f32[640,512]{1,0:T(8,128)} %copy-done.3) | copy-start | bytes 3932164
  169.9 7.8 %collective-permute-start.2 = (f32[640,512]{1,0:T(8,128)S(1)}, f32[640,512]{1,0:T(8,128)S(1)}, u32[]{:S(2)}, u32[]{:S(2)}) collective-permute-start(f32[640,512]{1,0:T(8,128)S(1)} %get-tuple-element.36), channel_id=1, source_target_pairs={{0,1},{1,0},{2,3},{3,2},{4,5},{5,4},{6,7},{7,6},{8,9},{9,8},{10,11... | collective-permute-start | bytes 3932168 | tf_op jit(solution)/shard_map/ppermute | solution.py:298
  182.4 52.1 %all-to-all-start.7 = ((f32[16,40,512]{2,1,0:T(8,128)}), f32[16,40,512]{2,1,0:T(8,128)S(1)}, u32[]{:S(2)}, u32[]{:S(2)}) async-start(f32[16,40,512]{2,1,0:T(8,128)} %bitcast.5), calls=%async_computation.7 | async-start | bytes 2621440 | tf_op jit(solution)/shard_map/all_to_all | solution.py:39
  186.1 21.1 %collective-permute-start.4 = (f32[2,40,512]{2,1,0:T(8,128)S(1)}, f32[2,40,512]{2,1,0:T(8,128)S(1)}, u32[]{:S(2)}, u32[]{:S(2)}) collective-permute-start(f32[2,40,512]{2,1,0:T(8,128)S(1)} %get-tuple-element.39), channel_id=1, source_target_pairs={{0,6},{2,8},{4,10},{6,12},{8,14},{10,0},{12,2},{14,4},{1,7},{3,9},... | collective-permute-start | bytes 491528 | tf_op jit(solution)/shard_map/ppermute | solution.py:60
  190.6 19.7 %collective-permute-start.5 = (f32[2,40,512]{2,1,0:T(8,128)S(1)}, f32[2,40,512]{2,1,0:T(8,128)S(1)}, u32[]{:S(2)}, u32[]{:S(2)}) collective-permute-start(f32[2,40,512]{2,1,0:T(8,128)S(1)} %get-tuple-element.40), channel_id=1, source_target_pairs={{0,10},{2,12},{4,14},{6,0},{8,2},{10,4},{12,6},{14,8},{1,11},{3,13... | collective-permute-start | bytes 491528 | tf_op jit(solution)/shard_map/ppermute | solution.py:60
  193.8 19.2 %collective-permute-start.6 = (f32[2,40,512]{2,1,0:T(8,128)S(1)}, f32[2,40,512]{2,1,0:T(8,128)S(1)}, u32[]{:S(2)}, u32[]{:S(2)}) collective-permute-start(f32[2,40,512]{2,1,0:T(8,128)S(1)} %get-tuple-element.41), channel_id=1, source_target_pairs={{0,4},{2,6},{4,8},{6,10},{8,12},{10,14},{12,0},{14,2},{1,5},{3,7},... | collective-permute-start | bytes 491528 | tf_op jit(solution)/shard_map/ppermute | solution.py:60
  199.4 16.7 %collective-permute-start.7 = (f32[2,40,512]{2,1,0:T(8,128)S(1)}, f32[2,40,512]{2,1,0:T(8,128)S(1)}, u32[]{:S(2)}, u32[]{:S(2)}) collective-permute-start(f32[2,40,512]{2,1,0:T(8,128)S(1)} %get-tuple-element.42), channel_id=1, source_target_pairs={{0,12},{2,14},{4,0},{6,2},{8,4},{10,6},{12,8},{14,10},{1,13},{3,15... | collective-permute-start | bytes 491528 | tf_op jit(solution)/shard_map/ppermute | solution.py:60
  201.4 14.8 %collective-permute-start.8 = (f32[2,40,512]{2,1,0:T(8,128)S(1)}, f32[2,40,512]{2,1,0:T(8,128)S(1)}, u32[]{:S(2)}, u32[]{:S(2)}) collective-permute-start(f32[2,40,512]{2,1,0:T(8,128)S(1)} %get-tuple-element.43), channel_id=1, source_target_pairs={{0,2},{2,4},{4,6},{6,8},{8,10},{10,12},{12,14},{14,0},{1,3},{3,5},... | collective-permute-start | bytes 491528 | tf_op jit(solution)/shard_map/ppermute | solution.py:60
  207.2 19.0 %collective-permute-start.9 = (f32[2,40,512]{2,1,0:T(8,128)S(1)}, f32[2,40,512]{2,1,0:T(8,128)S(1)}, u32[]{:S(2)}, u32[]{:S(2)}) collective-permute-start(f32[2,40,512]{2,1,0:T(8,128)S(1)} %get-tuple-element.44), channel_id=1, source_target_pairs={{0,14},{2,0},{4,2},{6,4},{8,6},{10,8},{12,10},{14,12},{1,15},{3,1}... | collective-permute-start | bytes 491528 | tf_op jit(solution)/shard_map/ppermute | solution.py:60
  210.3 15.9 %collective-permute-start.3 = (f32[2,40,512]{2,1,0:T(8,128)S(1)}, f32[2,40,512]{2,1,0:T(8,128)S(1)}, u32[]{:S(2)}, u32[]{:S(2)}) collective-permute-start(f32[2,40,512]{2,1,0:T(8,128)S(1)} %get-tuple-element.38), channel_id=1, source_target_pairs={{0,8},{2,10},{4,12},{6,14},{8,0},{10,2},{12,4},{14,6},{1,9},{3,11}... | collective-permute-start | bytes 491528 | tf_op jit(solution)/shard_map/ppermute | solution.py:60
  226.3 7.5 %collective-permute-start.10 = (f32[40,512]{1,0:T(8,128)S(1)}, f32[40,512]{1,0:T(8,128)S(1)}, u32[]{:S(2)}, u32[]{:S(2)}) collective-permute-start(f32[40,512]{1,0:T(8,128)S(1)} %dynamic-slice_bitcast_fusion), channel_id=1, source_target_pairs={{0,48},{16,32},{32,16},{48,0},{1,49},{17,33},{33,17},{49,1},{2,50}... | collective-permute-start | bytes 245768 | tf_op jit(solution)/shard_map/ppermute | solution.py:61
  (1 other events, 0.8 us)
